TPU v7x, 256 devices: a whole 4x4x8 slice. The times are simulated.
256 devices in a mesh: dp: 32 (over x, z_lo, core), group: 8 (over y, z_hi).
Axes of the slice: x: 4, y: 4, z: 8 (z_hi: 2, z_lo: 4; z = z_hi * 4 + z_lo), core: 2. Of those that a mesh axis runs over, the one named last changes fastest.
Arguments:
- hidden_act: bfloat16 [32768, 2, 1536], P('dp'), may hold values from -12 to 12
- out_grad: bfloat16 [32768, 2, 4096], P('dp', None, 'group'), may hold values from -0.03125 to 0.03125
- router_grads: float32 [32, 2, 4096], P('dp'), may hold values from -4 to 4
- small_grads: float32 [32, 8192], P('dp'), may hold values from -2 to 2
- expert_ids: int32 [2], replicated, may hold values from 0 to 127, as said below
- small_lengths: int32 [16], replicated, may hold values from 1 to 2048, 8192 in all
- small_rate: float32 [16], replicated, may hold values from 0.25 to 4
- expert_w: float32 [2, 1536, 4096], P(None, 'dp', 'group'), may hold values from -6 to 6
- expert_m: float32 [2, 1536, 4096], P(None, 'dp', 'group'), may hold values from -3 to 3
- expert_v: float32 [2, 1536, 4096], P(None, 'dp', 'group'), may hold values from 0.1 to 4
- router_w: float32 [128, 4096], P(None, 'dp'), may hold values from -6 to 6
- router_m: float32 [128, 4096], P(None, 'dp'), may hold values from -3 to 3
- router_v: float32 [128, 4096], P(None, 'dp'), may hold values from 0.1 to 4
- small_w: float32 [8192], P('dp'), may hold values from 0.5 to 1.5
- small_m: float32 [8192], P('dp'), may hold values from -3 to 3
- small_v: float32 [8192], P('dp'), may hold values from 0.1 to 4
Outputs:
- new_expert: float32 [2, 1536, 4096], P(None, 'dp', 'group')
- expert_moment: float32 [2, 1536, 4096], P(None, 'dp', 'group')
- expert_second: float32 [2, 1536, 4096], P(None, 'dp', 'group')
- new_router: float32 [128, 4096], P(None, 'dp')
- router_moment: float32 [128, 4096], P(None, 'dp')
- router_second: float32 [128, 4096], P(None, 'dp')
- new_small: float32 [8192], P('dp')
- small_moment: float32 [8192], P('dp')
- small_second: float32 [8192], P('dp')
- expert_rollout: bfloat16 [2, 1536, 4096], P(None, 'group')
- router_rollout: bfloat16 [128, 4096], replicated
- small_rollout: bfloat16 [8192], replicated
Inputs may be any that keep to these rules, and one draw needn't show every extreme that they name: `expert_ids`: 2 distinct expert numbers below 128, the last expert among them. `small_lengths`: they sum to 8192.
All inputs are finite; a program needn't handle non-finite values.
Results may differ from a plain program's by a relative error of at most 0.009.
Values may be sent and summed in bfloat16 or wider, within the bound.
No kernel may reach another device: no remote copies, remote signals or barrier semaphores. Data moves between devices by JAX's collectives and lax.ppermute only.
A program may use at most 128 MiB of HBM per device.

v0:
```python
import jax
import jax.numpy as jnp
from jax import lax
from jax.sharding import PartitionSpec as P

beta_one = 0.9
beta_two = 0.95
learn_rate = 0.1
decay_rate = 0.1
eps = 1e-08
adam_step = 12


def adamw(weight, moment, second, grad, factor, decay):
    moment_new = beta_one * moment + (1.0 - beta_one) * grad
    second_new = beta_two * second + (1.0 - beta_two) * grad * grad
    corrected = moment_new / (1.0 - beta_one**adam_step)
    scaled = second_new / (1.0 - beta_two**adam_step)
    weight_new = weight - learn_rate * factor * (
        corrected / (jnp.sqrt(scaled) + eps) + decay * weight
    )
    return (weight_new, moment_new, second_new)


def body(
    hidden_act,
    out_grad,
    router_grads,
    small_grads,
    expert_ids,
    small_lengths,
    small_rate,
    expert_w,
    expert_m,
    expert_v,
    router_w,
    router_m,
    router_v,
    small_w,
    small_m,
    small_v,
):
    dp_index = lax.axis_index("dp")
    local_router = router_grads[0]
    partial_value = jnp.einsum(
        "tef,ted->efd", hidden_act, out_grad, preferred_element_type=jnp.float32
    )
    expert_grad, router_part, small_part = (
        lax.psum_scatter(
            partial_value.astype(jnp.bfloat16), "dp", scatter_dimension=1, tiled=True
        ).astype(jnp.float32),
        lax.psum_scatter(
            local_router.astype(jnp.bfloat16), "dp", scatter_dimension=1, tiled=True
        ).astype(jnp.float32),
        lax.psum_scatter(
            small_grads.astype(jnp.bfloat16), "dp", scatter_dimension=1, tiled=True
        ).astype(jnp.float32),
    )
    new_expert, expert_moment, expert_second = adamw(
        expert_w, expert_m, expert_v, expert_grad, 1.0, decay_rate
    )
    experts_all = router_w.shape[0]
    selector = (expert_ids[:, None] == jnp.arange(experts_all, dtype=jnp.int32)[None, :]).astype(
        jnp.float32
    )
    router_grad = jnp.sum(selector[:, :, None] * router_part[:, None, :], axis=0)
    new_router, router_moment, router_second = adamw(
        router_w, router_m, router_v, router_grad, 1.0, decay_rate
    )
    shard_len = small_w.shape[0]
    places = dp_index * shard_len + jnp.arange(shard_len, dtype=jnp.int32)
    ends = jnp.cumsum(small_lengths)
    tensor_of = jnp.sum((places[:, None] >= ends[None, :]).astype(jnp.int32), axis=1)
    tensor_count = small_rate.shape[0]
    picked = (tensor_of[:, None] == jnp.arange(tensor_count, dtype=jnp.int32)[None, :]).astype(
        jnp.float32
    )
    small_factor = jnp.sum(picked * small_rate[None, :], axis=1)
    new_small, small_moment, small_second = adamw(
        small_w, small_m, small_v, small_part[0], small_factor, 0.0
    )
    expert_low = new_expert.astype(jnp.bfloat16)
    router_low = new_router.astype(jnp.bfloat16)
    small_low = new_small.astype(jnp.bfloat16)[None, :]
    expert_full, router_full, small_full = (
        lax.all_gather(expert_low, "dp", axis=1, tiled=True),
        lax.all_gather(router_low, "dp", axis=1, tiled=True),
        lax.all_gather(small_low, "dp", axis=1, tiled=True),
    )
    expert_rollout = lax.all_to_all(expert_full, "group", split_axis=1, concat_axis=2, tiled=True)
    return (
        new_expert,
        expert_moment,
        expert_second,
        new_router,
        router_moment,
        router_second,
        new_small,
        small_moment,
        small_second,
        expert_rollout,
        router_full,
        small_full[0],
    )


def solution(mesh):
    placed = (
        P("dp", None, None),
        P("dp", None, "group"),
        P("dp", None, None),
        P("dp", None),
        P(),
        P(),
        P(),
        P(None, "dp", "group"),
        P(None, "dp", "group"),
        P(None, "dp", "group"),
        P(None, "dp"),
        P(None, "dp"),
        P(None, "dp"),
        P("dp"),
        P("dp"),
        P("dp"),
    )
    return jax.shard_map(
        body,
        mesh=mesh,
        in_specs=placed,
        out_specs=(
            P(None, "dp", "group"),
            P(None, "dp", "group"),
            P(None, "dp", "group"),
            P(None, "dp"),
            P(None, "dp"),
            P(None, "dp"),
            P("dp"),
            P("dp"),
            P("dp"),
            P(None, "group", None),
            P(),
            P(),
        ),
        check_vma=False,
    )
```

profile of v0, /device:TPU:1, one launch (start us, length us, event | category | flops | bytes accessed | tf_op | source)
XLA Modules:
  0.0 644.9 jit_solution(10977954930512951846)
XLA Ops:
  7.2 1.5 copy-done
  8.8 11.4 %fusion.2 = bf16[2,1536,512]{2,1,0:T(8,128)(2,1)} fusion(bf16[1024,2,1536]{2,1,0:T(2,128)(2,1)} %param.16, bf16[1024,2,512]{2,1,0:T(2,128)(2,1)S(1)} %copy-done), kind=kOutput, calls=%fused_computation.2 | convolution fusion | flops 3222798336 | bytes 11534336 | tf_op jit(solution)/shard_map/tef,ted->efd/dot_general | solution.py:45
  20.2 0.0 all-gather.5.cloned.1.call-start
  20.2 149.1 %reduce-scatter.8.cloned.1.call-done = bf16[2,48,512]{2,1,0:T(8,128)(2,1)} async-done(((bf16[2,1536,512]{2,1,0:T(8,128)(2,1)}), bf16[2,48,512]{2,1,0:T(8,128)(2,1)}) %reduce-scatter.8.cloned.1.call-update) | async-done | bytes 98320 | tf_op jit(solution)/shard_map/reduce_scatter | solution.py:49
  169.3 1.8 fusion.14
  171.1 63.4 %all-gather.5.cloned.1.call-done = bf16[2,1536,512]{2,1,0:T(8,128)(2,1)} async-done(((bf16[2,48,512]{2,1,0:T(8,128)(2,1)}), bf16[2,1536,512]{2,1,0:T(8,128)(2,1)}) %all-gather.5.cloned.1.call-update) | async-done | bytes 3145744 | tf_op jit(solution)/shard_map/all_gather | solution.py:86
  234.6 7.9 %copy.44 = bf16[2,1536,512]{2,0,1:T(2,128)(2,1)} copy(bf16[2,1536,512]{2,1,0:T(8,128)(2,1)} %all-gather.5.cloned.1.call-done) | data formatting | bytes 6291456 | tf_op jit(solution)/shard_map/all_gather | solution.py:86
  242.5 8.0 %all-to-all-start = ((bf16[2,1536,512]{2,0,1:T(2,128)(2,1)}), bf16[2,1536,512]{2,0,1:T(2,128)(2,1)}, u32[]{:S(2)}, u32[]{:S(2)}) async-start(bf16[2,1536,512]{2,0,1:T(2,128)(2,1)} %copy.44), calls=%async_computation.1 | async-start | bytes 6291456 | tf_op jit(solution)/shard_map/all_to_all | solution.py:90
  250.6 1.4 copy.46
  252.0 0.0 reduce-scatter.12.cloned.1.call-start
  252.1 1.8 copy.48
  254.0 0.0 all-gather.7.cloned.1.call-start
  254.0 0.1 compare_convert_fusion
  254.1 162.5 %reduce-scatter.10.cloned.1.call-done = bf16[128,2]{1,0:T(8,128)(2,1)} async-done(((bf16[4096,2]{1,0:T(8,128)(2,1)}), bf16[128,2]{1,0:T(8,128)(2,1)}) %reduce-scatter.10.cloned.1.call-update) | async-done | bytes 528
  416.6 0.8 copy.47
  417.4 0.1 multiply_reduce_fusion
  417.6 0.7 fusion.12
  418.3 0.1 copy.43
  418.5 0.1 reduce
  418.6 0.1 convert_reduce_fusion
  418.7 0.1 select_reduce_fusion
  418.8 142.2 %reduce-scatter.12.cloned.1.call-done = bf16[256,1]{1,0:T(8,128)(2,1)} async-done(((bf16[8192,1]{1,0:T(8,128)(2,1)}), bf16[256,1]{1,0:T(8,128)(2,1)}) %reduce-scatter.12.cloned.1.call-update) | async-done | bytes 528
  561.0 0.8 convert_bitcast_fusion
  561.8 0.1 copy.51
  561.9 0.6 fusion.10
  562.5 43.5 %all-gather.1 = bf16[32,1,256]{2,1,0:T(2,128)(2,1)S(1)} all-gather(bf16[1,1,256]{2,1,0:T(2,128)(2,1)S(1)} %reshape.83), channel_id=2, replica_groups=mesh['dp'=32,'group'=8] {'dp'}, dimensions={0}, use_global_device_ids=true | all-gather | bytes 16896 | tf_op jit(solution)/shard_map/all_gather | solution.py:88
  606.1 0.1 reduce.1
  606.2 0.6 copy.50
  606.8 19.4 %all-gather.7.cloned.1.call-done = bf16[128,4096]{1,0:T(8,128)(2,1)} async-done(((bf16[128,128]{1,0:T(8,128)(2,1)}), bf16[128,4096]{1,0:T(8,128)(2,1)}) %all-gather.7.cloned.1.call-update) | async-done | bytes 1048592 | tf_op jit(solution)/shard_map/all_gather | solution.py:87
  626.1 5.3 copy.45
  631.5 5.9 all_to_all.16
  637.4 1.0 copy.59
  (45 shorter events, 0.3 us)
Async XLA Ops:
  7.2 1.6 copy-start
  7.2 162.1 %reduce-scatter.8.cloned.1.call-start = ((), (), s32[]{:S(2)}) async-start(), calls=%async_computation.4 | async-start | bytes 3244032 | tf_op jit(solution)/shard_map/reduce_scatter | solution.py:49
  20.1 149.2 %copy-start.2 = (f32[2,48,512]{2,1,0:T(8,128)S(1)}, f32[2,48,512]{2,1,0:T(8,128)}, u32[]{:S(2)}) copy-start(f32[2,48,512]{2,1,0:T(8,128)} %param.23) | copy-start | bytes 589828
  20.1 149.2 %copy-start.3 = (f32[2,48,512]{2,1,0:T(8,128)S(1)}, f32[2,48,512]{2,1,0:T(8,128)}, u32[]{:S(2)}) copy-start(f32[2,48,512]{2,1,0:T(8,128)} %param.24) | copy-start | bytes 589828
  20.1 149.2 %copy-start.4 = (f32[2,48,512]{2,1,0:T(8,128)S(1)}, f32[2,48,512]{2,1,0:T(8,128)}, u32[]{:S(2)}) copy-start(f32[2,48,512]{2,1,0:T(8,128)} %param.25) | copy-start | bytes 589828
  20.2 214.4 %all-gather.5.cloned.1.call-start = ((), (), s32[]{:S(2)}) async-start(), calls=%async_computation.5 | async-start | bytes 3244032 | tf_op jit(solution)/shard_map/all_gather | solution.py:86
  242.5 8.0 %copy-start.8 = (f32[1,2,4096]{2,1,0:T(2,128)S(1)}, f32[1,2,4096]{2,1,0:T(2,128)}, u32[]{:S(2)}) copy-start(f32[1,2,4096]{2,1,0:T(2,128)} %param.18) | copy-start | bytes 98308
  242.5 9.6 %copy-start.9 = (f32[1,8192]{1,0:T(1,128)S(1)}, f32[1,8192]{1,0:T(1,128)}, u32[]{:S(2)}) copy-start(f32[1,8192]{1,0:T(1,128)} %param.19) | copy-start | bytes 98308
  242.5 383.6 %all-to-all-start = ((bf16[2,1536,512]{2,0,1:T(2,128)(2,1)}), bf16[2,1536,512]{2,0,1:T(2,128)(2,1)}, u32[]{:S(2)}, u32[]{:S(2)}) async-start(bf16[2,1536,512]{2,0,1:T(2,128)(2,1)} %copy.44), calls=%async_computation.1 | async-start | bytes 6291456 | tf_op jit(solution)/shard_map/all_to_all | solution.py:90
  250.5 166.1 %reduce-scatter.10.cloned.1.call-start = ((), (), s32[]{:S(2)}) async-start(), calls=%async_computation.7 | async-start | bytes 1081344
  250.5 3.5 copy-start.15
  250.6 167.0 %copy-start.5 = (f32[128,128]{1,0:T(8,128)S(1)}, f32[128,128]{1,0:T(8,128)}, u32[]{:S(2)}) copy-start(f32[128,128]{1,0:T(8,128)} %param.26) | copy-start | bytes 196612
  250.6 167.0 %copy-start.6 = (f32[128,128]{1,0:T(8,128)S(1)}, f32[128,128]{1,0:T(8,128)}, u32[]{:S(2)}) copy-start(f32[128,128]{1,0:T(8,128)} %param.27) | copy-start | bytes 196612
  250.6 167.0 %copy-start.7 = (f32[128,128]{1,0:T(8,128)S(1)}, f32[128,128]{1,0:T(8,128)}, u32[]{:S(2)}) copy-start(f32[128,128]{1,0:T(8,128)} %param.28) | copy-start | bytes 196612
  252.0 166.4 %copy-start.13 = (s32[16]{0:T(128)S(1)}, s32[16]{0:T(128)}, u32[]{:S(2)}) copy-start(s32[16]{0:T(128)} %param.21) | copy-start | bytes 196
  252.0 166.7 %copy-start.14 = (f32[16]{0:T(128)S(1)}, f32[16]{0:T(128)}, u32[]{:S(2)}) copy-start(f32[16]{0:T(128)} %param.22) | copy-start | bytes 196
  252.0 309.9 %copy-start.10 = (f32[256]{0:T(256)S(1)}, f32[256]{0:T(256)}, u32[]{:S(2)}) copy-start(f32[256]{0:T(256)} %param.29) | copy-start | bytes 3076
  252.0 309.9 %copy-start.11 = (f32[256]{0:T(256)S(1)}, f32[256]{0:T(256)}, u32[]{:S(2)}) copy-start(f32[256]{0:T(256)} %param.30) | copy-start | bytes 3076
  252.0 309.9 %copy-start.12 = (f32[256]{0:T(256)S(1)}, f32[256]{0:T(256)}, u32[]{:S(2)}) copy-start(f32[256]{0:T(256)} %param.31) | copy-start | bytes 3076
  252.0 309.0 %reduce-scatter.12.cloned.1.call-start = ((), (), s32[]{:S(2)}) async-start(), calls=%async_computation.8 | async-start | bytes 2162688
  254.0 372.2 %all-gather.7.cloned.1.call-start = ((), (), s32[]{:S(2)}) async-start(), calls=%async_computation.6 | async-start | bytes 1081344 | tf_op jit(solution)/shard_map/all_gather | solution.py:87
  631.5 5.9 copy-start.1
Sparse Core Ops, SparseCore 0:
  20.3 148.9 reduce-scatter.7
  171.8 62.7 all-gather.4
  254.5 162.0 reduce-scatter.9
  419.0 141.9 reduce-scatter.11
  563.3 62.7 all-gather.6
where the time goes:
time: 646 us; the launch traced here: 645 us
  waiting for transfers between devices  537 us (83%)
  blocking collectives  43.5 us (7%)
  local copies, waits for them, and re-layouts  26.6 us (4%)
  between operations  14 us (2%)
  matrix products  11.4 us (2%)
  starting transfers between devices  8.17 us (1%)
    unnamed x7, waiting for transfers between devices  305 us
    reduce_scatter x1, waiting for transfers between devices, body(): lax.psum_scatter(partial_value.astype(jnp.bfloat16), 'dp', scatter_dimens...  149 us
    all_gather x1, waiting for transfers between devices, body(): lax.all_gather(expert_low, 'dp', axis=1, tiled=True)  63.4 us
    all_gather x1, blocking collectives, body(): lax.all_gather(small_low, 'dp', axis=1, tiled=True)  43.5 us
    all_gather x1, waiting for transfers between devices, body(): lax.all_gather(router_low, 'dp', axis=1, tiled=True)  19.4 us
  transfers between devices with their start and end apart: 6, of which 5 were waited for; matrix products, arithmetic and copies ran while one was open for 1% of the time, Pallas kernels for 0%

commit v1 on v0

v1 whole, which is shorter than its diff:
```python
import jax
import jax.numpy as jnp
from jax import lax
from jax.sharding import Mesh, PartitionSpec as P

beta_one = 0.9
beta_two = 0.95
learn_rate = 0.1
decay_rate = 0.1
eps = 1e-08
adam_step = 12

AXES = ("x", "zl", "core", "y", "zh")
SIZES = (4, 4, 2, 4, 2)
DP = AXES[:3]
GROUP = AXES[3:]
NX, NZ, NC, NY, NH = SIZES


def adamw(weight, moment, second, grad, factor, decay):
    moment_new = beta_one * moment + (1.0 - beta_one) * grad
    second_new = beta_two * second + (1.0 - beta_two) * grad * grad
    corrected = moment_new / (1.0 - beta_one**adam_step)
    scaled = second_new / (1.0 - beta_two**adam_step)
    weight_new = weight - learn_rate * factor * (
        corrected / (jnp.sqrt(scaled) + eps) + decay * weight
    )
    return (weight_new, moment_new, second_new)


def shift(value, axis, size, step):
    return lax.ppermute(value, axis, [(i, (i + step) % size) for i in range(size)])


def swap_core(value):
    return lax.ppermute(value, "core", [(0, 1), (1, 0)])


def flat(x, zl, core, y, zh):
    return (((x * NZ + zl) * NC + core) * NY + y) * NH + zh


def to_owner_group():
    pairs = []
    for x in range(NX):
        for zl in range(NZ):
            a, b = zl // 2, zl % 2
            for core in range(NC):
                for y in range(NY):
                    for zh in range(NH):
                        pairs.append((flat(x, zl, core, y, zh), flat(y, 2 * zh + b, core, x, a)))
    return pairs


def pick(value, index, axis):
    return lax.dynamic_index_in_dim(value, index, axis, keepdims=False)


def expert_reduce(hidden_act, out_grad, ix, iz, ic):
    experts, hidden, feats = hidden_act.shape[1], hidden_act.shape[2], out_grad.shape[2]
    wide = hidden // NX
    rows = wide // (NZ * NC)
    total = None
    arrived = []
    for k in (2, 1, 3, 0):
        part = lax.dynamic_slice_in_dim(hidden_act, ((ix + k) % NX) * wide, wide, 2)
        grad = jnp.einsum("tef,ted->efd", part, out_grad, preferred_element_type=jnp.float32)
        grad = grad.astype(jnp.bfloat16).reshape(experts, NZ, NC, rows, feats)
        theirs = swap_core(pick(grad, 1 - ic, 2))
        both = pick(grad, ic, 2).astype(jnp.float32) + theirs.astype(jnp.float32)
        if k:
            arrived.append(shift(both.astype(jnp.bfloat16), "x", NX, k))
        else:
            total = both
    for other in arrived:
        total = total + other.astype(jnp.float32)
    low = total.astype(jnp.bfloat16)
    result = pick(total, iz, 1)
    for j in (1, 2, 3):
        result = result + shift(pick(low, (iz + j) % NZ, 1), "zl", NZ, j).astype(jnp.float32)
    return result


def body(
    hidden_act,
    out_grad,
    router_grads,
    small_grads,
    expert_ids,
    small_lengths,
    small_rate,
    expert_w,
    expert_m,
    expert_v,
    router_w,
    router_m,
    router_v,
    small_w,
    small_m,
    small_v,
):
    ix, iz, ic = lax.axis_index("x"), lax.axis_index("zl"), lax.axis_index("core")
    dp_index = (ix * NZ + iz) * NC + ic
    n_dp = NX * NZ * NC

    selected = router_grads.shape[1]
    router_cols = router_w.shape[1]
    shard_len = small_w.shape[0]
    packed = jnp.concatenate(
        [
            router_grads[0].reshape(selected, n_dp, router_cols).swapaxes(0, 1).reshape(n_dp, -1),
            small_grads[0].reshape(n_dp, shard_len),
        ],
        axis=1,
    ).astype(jnp.bfloat16)
    packed = lax.all_to_all(packed, DP, 0, 0, tiled=True)
    packed = jnp.sum(packed.astype(jnp.float32), axis=0)
    router_part = packed[: selected * router_cols].reshape(selected, router_cols)
    small_part = packed[selected * router_cols :]

    experts_all = router_w.shape[0]
    selector = (expert_ids[:, None] == jnp.arange(experts_all, dtype=jnp.int32)[None, :]).astype(
        jnp.float32
    )
    router_grad = jnp.sum(selector[:, :, None] * router_part[:, None, :], axis=0)
    new_router, router_moment, router_second = adamw(
        router_w, router_m, router_v, router_grad, 1.0, decay_rate
    )
    places = dp_index * shard_len + jnp.arange(shard_len, dtype=jnp.int32)
    ends = jnp.cumsum(small_lengths)
    tensor_of = jnp.sum((places[:, None] >= ends[None, :]).astype(jnp.int32), axis=1)
    tensor_count = small_rate.shape[0]
    picked = (tensor_of[:, None] == jnp.arange(tensor_count, dtype=jnp.int32)[None, :]).astype(
        jnp.float32
    )
    small_factor = jnp.sum(picked * small_rate[None, :], axis=1)
    new_small, small_moment, small_second = adamw(
        small_w, small_m, small_v, small_part, small_factor, 0.0
    )

    extra = 16
    mine = jnp.concatenate(
        [
            new_router.astype(jnp.bfloat16),
            jnp.pad(
                new_small.astype(jnp.bfloat16).reshape(-1, router_cols),
                ((0, extra - shard_len // router_cols), (0, 0)),
            ),
        ],
        axis=0,
    )
    height = experts_all + extra
    line = jnp.zeros((height, NZ, router_cols), jnp.bfloat16)
    for j in range(NZ):
        piece = mine if j == 0 else shift(mine, "zl", NZ, j)
        line = lax.dynamic_update_slice(line, piece[:, None], (0, (iz - j) % NZ, 0))
    plane = jnp.zeros((height, NX, NZ, NC, router_cols), jnp.bfloat16)
    for k in range(NX):
        piece = line if k == 0 else shift(line, "x", NX, k)
        for core, block in ((ic, piece), (1 - ic, swap_core(piece))):
            plane = lax.dynamic_update_slice(
                plane, block[:, None, :, None], (0, (ix - k) % NX, 0, core, 0)
            )
    router_rollout = plane[:experts_all].reshape(experts_all, -1)
    small_rollout = (
        plane[experts_all : experts_all + shard_len // router_cols]
        .reshape(shard_len // router_cols, n_dp, router_cols)
        .swapaxes(0, 1)
        .reshape(-1)
    )

    expert_grad = expert_reduce(hidden_act, out_grad, ix, iz, ic)
    new_expert, expert_moment, expert_second = adamw(
        expert_w, expert_m, expert_v, expert_grad, 1.0, decay_rate
    )
    experts, rows, feats = expert_w.shape
    low = lax.ppermute(new_expert.astype(jnp.bfloat16), AXES, to_owner_group())
    half = jnp.zeros((experts, 2, rows, NH, feats), jnp.bfloat16)
    for j in range(NZ):
        piece = low if j == 0 else shift(low, "zl", NZ, j)
        came = (iz - j) % NZ
        half = lax.dynamic_update_slice(
            half, piece[:, None, :, None], (0, came % 2, 0, came // 2, 0)
        )
    half = half.reshape(experts, 2, rows, NH * feats)
    whole = jnp.zeros((experts, 2, NC, rows, NY * NH * feats), jnp.bfloat16)
    for k in range(NX):
        piece = half if k == 0 else shift(half, "x", NX, k)
        at = ((ix - k) % NX) * (NH * feats)
        for core, block in ((ic, piece), (1 - ic, swap_core(piece))):
            whole = lax.dynamic_update_slice(whole, block[:, :, None], (0, 0, core, 0, at))
    expert_rollout = whole.reshape(experts, 2 * NC * rows, NY * NH * feats)
    return (
        new_expert,
        expert_moment,
        expert_second,
        new_router,
        router_moment,
        router_second,
        new_small,
        small_moment,
        small_second,
        expert_rollout,
        router_rollout,
        small_rollout,
    )


def solution(mesh):
    fine = Mesh(mesh.devices.reshape(SIZES), AXES)
    placed = (
        P(DP, None, None),
        P(DP, None, GROUP),
        P(DP, None, None),
        P(DP, None),
        P(),
        P(),
        P(),
        P(None, DP, GROUP),
        P(None, DP, GROUP),
        P(None, DP, GROUP),
        P(None, DP),
        P(None, DP),
        P(None, DP),
        P(DP),
        P(DP),
        P(DP),
    )
    return jax.shard_map(
        body,
        mesh=fine,
        in_specs=placed,
        out_specs=(
            P(None, DP, GROUP),
            P(None, DP, GROUP),
            P(None, DP, GROUP),
            P(None, DP),
            P(None, DP),
            P(None, DP),
            P(DP),
            P(DP),
            P(DP),
            P(None, GROUP, None),
            P(),
            P(),
        ),
        check_vma=False,
    )
```

time: 646 us -> 161 us (0.25)
  waiting for transfers between devices: 537 us -> 48.1 us
  blocking collectives: 43.5 us -> 0 us
  starting transfers between devices: 8.17 us -> 49.6 us
  local copies, waits for them, and re-layouts: 26.6 us -> 46.3 us
  between operations: 14 us -> 1.76 us
    unnamed x7 -> x0, waiting for transfers between devices: 305 us -> none
    reduce_scatter x1 -> x0, waiting for transfers between devices: 149 us -> none  [body(): lax.psum_scatter(partial_value.astype(jnp.bfloat16), 'dp', scatter_dimens...]
    all_gather x2 -> x0, waiting for transfers between devices: 82.8 us -> none  [the longest x1 63.4 us: body(): lax.all_gather(expert_low, 'dp', axis=1, tiled=True)]
    all_gather x1 -> x0, blocking collectives: 43.5 us -> none  [body(): lax.all_gather(small_low, 'dp', axis=1, tiled=True)]
    ppermute x0 -> x31, starting transfers between devices: none -> 42.5 us  [the longest x18 27 us: shift(): lax.ppermute(value, axis, [(i, (i + step) % size) for i in range(size)])]
    ppermute x0 -> x31, waiting for transfers between devices: none -> 41.5 us  [the longest x18 41.4 us: shift(): lax.ppermute(value, axis, [(i, (i + step) % size) for i in range(size)])]
    dynamic_update_slice x0 -> x25, local copies, waits for them, and re-layouts: none -> 22.2 us  [the longest x9 12.4 us: body(): lax.dynamic_update_slice(plane, block[:, None, :, None], (0, (ix - k) % N...]
    all_to_all x2 -> x0, local copies, waits for them, and re-layouts: 11.3 us -> none  [body(): lax.all_to_all(expert_full, 'group', split_axis=1, concat_axis=2, tiled=T...]
  transfers between devices with their start and end apart: 6 -> 32, of which waited for: 5 -> 9; matrix products, arithmetic and copies ran while one was open for 1% -> 30% of each run, Pallas kernels for 0% -> 0%
where the time goes in v1:
time: 161 us; the launch traced here: 160 us
  starting transfers between devices  49.6 us (31%)
  waiting for transfers between devices  48.1 us (30%)
  local copies, waits for them, and re-layouts  46.3 us (29%)
  other arithmetic  8.31 us (5%)
  matrix products  5.63 us (3%)
  between operations  1.76 us (1%)
    ppermute x18, waiting for transfers between devices, shift(): lax.ppermute(value, axis, [(i, (i + step) % size) for i in range(size)])  41.4 us
    ppermute x18, starting transfers between devices, shift(): lax.ppermute(value, axis, [(i, (i + step) % size) for i in range(size)])  27 us
    ppermute x12, starting transfers between devices, swap_core(): return lax.ppermute(value, 'core', [(0, 1), (1, 0)])  14.8 us
    dynamic_update_slice x9, local copies, waits for them, and re-layouts, body(): lax.dynamic_update_slice(plane, block[:, None, :, None], (0, (ix - k) % N...  12.4 us
    dynamic_slice x1, local copies, waits for them, and re-layouts, expert_reduce(): part = lax.dynamic_slice_in_dim(hidden_act, (ix + k) % NX * wide, wide, 2)  7.61 us
    all_to_all x1, starting transfers between devices, body(): packed = lax.all_to_all(packed, DP, 0, 0, tiled=True)  7.13 us
    all_to_all x1, waiting for transfers between devices, body(): packed = lax.all_to_all(packed, DP, 0, 0, tiled=True)  6.62 us
    dot_general x4, matrix products, expert_reduce(): jnp.einsum('tef,ted->efd', part, out_grad, preferred_element_type=jnp.flo...  5.63 us
  transfers between devices with their start and end apart: 32, of which 9 were waited for; matrix products, arithmetic and copies ran while one was open for 30% of the time, Pallas kernels for 0%

profile of v1, /device:TPU:1, one launch (start us, length us, event | category | flops | bytes accessed | tf_op | source)
XLA Modules:
  0.0 159.6 jit_solution(13367559729182744398)
XLA Ops:
  0.7 7.6 %constant_dynamic-slice_fusion.3 = (bf16[1024,2,384]{2,1,0:T(2,128)(2,1)}, bf16[1024,2,384]{2,1,0:T(2,128)(2,1)}, bf16[1024,2,384]{2,1,0:T(2,128)(2,1)}, bf16[1024,2,384]{2,1,0:T(2,128)(2,1)S(1)}) fusion(bf16[1024,2,1536]{2,1,0:T(2,128)(2,1)} %param.16, s32[]{:T(128)S(6)} %select_n.238, s32[]{:T(128)S(6)} %select_n.244, s32[]{:T(128)S(6)} %select_n.242, ...), kind=kLoop, calls=%fused_computation.80 | loop fusion | bytes 12582928 | tf_op jit(solution)/shard_map/dynamic_slice | solution.py:66
  10.3 3.2 %collective-permute-start.5 = (bf16[2,4,48,512]{3,2,1,0:T(8,128)(2,1)}, bf16[2,4,48,512]{3,2,1,0:T(8,128)(2,1)}, u32[]{:S(2)}, u32[]{:S(2)}) collective-permute-start(bf16[2,4,48,512]{3,2,1,0:T(8,128)(2,1)} %dynamic-slice_bitcast_fusion), channel_id=1, source_target_pairs={{0,8},{8,0},{1,9},{9,1},{2,10},{10,2},{3,11},{11,3},{4,12},{12,4},... | collective-permute-start | bytes 1179656 | tf_op jit(solution)/shard_map/ppermute | solution.py:36
  13.5 2.6 %fusion.14 = bf16[2,384,512]{2,1,0:T(8,128)(2,1)S(1)} fusion(bf16[1024,2,384]{2,1,0:T(2,128)(2,1)} %get-tuple-element.27, bf16[1024,2,512]{2,1,0:T(2,128)(2,1)S(1)} %copy-done), kind=kOutput, calls=%fused_computation.10 | convolution fusion | flops 805699584 | bytes 4456448 | tf_op jit(solution)/shard_map/tef,ted->efd/dot_general | solution.py:67
  24.2 7.1 %all-to-all-start = ((bf16[32,2,256]{2,1,0:T(2,128)(2,1)}), bf16[32,2,256]{2,1,0:T(2,128)(2,1)S(1)}, u32[]{:S(2)}, u32[]{:S(2)}) async-start(bf16[32,2,256]{2,1,0:T(2,128)(2,1)} %reshape.178), calls=%async_computation | async-start | bytes 65536 | tf_op jit(solution)/shard_map/all_to_all | solution.py:116
  32.2 6.6 %all-to-all-done = bf16[32,2,256]{2,1,0:T(2,128)(2,1)S(1)} async-done(((bf16[32,2,256]{2,1,0:T(2,128)(2,1)}), bf16[32,2,256]{2,1,0:T(2,128)(2,1)S(1)}, u32[]{:S(2)}, u32[]{:S(2)}) %all-to-all-start) | async-done | bytes 32800 | tf_op jit(solution)/shard_map/all_to_all | solution.py:116
  40.9 4.2 %collective-permute-done.21 = bf16[144,128]{1,0:T(8,128)(2,1)S(1)} collective-permute-done((bf16[144,128]{1,0:T(8,128)(2,1)S(1)}, bf16[144,128]{1,0:T(8,128)(2,1)S(1)}, u32[]{:S(2)}, u32[]{:S(2)}) %collective-permute-start.21) | collective-permute-done | bytes 36896 | tf_op jit(solution)/shard_map/ppermute | solution.py:32
  45.1 4.1 %collective-permute-done.22 = bf16[144,128]{1,0:T(8,128)(2,1)S(1)} collective-permute-done((bf16[144,128]{1,0:T(8,128)(2,1)S(1)}, bf16[144,128]{1,0:T(8,128)(2,1)S(1)}, u32[]{:S(2)}, u32[]{:S(2)}) %collective-permute-start.22) | collective-permute-done | bytes 36896 | tf_op jit(solution)/shard_map/ppermute | solution.py:32
  49.2 2.8 %collective-permute-done.23 = bf16[144,128]{1,0:T(8,128)(2,1)S(1)} collective-permute-done((bf16[144,128]{1,0:T(8,128)(2,1)S(1)}, bf16[144,128]{1,0:T(8,128)(2,1)S(1)}, u32[]{:S(2)}, u32[]{:S(2)}) %collective-permute-start.23) | collective-permute-done | bytes 36896 | tf_op jit(solution)/shard_map/ppermute | solution.py:32
  52.0 3.9 %collective-permute-start.24 = (bf16[144,4,128]{2,0,1:T(8,128)(2,1)S(1)}, bf16[144,4,128]{2,0,1:T(8,128)(2,1)S(1)}, u32[]{:S(2)}, u32[]{:S(2)}) collective-permute-start(bf16[144,4,128]{2,0,1:T(8,128)(2,1)S(1)} %bitcast_dynamic-update-slice_fusion.17), channel_id=1, source_target_pairs={{0,8},{8,0},{1,9},{9,1},{2,10},{10,2},{3,11},{11,3},{4,12},{12,4},... | collective-permute-start | bytes 442376 | tf_op jit(solution)/shard_map/ppermute | solution.py:36
  56.5 1.2 fusion.24
  57.7 1.8 %collective-permute-start.27 = (bf16[144,4,128]{2,0,1:T(8,128)(2,1)S(1)}, bf16[144,4,128]{2,0,1:T(8,128)(2,1)}, u32[]{:S(2)}, u32[]{:S(2)}) collective-permute-start(bf16[144,4,128]{2,0,1:T(8,128)(2,1)S(1)} %bitcast_dynamic-update-slice_fusion.17), channel_id=1, source_target_pairs={{0,128},{64,192},{128,0},{192,64},{1,129},{65,193},{129,1},{193,65... | collective-permute-start | bytes 442376 | tf_op jit(solution)/shard_map/ppermute | solution.py:32
  63.4 2.6 %collective-permute-done.25 = bf16[144,4,128]{2,0,1:T(8,128)(2,1)S(1)} collective-permute-done((bf16[144,4,128]{2,0,1:T(8,128)(2,1)S(1)}, bf16[144,4,128]{2,0,1:T(8,128)(2,1)S(1)}, u32[]{:S(2)}, u32[]{:S(2)}) %collective-permute-start.25) | collective-permute-done | bytes 147488 | tf_op jit(solution)/shard_map/ppermute | solution.py:32
  67.2 17.4 %collective-permute-done.29 = bf16[144,4,128]{2,0,1:T(8,128)(2,1)} collective-permute-done((bf16[144,4,128]{2,0,1:T(8,128)(2,1)S(1)}, bf16[144,4,128]{2,0,1:T(8,128)(2,1)}, u32[]{:S(2)}, u32[]{:S(2)}) %collective-permute-start.29) | collective-permute-done | bytes 147488 | tf_op jit(solution)/shard_map/ppermute | solution.py:32
  86.2 1.3 fusion.42
  87.6 1.6 %collective-permute-start.9 = (bf16[2,48,512]{2,1,0:T(8,128)(2,1)S(1)}, bf16[2,48,512]{2,1,0:T(8,128)(2,1)S(1)}, u32[]{:S(2)}, u32[]{:S(2)}) collective-permute-start(bf16[2,48,512]{2,1,0:T(8,128)(2,1)S(1)} %get-tuple-element.31), channel_id=1, source_target_pairs={{0,48},{16,0},{32,16},{48,32},{1,49},{17,1},{33,17},{49,33},{2,50}... | collective-permute-start | bytes 294920 | tf_op jit(solution)/shard_map/ppermute | solution.py:32
  89.6 2.4 %collective-permute-done.9 = bf16[2,48,512]{2,1,0:T(8,128)(2,1)S(1)} collective-permute-done((bf16[2,48,512]{2,1,0:T(8,128)(2,1)S(1)}, bf16[2,48,512]{2,1,0:T(8,128)(2,1)S(1)}, u32[]{:S(2)}, u32[]{:S(2)}) %collective-permute-start.9) | collective-permute-done | bytes 98336 | tf_op jit(solution)/shard_map/ppermute | solution.py:32
  92.0 6.8 %collective-permute-done.8 = bf16[2,48,512]{2,1,0:T(8,128)(2,1)S(1)} collective-permute-done((bf16[2,48,512]{2,1,0:T(8,128)(2,1)S(1)}, bf16[2,48,512]{2,1,0:T(8,128)(2,1)S(1)}, u32[]{:S(2)}, u32[]{:S(2)}) %collective-permute-start.8) | collective-permute-done | bytes 98336 | tf_op jit(solution)/shard_map/ppermute | solution.py:32
  101.4 8.6 %collective-permute-start.12 = (bf16[2,48,512]{2,1,0:T(8,128)(2,1)S(1)}, bf16[2,48,512]{2,1,0:T(8,128)(2,1)S(1)}, u32[]{:S(2)}, u32[]{:S(2)}) collective-permute-start(bf16[2,48,512]{2,1,0:T(8,128)(2,1)S(1)} %collective-permute-done.10), channel_id=1, source_target_pairs={{0,32},{16,48},{32,0},{48,16},{1,33},{17,49},{33,1},{49,17},{2,34}... | collective-permute-start | bytes 294920 | tf_op jit(solution)/shard_map/ppermute | solution.py:32
  110.0 2.4 %collective-permute-start.13 = (bf16[2,48,512]{2,1,0:T(8,128)(2,1)S(1)}, bf16[2,48,512]{2,1,0:T(8,128)(2,1)S(1)}, u32[]{:S(2)}, u32[]{:S(2)}) collective-permute-start(bf16[2,48,512]{2,1,0:T(8,128)(2,1)S(1)} %collective-permute-done.10), channel_id=1, source_target_pairs={{0,48},{16,0},{32,16},{48,32},{1,49},{17,1},{33,17},{49,33},{2,50}... | collective-permute-start | bytes 294920 | tf_op jit(solution)/shard_map/ppermute | solution.py:32
  112.5 1.1 collective-permute-done.12
  113.6 1.2 copy.168
  114.9 4.3 %dynamic_update_slice.75 = bf16[2,2,48,2,512]{4,3,2,1,0:T(2,128)(2,1)} dynamic-update-slice(bf16[2,2,48,2,512]{4,3,2,1,0:T(2,128)(2,1)} %copy.168, bf16[2,1,48,1,512]{4,3,2,1,0:T(2,128)(2,1)S(1)} %copy.169, s32[]{:T(128)} %constant.234.clone.1, s32[]{:T(128)S(6)} %select_n.271, s32[]{:T(128)} %constant.234.clone.1, s32[]{:T(128)S(6)} %select_n.273, s32[]{:T(128)} %constant.234.clone.1) | dynamic-update-slice | bytes 196612 | tf_op jit(solution)/shard_map/dynamic_update_slice | solution.py:182
  119.2 2.0 %reshape.166 = bf16[2,2,48,1024]{3,2,1,0:T(8,128)(2,1)} reshape(bf16[2,2,48,2,512]{4,3,2,1,0:T(2,128)(2,1)} %dynamic_update_slice.75) | data formatting | bytes 786432 | tf_op jit(solution)/shard_map/reshape | solution.py:185
  121.2 4.1 %collective-permute-start.14 = (bf16[2,2,48,1024]{3,2,1,0:T(8,128)(2,1)}, bf16[2,2,48,1024]{3,2,1,0:T(8,128)(2,1)}, u32[]{:S(2)}, u32[]{:S(2)}) collective-permute-start(bf16[2,2,48,1024]{3,2,1,0:T(8,128)(2,1)} %reshape.166), channel_id=1, source_target_pairs={{0,8},{8,0},{1,9},{9,1},{2,10},{10,2},{3,11},{11,3},{4,12},{12,4},... | collective-permute-start | bytes 1179656 | tf_op jit(solution)/shard_map/ppermute | solution.py:36
  125.4 2.1 %collective-permute-start.15 = (bf16[2,2,48,1024]{3,2,1,0:T(8,128)(2,1)}, bf16[2,2,48,1024]{3,2,1,0:T(8,128)(2,1)}, u32[]{:S(2)}, u32[]{:S(2)}) collective-permute-start(bf16[2,2,48,1024]{3,2,1,0:T(8,128)(2,1)} %reshape.166), channel_id=1, source_target_pairs={{0,64},{64,128},{128,192},{192,0},{1,65},{65,129},{129,193},{193,1... | collective-permute-start | bytes 1179656 | tf_op jit(solution)/shard_map/ppermute | solution.py:32
  127.4 6.3 %collective-permute-start.17 = (bf16[2,2,48,1024]{3,2,1,0:T(8,128)(2,1)}, bf16[2,2,48,1024]{3,2,1,0:T(8,128)(2,1)}, u32[]{:S(2)}, u32[]{:S(2)}) collective-permute-start(bf16[2,2,48,1024]{3,2,1,0:T(8,128)(2,1)} %reshape.166), channel_id=1, source_target_pairs={{0,128},{64,192},{128,0},{192,64},{1,129},{65,193},{129,1},{193,65... | collective-permute-start | bytes 1179656 | tf_op jit(solution)/shard_map/ppermute | solution.py:32
  135.9 1.9 %copy.183 = bf16[144,4,4,2,128]{4,3,2,1,0:T(2,128)(2,1)} copy(bf16[144,4,4,2,128]{4,0,3,2,1:T(8,128)(2,1)S(1)} %bitcast_dynamic-update-slice_fusion.7) | data formatting | bytes 2359296 | tf_op jit(solution)/shard_map/dynamic_update_slice | solution.py:161
  137.8 1.1 copy.184
  138.9 7.6 %dynamic_update_slice.95 = bf16[144,4,4,2,128]{4,3,2,1,0:T(2,128)(2,1)} dynamic-update-slice(bf16[144,4,4,2,128]{4,3,2,1,0:T(2,128)(2,1)} %copy.183, bf16[144,1,4,1,128]{4,3,2,1,0:T(2,128)(2,1)S(1)} %copy.184, s32[]{:T(128)} %constant.234.clone.1, s32[]{:T(128)S(6)} %select_n.288, s32[]{:T(128)} %constant.234.clone.1, s32[]{:T(128)S(6)} %select_n.240, s32[]{:T(128)} %constant.234.clone.1) | dynamic-update-slice | bytes 294916 | tf_op jit(solution)/shard_map/dynamic_update_slice | solution.py:161
  146.5 1.9 %slice.27 = bf16[128,4,4,2,128]{4,3,2,1,0:T(2,128)(2,1)S(1)} slice(bf16[144,4,4,2,128]{4,3,2,1,0:T(2,128)(2,1)} %dynamic_update_slice.95), slice={[0:128], [0:4], [0:4], [0:2], [0:128]} | slice | bytes 2097152 | tf_op jit(solution)/shard_map/slice | solution.py:164
  149.2 1.6 %reshape.169 = bf16[128,4096]{1,0:T(8,128)(2,1)} reshape(bf16[128,4,4,2,128]{4,3,2,1,0:T(2,128)(2,1)S(1)} %slice.27) | data formatting | bytes 2097152 | tf_op jit(solution)/shard_map/reshape | solution.py:164
  158.0 1.7 %copy-done.2 = bf16[2,2,2,48,4096]{4,3,2,1,0:T(8,128)(2,1)} copy-done((bf16[2,2,2,48,4096]{4,3,2,1,0:T(8,128)(2,1)}, bf16[2,2,2,48,4096]{4,3,2,1,0:T(8,128)(2,1)S(1)}, u32[]{:S(2)}) %copy-start.2) | copy-done | bytes 3145752
  (158 shorter events, 32.8 us)
Async XLA Ops:
  10.3 45.8 %collective-permute-start.5 = (bf16[2,4,48,512]{3,2,1,0:T(8,128)(2,1)}, bf16[2,4,48,512]{3,2,1,0:T(8,128)(2,1)}, u32[]{:S(2)}, u32[]{:S(2)}) collective-permute-start(bf16[2,4,48,512]{3,2,1,0:T(8,128)(2,1)} %dynamic-slice_bitcast_fusion), channel_id=1, source_target_pairs={{0,8},{8,0},{1,9},{9,1},{2,10},{10,2},{3,11},{11,3},{4,12},{12,4},... | collective-permute-start | bytes 1179656 | tf_op jit(solution)/shard_map/ppermute | solution.py:36
  16.9 40.8 %collective-permute-start.3 = (bf16[2,4,48,512]{3,2,1,0:T(8,128)(2,1)}, bf16[2,4,48,512]{3,2,1,0:T(8,128)(2,1)}, u32[]{:S(2)}, u32[]{:S(2)}) collective-permute-start(bf16[2,4,48,512]{3,2,1,0:T(8,128)(2,1)} %dynamic-slice_bitcast_fusion.1), channel_id=1, source_target_pairs={{0,8},{8,0},{1,9},{9,1},{2,10},{10,2},{3,11},{11,3},{4,12},{12,4},... | collective-permute-start | bytes 1179656 | tf_op jit(solution)/shard_map/ppermute | solution.py:36
  19.0 41.7 %collective-permute-start.1 = (bf16[2,4,48,512]{3,2,1,0:T(8,128)(2,1)}, bf16[2,4,48,512]{3,2,1,0:T(8,128)(2,1)}, u32[]{:S(2)}, u32[]{:S(2)}) collective-permute-start(bf16[2,4,48,512]{3,2,1,0:T(8,128)(2,1)} %dynamic-slice_bitcast_fusion.2), channel_id=1, source_target_pairs={{0,8},{8,0},{1,9},{9,1},{2,10},{10,2},{3,11},{11,3},{4,12},{12,4},... | collective-permute-start | bytes 1179656 | tf_op jit(solution)/shard_map/ppermute | solution.py:36
  22.0 63.7 %collective-permute-start = (bf16[2,4,48,512]{3,2,1,0:T(8,128)(2,1)}, bf16[2,4,48,512]{3,2,1,0:T(8,128)(2,1)}, u32[]{:S(2)}, u32[]{:S(2)}) collective-permute-start(bf16[2,4,48,512]{3,2,1,0:T(8,128)(2,1)} %dynamic-slice_bitcast_fusion.3), channel_id=1, source_target_pairs={{0,8},{8,0},{1,9},{9,1},{2,10},{10,2},{3,11},{11,3},{4,12},{12,4},... | collective-permute-start | bytes 1179656 | tf_op jit(solution)/shard_map/ppermute | solution.py:36
  24.2 14.7 %all-to-all-start = ((bf16[32,2,256]{2,1,0:T(2,128)(2,1)}), bf16[32,2,256]{2,1,0:T(2,128)(2,1)S(1)}, u32[]{:S(2)}, u32[]{:S(2)}) async-start(bf16[32,2,256]{2,1,0:T(2,128)(2,1)} %reshape.178), calls=%async_computation | async-start | bytes 65536 | tf_op jit(solution)/shard_map/all_to_all | solution.py:116
  40.4 4.7 %collective-permute-start.21 = (bf16[144,128]{1,0:T(8,128)(2,1)S(1)}, bf16[144,128]{1,0:T(8,128)(2,1)S(1)}, u32[]{:S(2)}, u32[]{:S(2)}) collective-permute-start(bf16[144,128]{1,0:T(8,128)(2,1)S(1)} %fusion.35), channel_id=1, source_target_pairs={{0,16},{16,32},{32,48},{48,0},{1,17},{17,33},{33,49},{49,1},{2,18}... | collective-permute-start | bytes 110600 | tf_op jit(solution)/shard_map/ppermute | solution.py:32
  45.1 4.1 %collective-permute-start.22 = (bf16[144,128]{1,0:T(8,128)(2,1)S(1)}, bf16[144,128]{1,0:T(8,128)(2,1)S(1)}, u32[]{:S(2)}, u32[]{:S(2)}) collective-permute-start(bf16[144,128]{1,0:T(8,128)(2,1)S(1)} %fusion.35), channel_id=1, source_target_pairs={{0,32},{16,48},{32,0},{48,16},{1,33},{17,49},{33,1},{49,17},{2,34}... | collective-permute-start | bytes 110600 | tf_op jit(solution)/shard_map/ppermute | solution.py:32
  49.2 2.8 %collective-permute-start.23 = (bf16[144,128]{1,0:T(8,128)(2,1)S(1)}, bf16[144,128]{1,0:T(8,128)(2,1)S(1)}, u32[]{:S(2)}, u32[]{:S(2)}) collective-permute-start(bf16[144,128]{1,0:T(8,128)(2,1)S(1)} %fusion.35), channel_id=1, source_target_pairs={{0,48},{16,0},{32,16},{48,32},{1,49},{17,1},{33,17},{49,33},{2,50}... | collective-permute-start | bytes 110600 | tf_op jit(solution)/shard_map/ppermute | solution.py:32
  52.0 10.8 %collective-permute-start.24 = (bf16[144,4,128]{2,0,1:T(8,128)(2,1)S(1)}, bf16[144,4,128]{2,0,1:T(8,128)(2,1)S(1)}, u32[]{:S(2)}, u32[]{:S(2)}) collective-permute-start(bf16[144,4,128]{2,0,1:T(8,128)(2,1)S(1)} %bitcast_dynamic-update-slice_fusion.17), channel_id=1, source_target_pairs={{0,8},{8,0},{1,9},{9,1},{2,10},{10,2},{3,11},{11,3},{4,12},{12,4},... | collective-permute-start | bytes 442376 | tf_op jit(solution)/shard_map/ppermute | solution.py:36
  56.1 9.9 %collective-permute-start.25 = (bf16[144,4,128]{2,0,1:T(8,128)(2,1)S(1)}, bf16[144,4,128]{2,0,1:T(8,128)(2,1)S(1)}, u32[]{:S(2)}, u32[]{:S(2)}) collective-permute-start(bf16[144,4,128]{2,0,1:T(8,128)(2,1)S(1)} %bitcast_dynamic-update-slice_fusion.17), channel_id=1, source_target_pairs={{0,64},{64,128},{128,192},{192,0},{1,65},{65,129},{129,193},{193,1... | collective-permute-start | bytes 442376 | tf_op jit(solution)/shard_map/ppermute | solution.py:32
  57.7 8.3 %collective-permute-start.27 = (bf16[144,4,128]{2,0,1:T(8,128)(2,1)S(1)}, bf16[144,4,128]{2,0,1:T(8,128)(2,1)}, u32[]{:S(2)}, u32[]{:S(2)}) collective-permute-start(bf16[144,4,128]{2,0,1:T(8,128)(2,1)S(1)} %bitcast_dynamic-update-slice_fusion.17), channel_id=1, source_target_pairs={{0,128},{64,192},{128,0},{192,64},{1,129},{65,193},{129,1},{193,65... | collective-permute-start | bytes 442376 | tf_op jit(solution)/shard_map/ppermute | solution.py:32
  60.7 25.1 %collective-permute-start.6 = (bf16[2,4,48,512]{3,2,1,0:T(8,128)(2,1)S(1)}, bf16[2,4,48,512]{3,2,1,0:T(8,128)(2,1)S(1)}, u32[]{:S(2)}, u32[]{:S(2)}) collective-permute-start(bf16[2,4,48,512]{3,2,1,0:T(8,128)(2,1)S(1)} %fusion.24), channel_id=1, source_target_pairs={{0,192},{64,0},{128,64},{192,128},{1,193},{65,1},{129,65},{193,129... | collective-permute-start | bytes 1179656 | tf_op jit(solution)/shard_map/ppermute | solution.py:32
  62.8 23.4 %collective-permute-start.4 = (bf16[2,4,48,512]{3,2,1,0:T(8,128)(2,1)S(1)}, bf16[2,4,48,512]{3,2,1,0:T(8,128)(2,1)S(1)}, u32[]{:S(2)}, u32[]{:S(2)}) collective-permute-start(bf16[2,4,48,512]{3,2,1,0:T(8,128)(2,1)S(1)} %fusion.25), channel_id=1, source_target_pairs={{0,64},{64,128},{128,192},{192,0},{1,65},{65,129},{129,193},{193,1... | collective-permute-start | bytes 1179656 | tf_op jit(solution)/shard_map/ppermute | solution.py:32
  66.0 20.2 %collective-permute-start.2 = (bf16[2,4,48,512]{3,2,1,0:T(8,128)(2,1)S(1)}, bf16[2,4,48,512]{3,2,1,0:T(8,128)(2,1)S(1)}, u32[]{:S(2)}, u32[]{:S(2)}) collective-permute-start(bf16[2,4,48,512]{3,2,1,0:T(8,128)(2,1)S(1)} %fusion.26), channel_id=1, source_target_pairs={{0,128},{64,192},{128,0},{192,64},{1,129},{65,193},{129,1},{193,65... | collective-permute-start | bytes 1179656 | tf_op jit(solution)/shard_map/ppermute | solution.py:32
  66.0 18.6 %collective-permute-start.29 = (bf16[144,4,128]{2,0,1:T(8,128)(2,1)S(1)}, bf16[144,4,128]{2,0,1:T(8,128)(2,1)}, u32[]{:S(2)}, u32[]{:S(2)}) collective-permute-start(bf16[144,4,128]{2,0,1:T(8,128)(2,1)S(1)} %bitcast_dynamic-update-slice_fusion.17), channel_id=1, source_target_pairs={{0,192},{64,0},{128,64},{192,128},{1,193},{65,1},{129,65},{193,129... | collective-permute-start | bytes 442376 | tf_op jit(solution)/shard_map/ppermute | solution.py:32
  84.6 4.6 %collective-permute-start.26 = (bf16[144,4,128]{2,0,1:T(8,128)(2,1)S(1)}, bf16[144,4,128]{2,0,1:T(8,128)(2,1)S(1)}, u32[]{:S(2)}, u32[]{:S(2)}) collective-permute-start(bf16[144,4,128]{2,0,1:T(8,128)(2,1)S(1)} %collective-permute-done.25), channel_id=1, source_target_pairs={{0,8},{8,0},{1,9},{9,1},{2,10},{10,2},{3,11},{11,3},{4,12},{12,4},... | collective-permute-start | bytes 442376 | tf_op jit(solution)/shard_map/ppermute | solution.py:36
  85.7 48.1 %collective-permute-start.28 = (bf16[144,4,128]{2,0,1:T(8,128)(2,1)}, bf16[144,4,128]{2,0,1:T(8,128)(2,1)}, u32[]{:S(2)}, u32[]{:S(2)}) collective-permute-start(bf16[144,4,128]{2,0,1:T(8,128)(2,1)} %collective-permute-done.27), channel_id=1, source_target_pairs={{0,8},{8,0},{1,9},{9,1},{2,10},{10,2},{3,11},{11,3},{4,12},{12,4},... | collective-permute-start | bytes 442376 | tf_op jit(solution)/shard_map/ppermute | solution.py:36
  85.7 52.1 %collective-permute-start.30 = (bf16[144,4,128]{2,0,1:T(8,128)(2,1)}, bf16[144,4,128]{2,0,1:T(8,128)(2,1)}, u32[]{:S(2)}, u32[]{:S(2)}) collective-permute-start(bf16[144,4,128]{2,0,1:T(8,128)(2,1)} %collective-permute-done.29), channel_id=1, source_target_pairs={{0,8},{8,0},{1,9},{9,1},{2,10},{10,2},{3,11},{11,3},{4,12},{12,4},... | collective-permute-start | bytes 442376 | tf_op jit(solution)/shard_map/ppermute | solution.py:36
  87.6 4.4 %collective-permute-start.9 = (bf16[2,48,512]{2,1,0:T(8,128)(2,1)S(1)}, bf16[2,48,512]{2,1,0:T(8,128)(2,1)S(1)}, u32[]{:S(2)}, u32[]{:S(2)}) collective-permute-start(bf16[2,48,512]{2,1,0:T(8,128)(2,1)S(1)} %get-tuple-element.31), channel_id=1, source_target_pairs={{0,48},{16,0},{32,16},{48,32},{1,49},{17,1},{33,17},{49,33},{2,50}... | collective-permute-start | bytes 294920 | tf_op jit(solution)/shard_map/ppermute | solution.py:32
  89.2 9.6 %collective-permute-start.8 = (bf16[2,48,512]{2,1,0:T(8,128)(2,1)S(1)}, bf16[2,48,512]{2,1,0:T(8,128)(2,1)S(1)}, u32[]{:S(2)}, u32[]{:S(2)}) collective-permute-start(bf16[2,48,512]{2,1,0:T(8,128)(2,1)S(1)} %get-tuple-element.32), channel_id=1, source_target_pairs={{0,32},{16,48},{32,0},{48,16},{1,33},{17,49},{33,1},{49,17},{2,34}... | collective-permute-start | bytes 294920 | tf_op jit(solution)/shard_map/ppermute | solution.py:32
  89.2 9.6 %collective-permute-start.7 = (bf16[2,48,512]{2,1,0:T(8,128)(2,1)S(1)}, bf16[2,48,512]{2,1,0:T(8,128)(2,1)S(1)}, u32[]{:S(2)}, u32[]{:S(2)}) collective-permute-start(bf16[2,48,512]{2,1,0:T(8,128)(2,1)S(1)} %get-tuple-element.30), channel_id=1, source_target_pairs={{0,16},{16,32},{32,48},{48,0},{1,17},{17,33},{33,49},{49,1},{2,18}... | collective-permute-start | bytes 294920 | tf_op jit(solution)/shard_map/ppermute | solution.py:32
  99.7 1.6 %collective-permute-start.10 = (bf16[2,48,512]{2,1,0:T(8,128)(2,1)S(1)}, bf16[2,48,512]{2,1,0:T(8,128)(2,1)S(1)}, u32[]{:S(2)}, u32[]{:S(2)}) collective-permute-start(bf16[2,48,512]{2,1,0:T(8,128)(2,1)S(1)} %get-tuple-element.20), channel_id=1, source_target_pairs={{0,0},{1,32},{2,64},{3,96},{4,128},{5,160},{6,192},{7,224},{8,8},{... | collective-permute-start | bytes 294920 | tf_op jit(solution)/shard_map/ppermute | solution.py:177
  101.3 11.1 %collective-permute-start.11 = (bf16[2,48,512]{2,1,0:T(8,128)(2,1)S(1)}, bf16[2,48,512]{2,1,0:T(8,128)(2,1)S(1)}, u32[]{:S(2)}, u32[]{:S(2)}) collective-permute-start(bf16[2,48,512]{2,1,0:T(8,128)(2,1)S(1)} %collective-permute-done.10), channel_id=1, source_target_pairs={{0,16},{16,32},{32,48},{48,0},{1,17},{17,33},{33,49},{49,1},{2,18}... | collective-permute-start | bytes 294920 | tf_op jit(solution)/shard_map/ppermute | solution.py:32
  101.4 12.2 %collective-permute-start.12 = (bf16[2,48,512]{2,1,0:T(8,128)(2,1)S(1)}, bf16[2,48,512]{2,1,0:T(8,128)(2,1)S(1)}, u32[]{:S(2)}, u32[]{:S(2)}) collective-permute-start(bf16[2,48,512]{2,1,0:T(8,128)(2,1)S(1)} %collective-permute-done.10), channel_id=1, source_target_pairs={{0,32},{16,48},{32,0},{48,16},{1,33},{17,49},{33,1},{49,17},{2,34}... | collective-permute-start | bytes 294920 | tf_op jit(solution)/shard_map/ppermute | solution.py:32
  110.0 4.8 %collective-permute-start.13 = (bf16[2,48,512]{2,1,0:T(8,128)(2,1)S(1)}, bf16[2,48,512]{2,1,0:T(8,128)(2,1)S(1)}, u32[]{:S(2)}, u32[]{:S(2)}) collective-permute-start(bf16[2,48,512]{2,1,0:T(8,128)(2,1)S(1)} %collective-permute-done.10), channel_id=1, source_target_pairs={{0,48},{16,0},{32,16},{48,32},{1,49},{17,1},{33,17},{49,33},{2,50}... | collective-permute-start | bytes 294920 | tf_op jit(solution)/shard_map/ppermute | solution.py:32
  121.2 32.4 %collective-permute-start.14 = (bf16[2,2,48,1024]{3,2,1,0:T(8,128)(2,1)}, bf16[2,2,48,1024]{3,2,1,0:T(8,128)(2,1)}, u32[]{:S(2)}, u32[]{:S(2)}) collective-permute-start(bf16[2,2,48,1024]{3,2,1,0:T(8,128)(2,1)} %reshape.166), channel_id=1, source_target_pairs={{0,8},{8,0},{1,9},{9,1},{2,10},{10,2},{3,11},{11,3},{4,12},{12,4},... | collective-permute-start | bytes 1179656 | tf_op jit(solution)/shard_map/ppermute | solution.py:36
  125.4 26.8 %collective-permute-start.15 = (bf16[2,2,48,1024]{3,2,1,0:T(8,128)(2,1)}, bf16[2,2,48,1024]{3,2,1,0:T(8,128)(2,1)}, u32[]{:S(2)}, u32[]{:S(2)}) collective-permute-start(bf16[2,2,48,1024]{3,2,1,0:T(8,128)(2,1)} %reshape.166), channel_id=1, source_target_pairs={{0,64},{64,128},{128,192},{192,0},{1,65},{65,129},{129,193},{193,1... | collective-permute-start | bytes 1179656 | tf_op jit(solution)/shard_map/ppermute | solution.py:32
  127.4 25.7 %collective-permute-start.17 = (bf16[2,2,48,1024]{3,2,1,0:T(8,128)(2,1)}, bf16[2,2,48,1024]{3,2,1,0:T(8,128)(2,1)}, u32[]{:S(2)}, u32[]{:S(2)}) collective-permute-start(bf16[2,2,48,1024]{3,2,1,0:T(8,128)(2,1)} %reshape.166), channel_id=1, source_target_pairs={{0,128},{64,192},{128,0},{192,64},{1,129},{65,193},{129,1},{193,65... | collective-permute-start | bytes 1179656 | tf_op jit(solution)/shard_map/ppermute | solution.py:32
  133.8 19.5 %collective-permute-start.19 = (bf16[2,2,48,1024]{3,2,1,0:T(8,128)(2,1)}, bf16[2,2,48,1024]{3,2,1,0:T(8,128)(2,1)}, u32[]{:S(2)}, u32[]{:S(2)}) collective-permute-start(bf16[2,2,48,1024]{3,2,1,0:T(8,128)(2,1)} %reshape.166), channel_id=1, source_target_pairs={{0,192},{64,0},{128,64},{192,128},{1,193},{65,1},{129,65},{193,129... | collective-permute-start | bytes 1179656 | tf_op jit(solution)/shard_map/ppermute | solution.py:32
  152.2 3.5 %collective-permute-start.16 = (bf16[2,2,48,1024]{3,2,1,0:T(8,128)(2,1)}, bf16[2,2,48,1024]{3,2,1,0:T(8,128)(2,1)S(1)}, u32[]{:S(2)}, u32[]{:S(2)}) collective-permute-start(bf16[2,2,48,1024]{3,2,1,0:T(8,128)(2,1)} %collective-permute-done.15), channel_id=1, source_target_pairs={{0,8},{8,0},{1,9},{9,1},{2,10},{10,2},{3,11},{11,3},{4,12},{12,4},... | collective-permute-start | bytes 1179656 | tf_op jit(solution)/shard_map/ppermute | solution.py:36
  153.1 3.7 %collective-permute-start.18 = (bf16[2,2,48,1024]{3,2,1,0:T(8,128)(2,1)}, bf16[2,2,48,1024]{3,2,1,0:T(8,128)(2,1)S(1)}, u32[]{:S(2)}, u32[]{:S(2)}) collective-permute-start(bf16[2,2,48,1024]{3,2,1,0:T(8,128)(2,1)} %collective-permute-done.17), channel_id=1, source_target_pairs={{0,8},{8,0},{1,9},{9,1},{2,10},{10,2},{3,11},{11,3},{4,12},{12,4},... | collective-permute-start | bytes 1179656 | tf_op jit(solution)/shard_map/ppermute | solution.py:36
  153.2 4.7 %collective-permute-start.20 = (bf16[2,2,48,1024]{3,2,1,0:T(8,128)(2,1)}, bf16[2,2,48,1024]{3,2,1,0:T(8,128)(2,1)S(1)}, u32[]{:S(2)}, u32[]{:S(2)}) collective-permute-start(bf16[2,2,48,1024]{3,2,1,0:T(8,128)(2,1)} %collective-permute-done.19), channel_id=1, source_target_pairs={{0,8},{8,0},{1,9},{9,1},{2,10},{10,2},{3,11},{11,3},{4,12},{12,4},... | collective-permute-start | bytes 1179656 | tf_op jit(solution)/shard_map/ppermute | solution.py:36
  (26 other events, 330.8 us)

commit v2 on v1

v2 whole, which is shorter than its diff:
```python
import jax
import jax.numpy as jnp
from jax import lax
from jax.experimental import pallas as pl
from jax.experimental.pallas import tpu as pltpu
from jax.sharding import Mesh, PartitionSpec as P

beta_one = 0.9
beta_two = 0.95
learn_rate = 0.1
decay_rate = 0.1
eps = 1e-08
adam_step = 12

AXES = ("x", "zl", "core", "y", "zh")
SIZES = (4, 4, 2, 4, 2)
DP = AXES[:3]
GROUP = AXES[3:]
NX, NZ, NC, NY, NH = SIZES
EXTRA = 16

SCALARS = pl.BlockSpec(memory_space=pltpu.SMEM)
LOCAL = pl.BlockSpec(memory_space=pltpu.VMEM)
FAR = pl.BlockSpec(memory_space=pltpu.HBM)


def adamw(weight, moment, second, grad, factor, decay):
    moment_new = beta_one * moment + (1.0 - beta_one) * grad
    second_new = beta_two * second + (1.0 - beta_two) * grad * grad
    corrected = moment_new / (1.0 - beta_one**adam_step)
    scaled = second_new / (1.0 - beta_two**adam_step)
    weight_new = weight - learn_rate * factor * (
        corrected / (jnp.sqrt(scaled) + eps) + decay * weight
    )
    return (weight_new, moment_new, second_new)


def shift(value, axis, size, step):
    return lax.ppermute(value, axis, [(i, (i + step) % size) for i in range(size)])


def swap_core(value):
    return lax.ppermute(value, "core", [(0, 1), (1, 0)])


def flat(x, zl, core, y, zh):
    return (((x * NZ + zl) * NC + core) * NY + y) * NH + zh


def to_owner_group():
    pairs = []
    for x in range(NX):
        for zl in range(NZ):
            a, b = zl // 2, zl % 2
            for core in range(NC):
                for y in range(NY):
                    for zh in range(NH):
                        to = flat((x + y) % NX, 2 * zh + b, core, x, a)
                        pairs.append((flat(x, zl, core, y, zh), to))
    return pairs


def to_float(value):
    return value.astype(jnp.float32)


def to_low(value):
    return value.astype(jnp.bfloat16)


def numbers(*values):
    return jnp.stack([jnp.asarray(v, jnp.int32) for v in values])


def kernel(body, outs, ins, out_specs=None, scratch=(), aliases=None, name=None, room=12):
    shapes = [jax.ShapeDtypeStruct(*o) for o in outs]
    return pl.pallas_call(
        body,
        out_shape=shapes,
        in_specs=ins,
        out_specs=out_specs or [LOCAL] * len(outs),
        scratch_shapes=list(scratch),
        input_output_aliases=aliases or {},
        cost_estimate=pl.CostEstimate(flops=0, bytes_accessed=0, transcendentals=0),
        compiler_params=pltpu.CompilerParams(vmem_limit_bytes=room * 2**20),
        name=name,
    )


def fetch(sources, targets, sems):
    copies = [
        pltpu.make_async_copy(a, b, sems.at[n]) for n, (a, b) in enumerate(zip(sources, targets))
    ]
    for copy in copies:
        copy.start()
    return copies


def take_kernel(place, source, *refs):
    *outs, sems = refs
    parts = 8
    copies = []
    for n, out in enumerate(outs):
        tokens, _, wide = out.shape
        at = pl.multiple_of(place[n] * wide, 128)
        for p in range(parts):
            rows = pl.ds(p * (tokens // parts), tokens // parts)
            copies.append(
                pltpu.make_async_copy(
                    source.at[rows, :, pl.ds(at, wide)], out.at[rows], sems.at[len(copies)]
                )
            )
            copies[-1].start()
    for copy in copies:
        copy.wait()


def take(hidden_act, indices, room):
    tokens, experts, hidden = hidden_act.shape
    call = kernel(
        take_kernel,
        [((tokens, experts, hidden // NX), hidden_act.dtype)] * len(indices),
        [SCALARS, FAR],
        scratch=[pltpu.SemaphoreType.DMA((8 * len(indices),))],
        name="take",
        room=room,
    )
    return call(numbers(*indices), hidden_act)


def hold_kernel(*refs):
    *refs, sems = refs
    far, near = refs[: len(refs) // 2], refs[len(refs) // 2 :]
    for copy in fetch(far, near, sems):
        copy.wait()


def hold(*values):
    call = kernel(
        hold_kernel,
        [(v.shape, v.dtype) for v in values],
        [FAR] * len(values),
        scratch=[pltpu.SemaphoreType.DMA((len(values),))],
        name="hold",
    )
    return call(*values)


def extras_kernel(router, small, out, wide):
    cols, shard = 128, 256
    wide[...] = jnp.zeros_like(wide)
    for x in range(NX):
        for d in range(NZ * NC):
            at = x * NZ * NC + d
            for e in range(2):
                wide[x, d : d + 1, e * cols : (e + 1) * cols] = router[
                    e : e + 1, at * cols : (at + 1) * cols
                ]
            wide[x, d : d + 1, 2 * cols : 2 * cols + shard] = small[
                0:1, at * shard : (at + 1) * shard
            ]
    out[...] = to_low(wide[...])


def pack_extras(router_grads, small_grads):
    feats = 512
    call = kernel(
        extras_kernel,
        [((NX, EXTRA, feats), jnp.bfloat16)],
        [LOCAL, LOCAL],
        scratch=[pltpu.VMEM((NX, EXTRA, feats), jnp.float32)],
        name="extras",
    )
    return call(router_grads, small_grads)[0]


def both_cores(place, own, theirs, e, zl):
    rows = own.shape[1] // (NZ * NC)
    at = pl.multiple_of((zl * NC + place[0]) * rows, 16)
    return to_float(own[e, pl.ds(at, rows), :]) + to_float(theirs[e, pl.ds(at, rows), :])


def far_kernel(place, own, theirs, extras, up, down):
    experts, wide, feats = own.shape
    rows = wide // (NZ * NC)
    for e, out in enumerate((up, down)):
        for zl in range(NZ):
            out[zl * rows : (zl + 1) * rows, :] = to_low(both_cores(place, own, theirs, e, zl))
    up[NZ * rows :, :] = extras[place[1]]


def pair_far(place, own, theirs, extras):
    experts, wide, feats = own.shape
    rows = wide // NC
    call = kernel(
        far_kernel,
        [((rows + EXTRA, feats), jnp.bfloat16), ((rows, feats), jnp.bfloat16)],
        [SCALARS] + [LOCAL] * 3,
        name="pair_far",
    )
    return call(place, own, theirs, extras)


def near_kernel(place, own_up, theirs_up, own_down, theirs_down, extras, up, down, to_up, to_down):
    experts, wide, feats = own_up.shape
    rows = wide // (NZ * NC)
    half = NZ * rows
    for n, (own, theirs, out) in enumerate(
        ((own_up, theirs_up, to_up), (own_down, theirs_down, to_down))
    ):
        for e in range(experts):
            for zl in range(NZ):
                total = both_cores(place, own, theirs, e, zl)
                if e == n:
                    more = (up, down)[n]
                    total = total + to_float(more[zl * rows : (zl + 1) * rows, :])
                at = (e * NZ + zl) * rows
                out[at : at + rows, :] = to_low(total)
    to_up[2 * half :, :] = to_low(to_float(extras[place[1]]) + to_float(up[half:, :]))
    to_down[2 * half :, :] = extras[place[2]]


def pair_near(place, ups, downs, extras, up, down):
    experts, wide, feats = ups[0].shape
    rows = experts * wide // NC + EXTRA
    call = kernel(
        near_kernel,
        [((rows, feats), jnp.bfloat16)] * 2,
        [SCALARS] + [LOCAL] * 7,
        name="pair_near",
    )
    return call(place, *ups, *downs, extras, up, down)


def total_kernel(place, own, theirs, extras, r1, r2, mine, s1, s2, s3):
    experts, wide, feats = own.shape
    rows = wide // (NZ * NC)
    count = experts * NZ * rows
    more = to_float(extras[place[1]]) + to_float(r1[count:, :]) + to_float(r2[count:, :])
    for j, out in enumerate((mine, s1, s2, s3)):
        zl = lax.rem(place[2] + j, NZ)
        for e in range(experts):
            total = both_cores(place, own, theirs, e, zl)
            at = pl.multiple_of((e * NZ + zl) * rows, 16)
            for r in (r1, r2):
                total = total + to_float(r[pl.ds(at, rows), :])
            out[e * rows : (e + 1) * rows, :] = total.astype(out.dtype)
        out[experts * rows :, :] = more.astype(out.dtype)


def total_up(place, own, theirs, extras, arrived):
    experts, wide, feats = own.shape
    rows = experts * wide // (NC * NZ) + EXTRA
    call = kernel(
        total_kernel,
        [((rows, feats), jnp.float32)] + [((rows, feats), jnp.bfloat16)] * 3,
        [SCALARS] + [LOCAL] * 5,
        name="total",
    )
    return call(place, own, theirs, extras, *arrived)


def expert_kernel(mine, r1, r2, r3, w, m, v, new, moment, second, low, more):
    experts, rows, feats = w.shape
    at = slice(experts * rows, experts * rows + EXTRA)
    more[...] = mine[at, :] + to_float(r1[at, :]) + to_float(r2[at, :]) + to_float(r3[at, :])
    for e in range(experts):
        at = slice(e * rows, (e + 1) * rows)
        grad = mine[at, :] + to_float(r1[at, :]) + to_float(r2[at, :]) + to_float(r3[at, :])
        weight, first, squared = adamw(w[e], m[e], v[e], grad, 1.0, decay_rate)
        new[e] = weight
        moment[e] = first
        second[e] = squared
        low[e] = to_low(weight)


def expert_update(mine, arrived, w, m, v):
    state = (w.shape, jnp.float32)
    call = kernel(
        expert_kernel,
        [state, state, state, (w.shape, jnp.bfloat16), ((EXTRA, w.shape[2]), jnp.float32)],
        [LOCAL] * 7,
        name="expert_update",
    )
    return call(mine, *arrived, w, m, v)


def others_kernel(place, ids, lengths, rate, own, theirs, *refs):
    w, m, v, sw, sm, sv = refs[:6]
    new, moment, second, small_new, small_moment, small_second, low, held = refs[6:]
    tall, cols = w.shape
    shard_rows = sw.shape[0]
    rows = lax.broadcasted_iota(jnp.int32, own.shape, 0)
    grad_row = jnp.sum(
        jnp.where(rows == place[0], own[...] + theirs[...], 0.0), axis=0, keepdims=True
    )
    at = lax.broadcasted_iota(jnp.int32, (tall, cols), 0)
    grad = jnp.zeros((tall, cols), jnp.float32)
    for e in range(ids.shape[0]):
        part = grad_row[:, e * cols : (e + 1) * cols]
        grad = grad + jnp.where(at == ids[e], part, 0.0)
    held[...] = jnp.zeros_like(held)
    for i in range(shard_rows):
        part = (ids.shape[0] + i) * cols
        held[i : i + 1, :cols] = grad_row[:, part : part + cols]
    small_grad = held[:shard_rows, :cols]
    held[...] = jnp.zeros_like(held)
    spot = (
        place[2]
        + lax.broadcasted_iota(jnp.int32, (shard_rows, cols), 0) * cols
        + lax.broadcasted_iota(jnp.int32, (shard_rows, cols), 1)
    )
    factor = jnp.zeros((shard_rows, cols), jnp.float32)
    begin = jnp.int32(0)
    for k in range(lengths.shape[0]):
        end = begin + lengths[k]
        factor = jnp.where((spot >= begin) & (spot < end), rate[k], factor)
        begin = end
    weight, first, squared = adamw(w[...], m[...], v[...], grad, 1.0, decay_rate)
    new[...] = weight
    moment[...] = first
    second[...] = squared
    rows = lax.broadcasted_iota(jnp.int32, (held.shape[0], cols), 0)
    for e in range(ids.shape[0]):
        picked = jnp.sum(jnp.where(at == ids[e], weight, 0.0), axis=0, keepdims=True)
        held[:, e * cols : (e + 1) * cols] = jnp.where(rows == place[1], picked, 0.0)
    weight, first, squared = adamw(sw[...], sm[...], sv[...], small_grad, factor, 0.0)
    small_new[...] = weight
    small_moment[...] = first
    small_second[...] = squared
    for i in range(shard_rows):
        part = (ids.shape[0] + i) * cols
        held[:, part : part + cols] = jnp.where(rows == place[1], weight[i : i + 1, :], 0.0)
    low[...] = to_low(held[...])


def others_update(place, ids, lengths, rate, own, theirs, router, small):
    tall, cols = router[0].shape
    state, packed = (router[0].shape, jnp.float32), (small[0].shape, jnp.float32)
    call = kernel(
        others_kernel,
        [state] * 3 + [packed] * 3 + [(own.shape, jnp.bfloat16)],
        [SCALARS] * 4 + [LOCAL] * 8,
        scratch=[pltpu.VMEM(own.shape, jnp.float32)],
        name="others_update",
    )
    return call(place, ids, lengths, rate, own, theirs, *router, *small)


def join_kernel(low, extras, out):
    experts, rows, feats = low.shape
    for e in range(experts):
        out[e * rows : (e + 1) * rows, :] = low[e]
    out[experts * rows :, :] = extras[...]


def join(low, extras):
    experts, rows, feats = low.shape
    shape = (experts * rows + EXTRA, feats)
    return kernel(join_kernel, [(shape, jnp.bfloat16)], [LOCAL] * 2, name="join")(low, extras)[0]


def halve_kernel(place, *refs):
    *pieces, upper, lower = refs
    tall, feats = pieces[0].shape
    rows = (tall - EXTRA) // 2
    for s in range(NZ):
        for j in range(NZ):

            @pl.when(lax.rem(place[0] - j + NZ, NZ) == s)
            def _():
                for e, out in enumerate((upper, lower)):
                    to = (s % 2) * rows
                    out[to : to + rows, (s // 2) * feats : (s // 2 + 1) * feats] = pieces[j][
                        e * rows : (e + 1) * rows, :
                    ]

    extras = to_float(pieces[0][2 * rows :, :])
    for piece in pieces[1:]:
        extras = extras + to_float(piece[2 * rows :, :])
    upper[2 * rows :, :feats] = to_low(extras)
    upper[2 * rows :, feats:] = jnp.zeros((EXTRA, feats), jnp.bfloat16)


def halve(place, pieces):
    tall, feats = pieces[0].shape
    rows = tall - EXTRA
    call = kernel(
        halve_kernel,
        [((rows + EXTRA, NH * feats), jnp.bfloat16), ((rows, NH * feats), jnp.bfloat16)],
        [SCALARS] + [LOCAL] * NZ,
        name="halve",
    )
    return call(place, *pieces)


def finish_kernel(place, ids, router, *refs):
    pieces, refs = refs[:16], refs[16:]
    out, patched, small = refs[:3]
    near, refs = refs[3:19], refs[19:]
    lines, packed, sems, out_sems = refs
    cols = 128
    rows = out.shape[3]
    wide = near[0].shape[1]
    feats = wide // NH
    arriving = fetch(pieces, near, sems)
    leaving = []
    for n, piece in enumerate(near):
        core = place[0] ^ (n % 2)
        e = n // 2 % 2
        at = pl.multiple_of(place[1 + n // 4] * wide, wide)
        arriving[n].wait()
        for b in range(2):
            leaving.append(
                pltpu.make_async_copy(
                    piece.at[b * rows : (b + 1) * rows, :],
                    out.at[e, b, core, :, pl.ds(at, wide)],
                    out_sems.at[len(leaving)],
                )
            )
            leaving[-1].start()
    for n in range(2):
        core = place[0] ^ n
        extras = sum(to_float(p[2 * rows :, :feats]) for p in near[n::4])
        for r in range(NX * NZ):
            d = r * NC + core
            for e in range(2):
                lines[e : e + 1, pl.ds(pl.multiple_of(d * cols, cols), cols)] = extras[
                    r : r + 1, e * cols : (e + 1) * cols
                ]
            for i in range(2):
                part = (2 + i) * cols
                packed[pl.ds(2 * d + i, 1), :] = extras[r : r + 1, part : part + cols]
    small[...] = to_low(packed[...])
    spot = lax.broadcasted_iota(jnp.int32, (16, router.shape[1]), 0)
    for at in range(0, router.shape[0], 16):
        block = router[at : at + 16, :]
        patched[at : at + 16, :] = block

        @pl.when((ids[0] // 16 == at // 16) | (ids[1] // 16 == at // 16))
        def _():
            value = to_float(block)
            for e in range(2):
                value = jnp.where(spot + at == ids[e], lines[e : e + 1, :], value)
            patched[at : at + 16, :] = to_low(value)

    for copy in leaving:
        copy.wait()


def finish(place, ids, router, pieces):
    n_dp = NX * NZ * NC
    rows, wide = pieces[2].shape
    shape = (2, 2, NC, rows // 2, NY * wide)
    call = kernel(
        finish_kernel,
        [
            (shape, jnp.bfloat16),
            (router.shape, jnp.bfloat16),
            ((2 * n_dp, 128), jnp.bfloat16),
        ],
        [SCALARS] * 2 + [LOCAL] + [FAR] * len(pieces),
        out_specs=[FAR, LOCAL, LOCAL],
        scratch=[pltpu.VMEM(p.shape, jnp.bfloat16) for p in pieces]
        + [
            pltpu.VMEM((2, router.shape[1]), jnp.float32),
            pltpu.VMEM((2 * n_dp, 128), jnp.float32),
            pltpu.SemaphoreType.DMA((len(pieces),)),
            pltpu.SemaphoreType.DMA((2 * len(pieces),)),
        ],
        name="finish",
    )
    return call(place, ids, router, *pieces)


def body(
    hidden_act,
    out_grad,
    router_grads,
    small_grads,
    expert_ids,
    small_lengths,
    small_rate,
    expert_w,
    expert_m,
    expert_v,
    router_w,
    router_m,
    router_v,
    small_w,
    small_m,
    small_v,
):
    ix, iy, iz, ic = (lax.axis_index(name) for name in ("x", "y", "zl", "core"))
    dp_index = (ix * NZ + iz) * NC + ic
    shard_len = small_w.shape[0]

    router_rollout = lax.all_gather(
        to_low(adamw(router_w, router_m, router_v, jnp.zeros_like(router_w), 1.0, decay_rate)[0]),
        DP,
        axis=1,
        tiled=True,
    )

    def product(part):
        grad = jnp.einsum("tef,ted->efd", part, out_grad, preferred_element_type=jnp.float32)
        return to_low(grad), swap_core(to_low(grad))

    extras = pack_extras(router_grads[0], small_grads)
    opposite, above, below = ((ix + k) % NX for k in (2, 1, 3))
    far_away = product(take(hidden_act, [opposite], 57)[0])
    parts = take(hidden_act, [above, below, ix], 12)
    ups, downs, own = (product(part) for part in parts)
    up, down = pair_far(numbers(ic, opposite), *far_away, extras)
    up, down = shift(up, "x", NX, 1), shift(down, "x", NX, 3)
    up, down = pair_near(numbers(ic, above, below), ups, downs, extras, up, down)
    arrived = [shift(up, "x", NX, 1), shift(down, "x", NX, 3)]
    mine, *sends = total_up(numbers(ic, ix, iz), *own, extras, arrived)
    arrived = [shift(send, "zl", NZ, j + 1) for j, send in enumerate(sends)]

    small_state = [s.reshape(-1, 128) for s in (small_w, small_m, small_v)]
    state = hold(expert_w, expert_m, expert_v, router_w, router_m, router_v, *small_state)
    new_expert, expert_moment, expert_second, low, more = expert_update(
        mine, arrived, *state[:3]
    )
    others = others_update(
        numbers(iz * NC + ic, ix * NZ + iz, dp_index * shard_len),
        expert_ids,
        small_lengths,
        small_rate,
        more,
        swap_core(more),
        state[3:6],
        state[6:],
    )
    new_router, router_moment, router_second = others[:3]
    new_small, small_moment, small_second = (s.reshape(-1) for s in others[3:6])

    low = join(lax.ppermute(low, AXES, to_owner_group()), others[6])
    upper, lower = halve(numbers(iz), [low] + [shift(low, "zl", NZ, j) for j in (1, 2, 3)])
    from_below = shift(upper, "x", NX, 1), shift(lower, "x", NX, 1)
    from_above = shift(upper, "x", NX, 3), shift(lower, "x", NX, 3)
    opposite = shift(from_below[0], "x", NX, 1), shift(from_above[1], "x", NX, 3)
    pieces = []
    for piece in (upper, lower) + from_below + from_above + opposite:
        pieces += [piece, swap_core(piece)]
    places = numbers(ic, *((ix - iy - k) % NX for k in (0, 1, 3, 2)))
    whole, router_rollout, small_rollout = finish(places, expert_ids, router_rollout, pieces)
    expert_rollout = whole.reshape(whole.shape[0], -1, whole.shape[-1])
    small_rollout = small_rollout.reshape(-1)
    return (
        new_expert,
        expert_moment,
        expert_second,
        new_router,
        router_moment,
        router_second,
        new_small,
        small_moment,
        small_second,
        expert_rollout,
        router_rollout,
        small_rollout,
    )


def solution(mesh):
    fine = Mesh(mesh.devices.reshape(SIZES), AXES)
    placed = (
        P(DP, None, None),
        P(DP, None, GROUP),
        P(DP, None, None),
        P(DP, None),
        P(),
        P(),
        P(),
        P(None, DP, GROUP),
        P(None, DP, GROUP),
        P(None, DP, GROUP),
        P(None, DP),
        P(None, DP),
        P(None, DP),
        P(DP),
        P(DP),
        P(DP),
    )
    return jax.shard_map(
        body,
        mesh=fine,
        in_specs=placed,
        out_specs=(
            P(None, DP, GROUP),
            P(None, DP, GROUP),
            P(None, DP, GROUP),
            P(None, DP),
            P(None, DP),
            P(None, DP),
            P(DP),
            P(DP),
            P(DP),
            P(None, GROUP, None),
            P(),
            P(),
        ),
        check_vma=False,
    )
```

time: 161 us -> 138 us (0.86)
  local copies, waits for them, and re-layouts: 46.3 us -> 14.5 us
  Pallas kernels: 0 us -> 22.2 us
  waiting for transfers between devices: 48.1 us -> 31.5 us
  between operations: 1.76 us -> 14.3 us
  other arithmetic: 8.31 us -> 1.03 us
  starting transfers between devices: 49.6 us -> 44.1 us
  matrix products: 5.63 us -> 9.61 us
    dynamic_update_slice x25 -> x0, local copies, waits for them, and re-layouts: 22.2 us -> none  [the longest x9 12.4 us: body(): lax.dynamic_update_slice(plane, block[:, None, :, None], (0, (ix - k) % N...]
    pallas_call x0 -> x12, Pallas kernels: none -> 22.2 us  [the longest x1 7.39 us: finish(): return call(place, ids, router, *pieces)]
    ppermute x18 -> x16, waiting for transfers between devices: 41.4 us -> 29.7 us  [shift(): lax.ppermute(value, axis, [(i, (i + step) % size) for i in range(size)])]
    unnamed x55 -> x52, local copies, waits for them, and re-layouts: 3.99 us -> 14.4 us
    dynamic_slice x1 -> x0, local copies, waits for them, and re-layouts: 7.61 us -> none  [expert_reduce(): part = lax.dynamic_slice_in_dim(hidden_act, (ix + k) % NX * wide, wide, 2)]
    all_to_all x1 -> x0, starting transfers between devices: 7.13 us -> none  [body(): packed = lax.all_to_all(packed, DP, 0, 0, tiled=True)]
    all_to_all x1 -> x0, waiting for transfers between devices: 6.62 us -> none  [body(): packed = lax.all_to_all(packed, DP, 0, 0, tiled=True)]
    convert_element_type x7 -> x1, other arithmetic: 6.41 us -> 0.65 us  [to_low(): return value.astype(jnp.bfloat16)]
  transfers between devices with their start and end apart: 32 -> 31, of which waited for: 9 -> 11; matrix products, arithmetic and copies ran while one was open for 30% -> 6% of each run, Pallas kernels for 0% -> 9%
where the time goes in v2:
time: 138 us; the launch traced here: 137 us
  starting transfers between devices  44.1 us (32%)
  waiting for transfers between devices  31.5 us (23%)
  Pallas kernels  22.2 us (16%)
  local copies, waits for them, and re-layouts  14.5 us (11%)
  between operations  14.3 us (10%)
  matrix products  9.61 us (7%)
    ppermute x16, starting transfers between devices, shift(): lax.ppermute(value, axis, [(i, (i + step) % size) for i in range(size)])  29.9 us
    ppermute x16, waiting for transfers between devices, shift(): lax.ppermute(value, axis, [(i, (i + step) % size) for i in range(size)])  29.7 us
    unnamed x52, local copies, waits for them, and re-layouts  14.4 us
    ppermute x13, starting transfers between devices, swap_core(): return lax.ppermute(value, 'core', [(0, 1), (1, 0)])  13.5 us
    dot_general x4, matrix products, product(): jnp.einsum('tef,ted->efd', part, out_grad, preferred_element_type=jnp.flo...  9.61 us
    pallas_call x1, Pallas kernels, finish(): return call(place, ids, router, *pieces)  7.39 us
    pallas_call x2, Pallas kernels, take(): return call(numbers(*indices), hidden_act)  4.69 us
    pallas_call x1, Pallas kernels, pair_near(): return call(place, *ups, *downs, extras, up, down)  2.99 us
  transfers between devices with their start and end apart: 31, of which 11 were waited for; matrix products, arithmetic and copies ran while one was open for 6% of the time, Pallas kernels for 9%

profile of v2, /device:TPU:1, one launch (start us, length us, event | category | flops | bytes accessed | tf_op | source)
XLA Modules:
  0.0 137.2 jit_solution(17288720509075311333)
XLA Ops:
  7.3 2.8 %take.3 = bf16[1024,2,384]{2,1,0:T(2,128)(2,1)} custom-call(s32[1]{0:T(128)} %bitcast.6.place, bf16[1024,2,1536]{2,1,0:T(2,128)(2,1)} %source.3), custom_call_target="tpu_custom_call" | custom-call | tf_op jit(solution)/shard_map/take/pallas_call | solution.py:128
  10.1 2.4 %fusion.17.own = bf16[2,384,512]{2,1,0:T(8,128)(2,1)S(1)} fusion(bf16[1024,2,384]{2,1,0:T(2,128)(2,1)} %take.3, bf16[1024,2,512]{2,1,0:T(2,128)(2,1)S(1)} %copy-done), kind=kOutput, calls=%fused_computation.11 | convolution fusion | flops 805699584 | bytes 4456448 | tf_op jit(solution)/shard_map/tef,ted->efd/dot_general | solution.py:506
  12.5 3.3 %collective-permute-start.3 = (bf16[2,384,512]{2,1,0:T(8,128)(2,1)S(1)}, bf16[2,384,512]{2,1,0:T(8,128)(2,1)}, u32[]{:S(2)}, u32[]{:S(2)}) collective-permute-start(bf16[2,384,512]{2,1,0:T(8,128)(2,1)S(1)} %fusion.17.own), channel_id=1, source_target_pairs={{0,8},{8,0},{1,9},{9,1},{2,10},{10,2},{3,11},{11,3},{4,12},{12,4},... | collective-permute-start | bytes 2359304 | tf_op jit(solution)/shard_map/ppermute | solution.py:43
  15.9 2.8 %copy-done.1 = bf16[1024,2,1536]{2,1,0:T(2,128)(2,1)S(1)} copy-done((bf16[1024,2,1536]{2,1,0:T(2,128)(2,1)S(1)}, bf16[1024,2,1536]{2,1,0:T(2,128)(2,1)}, u32[]{:S(2)}) %copy-start.1) | copy-done | bytes 6291480
  18.7 1.9 %take.2 = (bf16[1024,2,384]{2,1,0:T(2,128)(2,1)S(1)}, bf16[1024,2,384]{2,1,0:T(2,128)(2,1)S(1)}, bf16[1024,2,384]{2,1,0:T(2,128)(2,1)S(1)}) custom-call(s32[3]{0:T(128)S(1)} %pad_add_fusion.1.place, bf16[1024,2,1536]{2,1,0:T(2,128)(2,1)S(1)} %copy-done.1), custom_call_target="tpu_custom_call" | custom-call | tf_op jit(solution)/shard_map/take/pallas_call | solution.py:128
  21.7 1.9 %fusion.14.own_down = bf16[2,384,512]{2,1,0:T(8,128)(2,1)} fusion(bf16[1024,2,384]{2,1,0:T(2,128)(2,1)S(1)} %get-tuple-element.51, bf16[1024,2,512]{2,1,0:T(2,128)(2,1)S(1)} %copy-done), kind=kOutput, calls=%fused_computation.10 | convolution fusion | flops 805699584 | bytes 4456448 | tf_op jit(solution)/shard_map/tef,ted->efd/dot_general | solution.py:506
  23.7 1.9 %fusion.11.own_up = bf16[2,384,512]{2,1,0:T(8,128)(2,1)} fusion(bf16[1024,2,384]{2,1,0:T(2,128)(2,1)S(1)} %get-tuple-element.50, bf16[1024,2,512]{2,1,0:T(2,128)(2,1)S(1)} %copy-done), kind=kOutput, calls=%fused_computation.9 | convolution fusion | flops 805699584 | bytes 4456448 | tf_op jit(solution)/shard_map/tef,ted->efd/dot_general | solution.py:506
  26.8 3.3 %fusion.8.own = bf16[2,384,512]{2,1,0:T(8,128)(2,1)} fusion(bf16[1024,2,384]{2,1,0:T(2,128)(2,1)} %copy-done.25, bf16[1024,2,512]{2,1,0:T(2,128)(2,1)S(1)} %copy-done), kind=kOutput, calls=%fused_computation.8 | convolution fusion | flops 805699584 | bytes 4456448 | tf_op jit(solution)/shard_map/tef,ted->efd/dot_general | solution.py:506
  30.3 1.2 pair_far.1
  31.7 2.7 %collective-permute-start.5 = (bf16[192,512]{1,0:T(8,128)(2,1)S(1)}, bf16[192,512]{1,0:T(8,128)(2,1)S(1)}, u32[]{:S(2)}, u32[]{:S(2)}) collective-permute-start(bf16[192,512]{1,0:T(8,128)(2,1)S(1)} %get-tuple-element.53), channel_id=1, source_target_pairs={{0,192},{64,0},{128,64},{192,128},{1,193},{65,1},{129,65},{193,129... | collective-permute-start | bytes 589832 | tf_op jit(solution)/shard_map/ppermute | solution.py:39
  34.4 3.4 %collective-permute-done.5.down = bf16[192,512]{1,0:T(8,128)(2,1)S(1)} collective-permute-done((bf16[192,512]{1,0:T(8,128)(2,1)S(1)}, bf16[192,512]{1,0:T(8,128)(2,1)S(1)}, u32[]{:S(2)}, u32[]{:S(2)}) %collective-permute-start.5) | collective-permute-done | bytes 196640 | tf_op jit(solution)/shard_map/ppermute | solution.py:39
  37.8 1.4 %collective-permute-done.4.up = bf16[208,512]{1,0:T(8,128)(2,1)S(1)} collective-permute-done((bf16[208,512]{1,0:T(8,128)(2,1)S(1)}, bf16[208,512]{1,0:T(8,128)(2,1)S(1)}, u32[]{:S(2)}, u32[]{:S(2)}) %collective-permute-start.4) | collective-permute-done | bytes 213024 | tf_op jit(solution)/shard_map/ppermute | solution.py:39
  39.2 3.0 %pair_near.1 = (bf16[400,512]{1,0:T(8,128)(2,1)}, bf16[400,512]{1,0:T(8,128)(2,1)}) custom-call(s32[3]{0:T(128)S(1)} %pad_add_fusion.2.place, bf16[2,384,512]{2,1,0:T(8,128)(2,1)} %fusion.11.own_up, bf16[2,384,512]{2,1,0:T(8,128)(2,1)} %collective-permute-done.1.theirs_up, bf16[2,384,512]{2,1,0:T(8,128)(2,1)} %fusion.14.own_down, ...), custom_call_target="tpu_custom_call" | custom-call | tf_op jit(solution)/shard_map/pair_near/pallas_call | solution.py:232
  42.3 2.7 %collective-permute-start.7 = (bf16[400,512]{1,0:T(8,128)(2,1)}, bf16[400,512]{1,0:T(8,128)(2,1)S(1)}, u32[]{:S(2)}, u32[]{:S(2)}) collective-permute-start(bf16[400,512]{1,0:T(8,128)(2,1)} %get-tuple-element.55), channel_id=1, source_target_pairs={{0,192},{64,0},{128,64},{192,128},{1,193},{65,1},{129,65},{193,129... | collective-permute-start | bytes 1228808 | tf_op jit(solution)/shard_map/ppermute | solution.py:39
  45.0 8.3 %collective-permute-done.6.r1 = bf16[400,512]{1,0:T(8,128)(2,1)S(1)} collective-permute-done((bf16[400,512]{1,0:T(8,128)(2,1)}, bf16[400,512]{1,0:T(8,128)(2,1)S(1)}, u32[]{:S(2)}, u32[]{:S(2)}) %collective-permute-start.6) | collective-permute-done | bytes 409632 | tf_op jit(solution)/shard_map/ppermute | solution.py:39
  53.7 2.2 %total.1 = (f32[112,512]{1,0:T(8,128)S(1)}, bf16[112,512]{1,0:T(8,128)(2,1)}, bf16[112,512]{1,0:T(8,128)(2,1)}, bf16[112,512]{1,0:T(8,128)(2,1)}) custom-call(s32[3]{0:T(128)S(1)} %pad_add_fusion.place, bf16[2,384,512]{2,1,0:T(8,128)(2,1)} %fusion.8.own, bf16[2,384,512]{2,1,0:T(8,128)(2,1)} %collective-permute-done.theirs, bf16[4,16,512]{2,1,0:T(8,128)(2,1)S(1)} %extras.1, ...), custom_call_target="tpu_custom_call" | custom-call | tf_op jit(solution)/shard_map/total/pallas_call | solution.py:260
  56.1 2.7 %collective-permute-start.9 = (bf16[112,512]{1,0:T(8,128)(2,1)}, bf16[112,512]{1,0:T(8,128)(2,1)S(1)}, u32[]{:S(2)}, u32[]{:S(2)}) collective-permute-start(bf16[112,512]{1,0:T(8,128)(2,1)} %get-tuple-element.58), channel_id=1, source_target_pairs={{0,32},{16,48},{32,0},{48,16},{1,33},{17,49},{33,1},{49,17},{2,34}... | collective-permute-start | bytes 344072 | tf_op jit(solution)/shard_map/ppermute | solution.py:39
  63.4 4.5 %collective-permute-done.9.r2 = bf16[112,512]{1,0:T(8,128)(2,1)S(1)} collective-permute-done((bf16[112,512]{1,0:T(8,128)(2,1)}, bf16[112,512]{1,0:T(8,128)(2,1)S(1)}, u32[]{:S(2)}, u32[]{:S(2)}) %collective-permute-start.9) | collective-permute-done | bytes 114720 | tf_op jit(solution)/shard_map/ppermute | solution.py:39
  68.9 1.8 %collective-permute-start.11 = (f32[16,512]{1,0:T(8,128)S(1)}, f32[16,512]{1,0:T(8,128)S(1)}, u32[]{:S(2)}, u32[]{:S(2)}) collective-permute-start(f32[16,512]{1,0:T(8,128)S(1)} %get-tuple-element.66.own), channel_id=1, source_target_pairs={{0,8},{8,0},{1,9},{9,1},{2,10},{10,2},{3,11},{11,3},{4,12},{12,4},... | collective-permute-start | bytes 98312 | tf_op jit(solution)/shard_map/ppermute | solution.py:43
  71.7 1.3 others_update.1
  73.0 10.7 %collective-permute-start.15 = (bf16[112,512]{1,0:T(8,128)(2,1)S(1)}, bf16[112,512]{1,0:T(8,128)(2,1)S(1)}, u32[]{:S(2)}, u32[]{:S(2)}) collective-permute-start(bf16[112,512]{1,0:T(8,128)(2,1)S(1)} %join.1.refs_0_), channel_id=1, source_target_pairs={{0,48},{16,0},{32,16},{48,32},{1,49},{17,1},{33,17},{49,33},{2,50}... | collective-permute-start | bytes 344072 | tf_op jit(solution)/shard_map/ppermute | solution.py:39
  84.1 1.9 %collective-permute-done.15.refs_3_ = bf16[112,512]{1,0:T(8,128)(2,1)S(1)} collective-permute-done((bf16[112,512]{1,0:T(8,128)(2,1)S(1)}, bf16[112,512]{1,0:T(8,128)(2,1)S(1)}, u32[]{:S(2)}, u32[]{:S(2)}) %collective-permute-start.15) | collective-permute-done | bytes 114720 | tf_op jit(solution)/shard_map/ppermute | solution.py:39
  86.0 8.5 %collective-permute-done.14.refs_2_ = bf16[112,512]{1,0:T(8,128)(2,1)S(1)} collective-permute-done((bf16[112,512]{1,0:T(8,128)(2,1)S(1)}, bf16[112,512]{1,0:T(8,128)(2,1)S(1)}, u32[]{:S(2)}, u32[]{:S(2)}) %collective-permute-start.14) | collective-permute-done | bytes 114720 | tf_op jit(solution)/shard_map/ppermute | solution.py:39
  94.7 1.8 %collective-permute-start.18 = (bf16[112,1024]{1,0:T(8,128)(2,1)S(1)}, bf16[112,1024]{1,0:T(8,128)(2,1)S(1)}, u32[]{:S(2)}, u32[]{:S(2)}) collective-permute-start(bf16[112,1024]{1,0:T(8,128)(2,1)S(1)} %get-tuple-element.81.refs_0_), channel_id=1, source_target_pairs={{0,64},{64,128},{128,192},{192,0},{1,65},{65,129},{129,193},{193,1... | collective-permute-start | bytes 688136 | tf_op jit(solution)/shard_map/ppermute | solution.py:39
  96.5 2.6 %collective-permute-start.24 = (bf16[96,1024]{1,0:T(8,128)(2,1)S(1)}, bf16[96,1024]{1,0:T(8,128)(2,1)S(1)}, u32[]{:S(2)}, u32[]{:S(2)}) collective-permute-start(bf16[96,1024]{1,0:T(8,128)(2,1)S(1)} %get-tuple-element.82.refs_2_), channel_id=1, source_target_pairs={{0,192},{64,0},{128,64},{192,128},{1,193},{65,1},{129,65},{193,129... | collective-permute-start | bytes 589832 | tf_op jit(solution)/shard_map/ppermute | solution.py:39
  99.3 1.5 %collective-permute-start.17 = (bf16[96,1024]{1,0:T(8,128)(2,1)S(1)}, bf16[96,1024]{1,0:T(8,128)(2,1)S(1)}, u32[]{:S(2)}, u32[]{:S(2)}) collective-permute-start(bf16[96,1024]{1,0:T(8,128)(2,1)S(1)} %get-tuple-element.82.refs_2_), channel_id=1, source_target_pairs={{0,8},{8,0},{1,9},{9,1},{2,10},{10,2},{3,11},{11,3},{4,12},{12,4},... | collective-permute-start | bytes 589832 | tf_op jit(solution)/shard_map/ppermute | solution.py:43
  101.5 2.5 %collective-permute-start.22 = (bf16[112,1024]{1,0:T(8,128)(2,1)S(1)}, bf16[112,1024]{1,0:T(8,128)(2,1)S(1)}, u32[]{:S(2)}, u32[]{:S(2)}) collective-permute-start(bf16[112,1024]{1,0:T(8,128)(2,1)S(1)} %get-tuple-element.81.refs_0_), channel_id=1, source_target_pairs={{0,192},{64,0},{128,64},{192,128},{1,193},{65,1},{129,65},{193,129... | collective-permute-start | bytes 688136 | tf_op jit(solution)/shard_map/ppermute | solution.py:39
  104.0 1.4 %collective-permute-start.16 = (bf16[112,1024]{1,0:T(8,128)(2,1)S(1)}, bf16[112,1024]{1,0:T(8,128)(2,1)S(1)}, u32[]{:S(2)}, u32[]{:S(2)}) collective-permute-start(bf16[112,1024]{1,0:T(8,128)(2,1)S(1)} %get-tuple-element.81.refs_0_), channel_id=1, source_target_pairs={{0,8},{8,0},{1,9},{9,1},{2,10},{10,2},{3,11},{11,3},{4,12},{12,4},... | collective-permute-start | bytes 688136 | tf_op jit(solution)/shard_map/ppermute | solution.py:43
  105.4 1.5 %collective-permute-start.26 = (bf16[112,1024]{1,0:T(8,128)(2,1)S(1)}, bf16[112,1024]{1,0:T(8,128)(2,1)S(1)}, u32[]{:S(2)}, u32[]{:S(2)}) collective-permute-start(bf16[112,1024]{1,0:T(8,128)(2,1)S(1)} %collective-permute-done.18.refs_4_), channel_id=1, source_target_pairs={{0,64},{64,128},{128,192},{192,0},{1,65},{65,129},{129,193},{193,1... | collective-permute-start | bytes 688136 | tf_op jit(solution)/shard_map/ppermute | solution.py:39
  106.8 1.3 collective-permute-done.20.refs_6_
  110.0 2.7 %collective-permute-start.25 = (bf16[96,1024]{1,0:T(8,128)(2,1)S(1)}, bf16[96,1024]{1,0:T(8,128)(2,1)S(1)}, u32[]{:S(2)}, u32[]{:S(2)}) collective-permute-start(bf16[96,1024]{1,0:T(8,128)(2,1)S(1)} %collective-permute-done.24.refs_10_), channel_id=1, source_target_pairs={{0,8},{8,0},{1,9},{9,1},{2,10},{10,2},{3,11},{11,3},{4,12},{12,4},... | collective-permute-start | bytes 589832 | tf_op jit(solution)/shard_map/ppermute | solution.py:43
  123.0 7.4 %finish.1 = (bf16[2,2,2,48,4096]{4,3,2,1,0:T(8,128)(2,1)}, bf16[128,4096]{1,0:T(8,128)(2,1)}, bf16[64,128]{1,0:T(8,128)(2,1)}) custom-call(s32[5]{0:T(128)S(1)} %stack.83.place, s32[2]{0:T(128)S(1)} %copy-done.19, bf16[128,4096]{1,0:T(8,128)(2,1)S(1)} %copy-done.2, bf16[112,1024]{1,0:T(8,128)(2,1)S(1)} %get-tuple-element.81.refs_0_, ...), custom_call_target="tpu_custom_call" | custom-call | tf_op jit(solution)/shard_map/finish/pallas_call | solution.py:473
  (106 shorter events, 23.6 us)
Async XLA Ops:
  7.2 109.1 %all-gather.2.cloned.1.call-start = ((), (), s32[]{:S(2)}) async-start(), calls=%async_computation | async-start | bytes 1081344 | tf_op jit(solution)/shard_map/all_gather | solution.py:498
  12.5 17.8 %collective-permute-start.3 = (bf16[2,384,512]{2,1,0:T(8,128)(2,1)S(1)}, bf16[2,384,512]{2,1,0:T(8,128)(2,1)}, u32[]{:S(2)}, u32[]{:S(2)}) collective-permute-start(bf16[2,384,512]{2,1,0:T(8,128)(2,1)S(1)} %fusion.17.own), channel_id=1, source_target_pairs={{0,8},{8,0},{1,9},{9,1},{2,10},{10,2},{3,11},{11,3},{4,12},{12,4},... | collective-permute-start | bytes 2359304 | tf_op jit(solution)/shard_map/ppermute | solution.py:43
  23.7 10.7 %collective-permute-start.2 = (bf16[2,384,512]{2,1,0:T(8,128)(2,1)}, bf16[2,384,512]{2,1,0:T(8,128)(2,1)}, u32[]{:S(2)}, u32[]{:S(2)}) collective-permute-start(bf16[2,384,512]{2,1,0:T(8,128)(2,1)} %fusion.14.own_down), channel_id=1, source_target_pairs={{0,8},{8,0},{1,9},{9,1},{2,10},{10,2},{3,11},{11,3},{4,12},{12,4},... | collective-permute-start | bytes 2359304 | tf_op jit(solution)/shard_map/ppermute | solution.py:43
  25.6 8.8 %collective-permute-start.1 = (bf16[2,384,512]{2,1,0:T(8,128)(2,1)}, bf16[2,384,512]{2,1,0:T(8,128)(2,1)}, u32[]{:S(2)}, u32[]{:S(2)}) collective-permute-start(bf16[2,384,512]{2,1,0:T(8,128)(2,1)} %fusion.11.own_up), channel_id=1, source_target_pairs={{0,8},{8,0},{1,9},{9,1},{2,10},{10,2},{3,11},{11,3},{4,12},{12,4},... | collective-permute-start | bytes 2359304 | tf_op jit(solution)/shard_map/ppermute | solution.py:43
  30.1 14.9 %collective-permute-start = (bf16[2,384,512]{2,1,0:T(8,128)(2,1)}, bf16[2,384,512]{2,1,0:T(8,128)(2,1)}, u32[]{:S(2)}, u32[]{:S(2)}) collective-permute-start(bf16[2,384,512]{2,1,0:T(8,128)(2,1)} %fusion.8.own), channel_id=1, source_target_pairs={{0,8},{8,0},{1,9},{9,1},{2,10},{10,2},{3,11},{11,3},{4,12},{12,4},... | collective-permute-start | bytes 2359304 | tf_op jit(solution)/shard_map/ppermute | solution.py:43
  31.6 7.6 %collective-permute-start.4 = (bf16[208,512]{1,0:T(8,128)(2,1)S(1)}, bf16[208,512]{1,0:T(8,128)(2,1)S(1)}, u32[]{:S(2)}, u32[]{:S(2)}) collective-permute-start(bf16[208,512]{1,0:T(8,128)(2,1)S(1)} %get-tuple-element.52), channel_id=1, source_target_pairs={{0,64},{64,128},{128,192},{192,0},{1,65},{65,129},{129,193},{193,1... | collective-permute-start | bytes 638984 | tf_op jit(solution)/shard_map/ppermute | solution.py:39
  31.7 6.1 %collective-permute-start.5 = (bf16[192,512]{1,0:T(8,128)(2,1)S(1)}, bf16[192,512]{1,0:T(8,128)(2,1)S(1)}, u32[]{:S(2)}, u32[]{:S(2)}) collective-permute-start(bf16[192,512]{1,0:T(8,128)(2,1)S(1)} %get-tuple-element.53), channel_id=1, source_target_pairs={{0,192},{64,0},{128,64},{192,128},{1,193},{65,1},{129,65},{193,129... | collective-permute-start | bytes 589832 | tf_op jit(solution)/shard_map/ppermute | solution.py:39
  42.2 17.3 %copy-start.22 = (f32[256]{0:T(256)S(1)}, f32[256]{0:T(256)}, u32[]{:S(2)}) copy-start(f32[256]{0:T(256)} %param.31) | copy-start | bytes 3076
  42.2 11.1 %collective-permute-start.6 = (bf16[400,512]{1,0:T(8,128)(2,1)}, bf16[400,512]{1,0:T(8,128)(2,1)S(1)}, u32[]{:S(2)}, u32[]{:S(2)}) collective-permute-start(bf16[400,512]{1,0:T(8,128)(2,1)} %get-tuple-element.54), channel_id=1, source_target_pairs={{0,64},{64,128},{128,192},{192,0},{1,65},{65,129},{129,193},{193,1... | collective-permute-start | bytes 1228808 | tf_op jit(solution)/shard_map/ppermute | solution.py:39
  42.3 11.4 %collective-permute-start.7 = (bf16[400,512]{1,0:T(8,128)(2,1)}, bf16[400,512]{1,0:T(8,128)(2,1)S(1)}, u32[]{:S(2)}, u32[]{:S(2)}) collective-permute-start(bf16[400,512]{1,0:T(8,128)(2,1)} %get-tuple-element.55), channel_id=1, source_target_pairs={{0,192},{64,0},{128,64},{192,128},{1,193},{65,1},{129,65},{193,129... | collective-permute-start | bytes 1228808 | tf_op jit(solution)/shard_map/ppermute | solution.py:39
  55.9 7.6 %collective-permute-start.8 = (bf16[112,512]{1,0:T(8,128)(2,1)}, bf16[112,512]{1,0:T(8,128)(2,1)S(1)}, u32[]{:S(2)}, u32[]{:S(2)}) collective-permute-start(bf16[112,512]{1,0:T(8,128)(2,1)} %get-tuple-element.57), channel_id=1, source_target_pairs={{0,16},{16,32},{32,48},{48,0},{1,17},{17,33},{33,49},{49,1},{2,18}... | collective-permute-start | bytes 344072 | tf_op jit(solution)/shard_map/ppermute | solution.py:39
  56.1 11.8 %collective-permute-start.9 = (bf16[112,512]{1,0:T(8,128)(2,1)}, bf16[112,512]{1,0:T(8,128)(2,1)S(1)}, u32[]{:S(2)}, u32[]{:S(2)}) collective-permute-start(bf16[112,512]{1,0:T(8,128)(2,1)} %get-tuple-element.58), channel_id=1, source_target_pairs={{0,32},{16,48},{32,0},{48,16},{1,33},{17,49},{33,1},{49,17},{2,34}... | collective-permute-start | bytes 344072 | tf_op jit(solution)/shard_map/ppermute | solution.py:39
  58.8 9.2 %collective-permute-start.10 = (bf16[112,512]{1,0:T(8,128)(2,1)}, bf16[112,512]{1,0:T(8,128)(2,1)S(1)}, u32[]{:S(2)}, u32[]{:S(2)}) collective-permute-start(bf16[112,512]{1,0:T(8,128)(2,1)} %get-tuple-element.59), channel_id=1, source_target_pairs={{0,48},{16,0},{32,16},{48,32},{1,49},{17,1},{33,17},{49,33},{2,50}... | collective-permute-start | bytes 344072 | tf_op jit(solution)/shard_map/ppermute | solution.py:39
  68.9 2.7 %collective-permute-start.11 = (f32[16,512]{1,0:T(8,128)S(1)}, f32[16,512]{1,0:T(8,128)S(1)}, u32[]{:S(2)}, u32[]{:S(2)}) collective-permute-start(f32[16,512]{1,0:T(8,128)S(1)} %get-tuple-element.66.own), channel_id=1, source_target_pairs={{0,8},{8,0},{1,9},{9,1},{2,10},{10,2},{3,11},{11,3},{4,12},{12,4},... | collective-permute-start | bytes 98312 | tf_op jit(solution)/shard_map/ppermute | solution.py:43
  70.8 2.2 %collective-permute-start.12 = (bf16[2,48,512]{2,1,0:T(8,128)(2,1)S(1)}, bf16[2,48,512]{2,1,0:T(8,128)(2,1)S(1)}, u32[]{:S(2)}, u32[]{:S(2)}) collective-permute-start(bf16[2,48,512]{2,1,0:T(8,128)(2,1)S(1)} %get-tuple-element.79), channel_id=1, source_target_pairs={{0,0},{1,32},{2,64},{3,96},{4,128},{5,160},{6,192},{7,224},{8,8},{... | collective-permute-start | bytes 294920 | tf_op jit(solution)/shard_map/ppermute | solution.py:539
  73.0 13.0 %collective-permute-start.15 = (bf16[112,512]{1,0:T(8,128)(2,1)S(1)}, bf16[112,512]{1,0:T(8,128)(2,1)S(1)}, u32[]{:S(2)}, u32[]{:S(2)}) collective-permute-start(bf16[112,512]{1,0:T(8,128)(2,1)S(1)} %join.1.refs_0_), channel_id=1, source_target_pairs={{0,48},{16,0},{32,16},{48,32},{1,49},{17,1},{33,17},{49,33},{2,50}... | collective-permute-start | bytes 344072 | tf_op jit(solution)/shard_map/ppermute | solution.py:39
  83.7 10.8 %collective-permute-start.14 = (bf16[112,512]{1,0:T(8,128)(2,1)S(1)}, bf16[112,512]{1,0:T(8,128)(2,1)S(1)}, u32[]{:S(2)}, u32[]{:S(2)}) collective-permute-start(bf16[112,512]{1,0:T(8,128)(2,1)S(1)} %join.1.refs_0_), channel_id=1, source_target_pairs={{0,32},{16,48},{32,0},{48,16},{1,33},{17,49},{33,1},{49,17},{2,34}... | collective-permute-start | bytes 344072 | tf_op jit(solution)/shard_map/ppermute | solution.py:39
  83.7 10.8 %collective-permute-start.13 = (bf16[112,512]{1,0:T(8,128)(2,1)S(1)}, bf16[112,512]{1,0:T(8,128)(2,1)S(1)}, u32[]{:S(2)}, u32[]{:S(2)}) collective-permute-start(bf16[112,512]{1,0:T(8,128)(2,1)S(1)} %join.1.refs_0_), channel_id=1, source_target_pairs={{0,16},{16,32},{32,48},{48,0},{1,17},{17,33},{33,49},{49,1},{2,18}... | collective-permute-start | bytes 344072 | tf_op jit(solution)/shard_map/ppermute | solution.py:39
  94.7 10.7 %collective-permute-start.18 = (bf16[112,1024]{1,0:T(8,128)(2,1)S(1)}, bf16[112,1024]{1,0:T(8,128)(2,1)S(1)}, u32[]{:S(2)}, u32[]{:S(2)}) collective-permute-start(bf16[112,1024]{1,0:T(8,128)(2,1)S(1)} %get-tuple-element.81.refs_0_), channel_id=1, source_target_pairs={{0,64},{64,128},{128,192},{192,0},{1,65},{65,129},{129,193},{193,1... | collective-permute-start | bytes 688136 | tf_op jit(solution)/shard_map/ppermute | solution.py:39
  96.5 7.5 %collective-permute-start.24 = (bf16[96,1024]{1,0:T(8,128)(2,1)S(1)}, bf16[96,1024]{1,0:T(8,128)(2,1)S(1)}, u32[]{:S(2)}, u32[]{:S(2)}) collective-permute-start(bf16[96,1024]{1,0:T(8,128)(2,1)S(1)} %get-tuple-element.82.refs_2_), channel_id=1, source_target_pairs={{0,192},{64,0},{128,64},{192,128},{1,193},{65,1},{129,65},{193,129... | collective-permute-start | bytes 589832 | tf_op jit(solution)/shard_map/ppermute | solution.py:39
  99.0 9.1 %collective-permute-start.20 = (bf16[96,1024]{1,0:T(8,128)(2,1)S(1)}, bf16[96,1024]{1,0:T(8,128)(2,1)}, u32[]{:S(2)}, u32[]{:S(2)}) collective-permute-start(bf16[96,1024]{1,0:T(8,128)(2,1)S(1)} %get-tuple-element.82.refs_2_), channel_id=1, source_target_pairs={{0,64},{64,128},{128,192},{192,0},{1,65},{65,129},{129,193},{193,1... | collective-permute-start | bytes 589832 | tf_op jit(solution)/shard_map/ppermute | solution.py:39
  99.3 10.0 %collective-permute-start.17 = (bf16[96,1024]{1,0:T(8,128)(2,1)S(1)}, bf16[96,1024]{1,0:T(8,128)(2,1)S(1)}, u32[]{:S(2)}, u32[]{:S(2)}) collective-permute-start(bf16[96,1024]{1,0:T(8,128)(2,1)S(1)} %get-tuple-element.82.refs_2_), channel_id=1, source_target_pairs={{0,8},{8,0},{1,9},{9,1},{2,10},{10,2},{3,11},{11,3},{4,12},{12,4},... | collective-permute-start | bytes 589832 | tf_op jit(solution)/shard_map/ppermute | solution.py:43
  101.5 11.9 %collective-permute-start.22 = (bf16[112,1024]{1,0:T(8,128)(2,1)S(1)}, bf16[112,1024]{1,0:T(8,128)(2,1)S(1)}, u32[]{:S(2)}, u32[]{:S(2)}) collective-permute-start(bf16[112,1024]{1,0:T(8,128)(2,1)S(1)} %get-tuple-element.81.refs_0_), channel_id=1, source_target_pairs={{0,192},{64,0},{128,64},{192,128},{1,193},{65,1},{129,65},{193,129... | collective-permute-start | bytes 688136 | tf_op jit(solution)/shard_map/ppermute | solution.py:39
  104.0 9.4 %collective-permute-start.16 = (bf16[112,1024]{1,0:T(8,128)(2,1)S(1)}, bf16[112,1024]{1,0:T(8,128)(2,1)S(1)}, u32[]{:S(2)}, u32[]{:S(2)}) collective-permute-start(bf16[112,1024]{1,0:T(8,128)(2,1)S(1)} %get-tuple-element.81.refs_0_), channel_id=1, source_target_pairs={{0,8},{8,0},{1,9},{9,1},{2,10},{10,2},{3,11},{11,3},{4,12},{12,4},... | collective-permute-start | bytes 688136 | tf_op jit(solution)/shard_map/ppermute | solution.py:43
  105.4 8.5 %collective-permute-start.26 = (bf16[112,1024]{1,0:T(8,128)(2,1)S(1)}, bf16[112,1024]{1,0:T(8,128)(2,1)S(1)}, u32[]{:S(2)}, u32[]{:S(2)}) collective-permute-start(bf16[112,1024]{1,0:T(8,128)(2,1)S(1)} %collective-permute-done.18.refs_4_), channel_id=1, source_target_pairs={{0,64},{64,128},{128,192},{192,0},{1,65},{65,129},{129,193},{193,1... | collective-permute-start | bytes 688136 | tf_op jit(solution)/shard_map/ppermute | solution.py:39
  108.1 6.5 %collective-permute-start.28 = (bf16[96,1024]{1,0:T(8,128)(2,1)S(1)}, bf16[96,1024]{1,0:T(8,128)(2,1)}, u32[]{:S(2)}, u32[]{:S(2)}) collective-permute-start(bf16[96,1024]{1,0:T(8,128)(2,1)S(1)} %collective-permute-done.24.refs_10_), channel_id=1, source_target_pairs={{0,192},{64,0},{128,64},{192,128},{1,193},{65,1},{129,65},{193,129... | collective-permute-start | bytes 589832 | tf_op jit(solution)/shard_map/ppermute | solution.py:39
  110.0 5.6 %collective-permute-start.25 = (bf16[96,1024]{1,0:T(8,128)(2,1)S(1)}, bf16[96,1024]{1,0:T(8,128)(2,1)S(1)}, u32[]{:S(2)}, u32[]{:S(2)}) collective-permute-start(bf16[96,1024]{1,0:T(8,128)(2,1)S(1)} %collective-permute-done.24.refs_10_), channel_id=1, source_target_pairs={{0,8},{8,0},{1,9},{9,1},{2,10},{10,2},{3,11},{11,3},{4,12},{12,4},... | collective-permute-start | bytes 589832 | tf_op jit(solution)/shard_map/ppermute | solution.py:43
  113.4 3.6 %collective-permute-start.23 = (bf16[112,1024]{1,0:T(8,128)(2,1)S(1)}, bf16[112,1024]{1,0:T(8,128)(2,1)S(1)}, u32[]{:S(2)}, u32[]{:S(2)}) collective-permute-start(bf16[112,1024]{1,0:T(8,128)(2,1)S(1)} %collective-permute-done.22.refs_8_), channel_id=1, source_target_pairs={{0,8},{8,0},{1,9},{9,1},{2,10},{10,2},{3,11},{11,3},{4,12},{12,4},... | collective-permute-start | bytes 688136 | tf_op jit(solution)/shard_map/ppermute | solution.py:43
  113.4 3.6 %collective-permute-start.19 = (bf16[112,1024]{1,0:T(8,128)(2,1)S(1)}, bf16[112,1024]{1,0:T(8,128)(2,1)}, u32[]{:S(2)}, u32[]{:S(2)}) collective-permute-start(bf16[112,1024]{1,0:T(8,128)(2,1)S(1)} %collective-permute-done.18.refs_4_), channel_id=1, source_target_pairs={{0,8},{8,0},{1,9},{9,1},{2,10},{10,2},{3,11},{11,3},{4,12},{12,4},... | collective-permute-start | bytes 688136 | tf_op jit(solution)/shard_map/ppermute | solution.py:43
  113.9 4.2 %collective-permute-start.27 = (bf16[112,1024]{1,0:T(8,128)(2,1)S(1)}, bf16[112,1024]{1,0:T(8,128)(2,1)}, u32[]{:S(2)}, u32[]{:S(2)}) collective-permute-start(bf16[112,1024]{1,0:T(8,128)(2,1)S(1)} %collective-permute-done.26.refs_12_), channel_id=1, source_target_pairs={{0,8},{8,0},{1,9},{9,1},{2,10},{10,2},{3,11},{11,3},{4,12},{12,4},... | collective-permute-start | bytes 688136 | tf_op jit(solution)/shard_map/ppermute | solution.py:43
  114.6 2.4 %collective-permute-start.21 = (bf16[96,1024]{1,0:T(8,128)(2,1)}, bf16[96,1024]{1,0:T(8,128)(2,1)}, u32[]{:S(2)}, u32[]{:S(2)}) collective-permute-start(bf16[96,1024]{1,0:T(8,128)(2,1)} %collective-permute-done.20.refs_6_), channel_id=1, source_target_pairs={{0,8},{8,0},{1,9},{9,1},{2,10},{10,2},{3,11},{11,3},{4,12},{12,4},... | collective-permute-start | bytes 589832 | tf_op jit(solution)/shard_map/ppermute | solution.py:43
  116.2 1.8 %collective-permute-start.29 = (bf16[96,1024]{1,0:T(8,128)(2,1)}, bf16[96,1024]{1,0:T(8,128)(2,1)}, u32[]{:S(2)}, u32[]{:S(2)}) collective-permute-start(bf16[96,1024]{1,0:T(8,128)(2,1)} %collective-permute-done.28.refs_14_), channel_id=1, source_target_pairs={{0,8},{8,0},{1,9},{9,1},{2,10},{10,2},{3,11},{11,3},{4,12},{12,4},... | collective-permute-start | bytes 589832 | tf_op jit(solution)/shard_map/ppermute | solution.py:43
  (25 other events, 113.2 us)
Sparse Core Ops, SparseCore 0:
  26.9 64.7 all-gather.1

commit v3 on v2

v3 whole, which is shorter than its diff:
```python
import jax
import jax.numpy as jnp
from jax import lax
from jax.experimental import pallas as pl
from jax.experimental.pallas import tpu as pltpu
from jax.sharding import Mesh, PartitionSpec as P

beta_one = 0.9
beta_two = 0.95
learn_rate = 0.1
decay_rate = 0.1
eps = 1e-08
adam_step = 12

AXES = ("x", "zl", "core", "y", "zh")
SIZES = (4, 4, 2, 4, 2)
DP = AXES[:3]
GROUP = AXES[3:]
NX, NZ, NC, NY, NH = SIZES
EXTRA = 16

SCALARS = pl.BlockSpec(memory_space=pltpu.SMEM)
LOCAL = pl.BlockSpec(memory_space=pltpu.VMEM)
HELD = pl.BlockSpec(memory_space=pltpu.VMEM)
FAR = pl.BlockSpec(memory_space=pltpu.HBM)


def adamw(weight, moment, second, grad, factor, decay):
    moment_new = beta_one * moment + (1.0 - beta_one) * grad
    second_new = beta_two * second + (1.0 - beta_two) * grad * grad
    corrected = moment_new / (1.0 - beta_one**adam_step)
    scaled = second_new / (1.0 - beta_two**adam_step)
    weight_new = weight - learn_rate * factor * (
        corrected / (jnp.sqrt(scaled) + eps) + decay * weight
    )
    return (weight_new, moment_new, second_new)


def shift(value, axis, size, step):
    return lax.ppermute(value, axis, [(i, (i + step) % size) for i in range(size)])


def swap_with(value, axis, size, step):
    return lax.ppermute(value, axis, [(i, i ^ step) for i in range(size)])


def swap_core(value):
    return lax.ppermute(value, "core", [(0, 1), (1, 0)])


def flat(x, zl, core, y, zh):
    return (((x * NZ + zl) * NC + core) * NY + y) * NH + zh


def to_owner_group(step):
    pairs = []
    for x in range(NX):
        for zl in range(NZ):
            a, b = zl // 2, zl % 2
            for core in range(NC):
                for y in range(NY):
                    for zh in range(NH):
                        to = flat((x + y) % NX, (2 * zh + b) ^ step, core, x, a)
                        pairs.append((flat(x, zl, core, y, zh), to))
    return pairs


def after(value, *others):
    return lax.optimization_barrier((value,) + others)[0]


def to_float(value):
    return value.astype(jnp.float32)


def to_low(value):
    return value.astype(jnp.bfloat16)


def numbers(*values):
    return jnp.stack([jnp.asarray(v, jnp.int32) for v in values])


def kernel(body, outs, ins, scratch=(), aliases=None, name=None, cost=0, room=16):
    shapes = []
    for spec, shape, dtype in outs:
        if spec is HELD:
            shapes.append(pltpu.VMEM(shape, dtype))
        else:
            shapes.append(jax.ShapeDtypeStruct(shape, dtype))
    call = pl.pallas_call(
        body,
        out_shape=shapes,
        in_specs=ins,
        out_specs=[spec for spec, _, _ in outs],
        scratch_shapes=list(scratch),
        input_output_aliases=aliases or {},
        cost_estimate=pl.CostEstimate(flops=0, bytes_accessed=cost, transcendentals=0),
        compiler_params=pltpu.CompilerParams(vmem_limit_bytes=room * 2**20),
        name=name,
    )

    def run(*values):
        placed = []
        for spec, value in zip(ins, values):
            if spec is HELD:
                value = pltpu.with_memory_space_constraint(value, pltpu.VMEM)
            elif spec is FAR:
                value = pltpu.with_memory_space_constraint(value, pltpu.HBM)
            placed.append(value)
        return call(*placed)

    return run


def fetch(sources, targets, sems):
    copies = [
        pltpu.make_async_copy(a, b, sems.at[n]) for n, (a, b) in enumerate(zip(sources, targets))
    ]
    for copy in copies:
        copy.start()
    return copies


def product_kernel(place, hidden, grads, far_keep, far_send, keep, send, raw, left, right, sems):
    tokens, experts, wide = hidden.shape
    wide = wide // NX
    rows = wide // (NZ * NC)
    blocks = sems.shape[0]
    spans = [pl.ds(p * (tokens // blocks), tokens // blocks) for p in range(blocks)]
    copies = fetch([hidden.at[at] for at in spans], [raw.at[at] for at in spans], sems)
    for at, copy in zip(spans, copies):
        right[:, at, :] = jnp.swapaxes(grads[at], 0, 1)
        copy.wait()
        left[:, at, :] = jnp.swapaxes(raw[at], 0, 1)
    for n in range(NX):
        at = pl.multiple_of(place[1 + n] * wide, 128)
        for e in range(experts):
            value = lax.dot_general(
                left[e, :, pl.ds(at, wide)],
                right[e],
                (((0,), (0,)), ((), ())),
                preferred_element_type=jnp.float32,
            )
            mine, other = (far_keep, far_send) if n == 0 else (keep, send)
            m = max(n - 1, 0)
            for zl in range(NZ):
                first = value[2 * zl * rows : (2 * zl + 1) * rows, :]
                second = value[(2 * zl + 1) * rows : (2 * zl + 2) * rows, :]
                to = (e * NZ + zl) * rows
                mine[m, to : to + rows, :] = to_low(jnp.where(place[0] == 0, first, second))
                other[m, to : to + rows, :] = to_low(jnp.where(place[0] == 0, second, first))


def product(place, hidden_act, out_grad):
    tokens, experts, hidden = hidden_act.shape
    feats = out_grad.shape[2]
    rows = experts * hidden // NX // NC
    one, rest = (1, rows, feats), (NX - 1, rows, feats)
    call = kernel(
        product_kernel,
        [(HELD, shape, jnp.bfloat16) for shape in (one, one, rest, rest)],
        [SCALARS, FAR, LOCAL],
        scratch=[
            pltpu.VMEM(hidden_act.shape, jnp.bfloat16),
            pltpu.VMEM((experts, tokens, hidden), jnp.bfloat16),
            pltpu.VMEM((experts, tokens, feats), jnp.bfloat16),
            pltpu.SemaphoreType.DMA((4,)),
        ],
        name="product",
        room=40,
    )
    return call(place, hidden_act, out_grad)


def parts_kernel(ids, w, m, v, sw, sm, sv, out, wide):
    tall, cols = w.shape
    wide[...] = jnp.zeros_like(wide)
    at = lax.broadcasted_iota(jnp.int32, (tall, cols), 0)
    for n, (router, small) in enumerate(((w, sw), (m, sm), (v, sv))):
        values = [
            jnp.sum(jnp.where(at == ids[e], router[...], 0.0), axis=0, keepdims=True)
            for e in range(2)
        ] + [small[i : i + 1, :] for i in range(2)]
        for part, value in enumerate(values):
            lanes = slice(part * cols, (part + 1) * cols)
            top = to_float(to_low(value))
            wide[8 + 2 * n : 9 + 2 * n, lanes] = top
            wide[9 + 2 * n : 10 + 2 * n, lanes] = value - top
    out[...] = to_low(wide[...])


def selected_parts(ids, *values):
    shape = (EXTRA, 512)
    call = kernel(
        parts_kernel,
        [(HELD, shape, jnp.bfloat16)],
        [SCALARS] + [LOCAL] * len(values),
        scratch=[pltpu.VMEM(shape, jnp.float32)],
        name="parts",
        cost=2 * 2**20,
    )
    return call(ids, *values)[0]


def extras_kernel(router, small, out, wide):
    cols, shard = 128, 256
    wide[...] = jnp.zeros_like(wide)
    for x in range(NX):
        for d in range(NZ * NC):
            at = x * NZ * NC + d
            for e in range(2):
                wide[x, d : d + 1, e * cols : (e + 1) * cols] = router[
                    e : e + 1, at * cols : (at + 1) * cols
                ]
            wide[x, d : d + 1, 2 * cols : 2 * cols + shard] = small[
                0:1, at * shard : (at + 1) * shard
            ]
    out[...] = to_low(wide[...])


def pack_extras(router_grads, small_grads):
    feats = 512
    call = kernel(
        extras_kernel,
        [(LOCAL, (NX, EXTRA, feats), jnp.bfloat16)],
        [LOCAL, LOCAL],
        scratch=[pltpu.VMEM((NX, EXTRA, feats), jnp.float32)],
        name="extras",
    )
    return call(router_grads, small_grads)[0]


def both_cores(own, theirs, start, rows):
    at = pl.ds(start, rows)
    return to_float(own[at, :]) + to_float(theirs[at, :])


def far_kernel(place, own, theirs, extras, up, down):
    half = down.shape[0]
    for e, out in enumerate((up, down)):
        out[:half, :] = to_low(both_cores(own.at[0], theirs.at[0], e * half, half))
    up[half:, :] = extras[place[0]]


def pair_far(place, own, theirs, extras):
    _, rows, feats = own.shape
    call = kernel(
        far_kernel,
        [(HELD, (rows // 2 + EXTRA, feats), jnp.bfloat16), (HELD, (rows // 2, feats), jnp.bfloat16)],
        [SCALARS] + [HELD] * 3,
        name="pair_far",
    )
    return call(place, own, theirs, extras)


def near_kernel(place, own, theirs, extras, up, down, router, hop, to_up, to_down, routers):
    routers[0] = router[...]
    routers[1] = hop[...]
    half = down.shape[0]
    for n, (more, out) in enumerate(((up, to_up), (down, to_down))):
        for e in range(2):
            total = both_cores(own.at[n], theirs.at[n], e * half, half)
            if e == n:
                total = total + to_float(more[:half, :])
            out[e * half : (e + 1) * half, :] = to_low(total)
    to_up[2 * half :, :] = to_low(to_float(extras[place[0]]) + to_float(up[half:, :]))
    to_down[2 * half :, :] = extras[place[1]]


def pair_near(place, own, theirs, extras, up, down, router, hop):
    _, rows, feats = own.shape
    call = kernel(
        near_kernel,
        [(HELD, (rows + EXTRA, feats), jnp.bfloat16)] * 2
        + [(HELD, (2, *router.shape), jnp.bfloat16)],
        [SCALARS] + [HELD] * 7,
        name="pair_near",
    )
    return call(place, own, theirs, extras, up, down, router, hop)


def total_kernel(
    place, own, theirs, extras, state, r1, r2, router, hop, mine, s1, s2, s3, routers
):
    routers[:2] = router[...]
    routers[2:] = hop[...]
    _, count, feats = own.shape
    rows = count // (2 * NZ)
    more = to_float(extras[place[0]]) + to_float(r1[count:, :]) + to_float(r2[count:, :])
    more = more + to_float(state[...])
    for j, out in enumerate((mine, s1, s2, s3)):
        zl = lax.rem(place[1] + j, NZ)
        for e in range(2):
            at = pl.multiple_of((e * NZ + zl) * rows, 16)
            total = both_cores(own.at[2], theirs.at[2], at, rows)
            for r in (r1, r2):
                total = total + to_float(r[pl.ds(at, rows), :])
            out[e * rows : (e + 1) * rows, :] = total.astype(out.dtype)
        out[2 * rows :, :] = more.astype(out.dtype)


def total_up(place, own, theirs, extras, state, arrived, router, hop):
    _, count, feats = own.shape
    rows = count // NZ + EXTRA
    call = kernel(
        total_kernel,
        [(LOCAL, (rows, feats), jnp.float32)]
        + [(HELD, (rows, feats), jnp.bfloat16)] * 3
        + [(HELD, (4, *router.shape[1:]), jnp.bfloat16)],
        [SCALARS] + [HELD] * 8,
        name="total",
    )
    return call(place, own, theirs, extras, state, *arrived, router, hop)


def rate_at(spot, lengths, rate):
    factor = jnp.zeros(spot.shape, jnp.float32)
    begin = jnp.int32(0)
    for k in range(lengths.shape[0]):
        end = begin + lengths[k]
        factor = jnp.where((spot >= begin) & (spot < end), rate[k], factor)
        begin = end
    return factor


def expert_kernel(
    place, lengths, rate, r1, r2, r3, router, hop, mine_far, w_far, m_far, v_far, *refs
):
    new, moment, second, low, extras, more, routers, mine, w, m, v, sems = refs
    experts, rows, feats = w.shape
    copies = fetch((mine_far, w_far, m_far, v_far), (mine, w, m, v), sems)
    routers[:4] = router[...]
    routers[4:] = hop[...]
    copies[0].wait()

    ix, iz, ic = place[0], place[1], place[2]
    blocks = [to_float(r[experts * rows :, :]) for r in (mine, r1, r2, r3)]
    sums = blocks[0] + blocks[1] + blocks[2] + blocks[3]
    more[...] = sums
    shape = blocks[0].shape
    row = lax.broadcasted_iota(jnp.int32, shape, 0)
    lane = lax.broadcasted_iota(jnp.int32, shape, 1)
    state = [jnp.zeros(shape, jnp.float32) for _ in range(4)]
    for j, block in enumerate(blocks):
        zl = lax.rem(iz - j + NZ, NZ)
        here = row == ix * NZ + zl
        for n in range(3):
            value = block[8 + 2 * n : 9 + 2 * n, :] + block[9 + 2 * n : 10 + 2 * n, :]
            state[n] = jnp.where(here, value, state[n])
        grad = jnp.sum(jnp.where(row == zl * NC + ic, sums, 0.0), axis=0, keepdims=True)
        state[3] = jnp.where(here, grad, state[3])
    half = feats // 2
    spot = (row * NC + ic) * half + lane - half
    factor = jnp.where(lane < half, 1.0, rate_at(spot, lengths, rate))
    decay = jnp.where(lane < half, decay_rate, 0.0)
    extras[...] = to_low(adamw(*state, factor, decay)[0])

    for copy in copies[1:]:
        copy.wait()
    for e in range(experts):
        at = slice(e * rows, (e + 1) * rows)
        grad = mine[at, :] + to_float(r1[at, :]) + to_float(r2[at, :]) + to_float(r3[at, :])
        weight, first, squared = adamw(w[e], m[e], v[e], grad, 1.0, decay_rate)
        new[e] = weight
        moment[e] = first
        second[e] = squared
        low[e] = to_low(weight)


def expert_update(place, lengths, rate, mine, arrived, w, m, v, router, hop):
    state = (LOCAL, w.shape, jnp.float32)
    feats = w.shape[2]
    call = kernel(
        expert_kernel,
        [state, state, state]
        + [
            (HELD, w.shape, jnp.bfloat16),
            (HELD, (EXTRA, feats), jnp.bfloat16),
            (HELD, (EXTRA, feats), jnp.float32),
            (HELD, (8, *router.shape[1:]), jnp.bfloat16),
        ],
        [SCALARS] * 3 + [HELD] * 5 + [FAR] * 4,
        scratch=[pltpu.VMEM(mine.shape, jnp.float32)]
        + [pltpu.VMEM(w.shape, jnp.float32)] * 3
        + [pltpu.SemaphoreType.DMA((4,))],
        name="expert_update",
    )
    return call(place, lengths, rate, *arrived, router, hop, mine, w, m, v)


def others_kernel(place, ids, lengths, rate, more, w, m, v, sw, sm, sv, *refs):
    new, moment, second, small_new, small_moment, small_second, token, held = refs
    token[...] = jnp.zeros_like(token)
    tall, cols = w.shape
    shard_rows = sw.shape[0]
    rows = lax.broadcasted_iota(jnp.int32, more.shape, 0)
    grad_row = jnp.sum(jnp.where(rows == place[0], more[...], 0.0), axis=0, keepdims=True)
    at = lax.broadcasted_iota(jnp.int32, (tall, cols), 0)
    grad = jnp.zeros((tall, cols), jnp.float32)
    for e in range(ids.shape[0]):
        part = grad_row[:, e * cols : (e + 1) * cols]
        grad = grad + jnp.where(at == ids[e], part, 0.0)
    for i in range(shard_rows):
        part = (ids.shape[0] + i) * cols
        held[i : i + 1, :] = grad_row[:, part : part + cols]
    weight, first, squared = adamw(w[...], m[...], v[...], grad, 1.0, decay_rate)
    new[...] = weight
    moment[...] = first
    second[...] = squared
    spot = (
        place[1]
        + lax.broadcasted_iota(jnp.int32, (shard_rows, cols), 0) * cols
        + lax.broadcasted_iota(jnp.int32, (shard_rows, cols), 1)
    )
    factor = rate_at(spot, lengths, rate)
    weight, first, squared = adamw(
        sw[...], sm[...], sv[...], held[:shard_rows, :], factor, 0.0
    )
    small_new[...] = weight
    small_moment[...] = first
    small_second[...] = squared


def others_update(place, ids, lengths, rate, more, router, small):
    cols = router[0].shape[1]
    call = kernel(
        others_kernel,
        [(LOCAL, r.shape, jnp.float32) for r in (*router, *small)]
        + [(HELD, (8, cols), jnp.float32)],
        [SCALARS] * 4 + [HELD] + [LOCAL] * 6,
        scratch=[pltpu.VMEM((8, cols), jnp.float32)],
        name="others_update",
        cost=4 * 2**20,
    )
    return call(place, ids, lengths, rate, more, *router, *small)


def halve_kernel(place, *refs):
    pieces, (extras, token, router, hop, upper, lower, routers) = refs[:NZ], refs[NZ:]
    routers[:8] = router[...]
    routers[8:] = hop[...]
    experts, rows, feats = pieces[0].shape
    for s in range(NZ):
        for q in range(NZ):

            @pl.when((place[0] ^ q) == s)
            def _():
                for e, out in enumerate((upper, lower)):
                    to = (s % 2) * rows
                    out[to : to + rows, (s // 2) * feats : (s // 2 + 1) * feats] = pieces[q][e]

    upper[2 * rows :, :feats] = extras[...]
    upper[2 * rows :, feats:] = jnp.zeros((EXTRA, feats), jnp.bfloat16)


def halve(place, pieces, extras, token, router, hop):
    experts, rows, feats = pieces[0].shape
    call = kernel(
        halve_kernel,
        [
            (LOCAL, (2 * rows + EXTRA, NH * feats), jnp.bfloat16),
            (LOCAL, (2 * rows, NH * feats), jnp.bfloat16),
            (HELD, (16, *router.shape[1:]), jnp.bfloat16),
        ],
        [SCALARS] + [HELD] * (NZ + 4),
        name="halve",
    )
    return call(place, *pieces, extras, token, router, hop)


def lay(place, pieces, out, sems):
    rows = out.shape[3]
    copies = []
    for e, n, x, piece in pieces:
        core = place[0] ^ n
        wide = piece.shape[1]
        at = pl.multiple_of(x * wide, wide)
        for b in range(2):
            copies.append(
                pltpu.make_async_copy(
                    piece.at[b * rows : (b + 1) * rows, :],
                    out.at[e, b, core, :, pl.ds(at, wide)],
                    sems.at[len(copies)],
                )
            )
            copies[-1].start()
    return copies


def spread(core, row, d, lines, packed):
    cols = packed.shape[1]
    for e in range(2):
        at = pl.multiple_of(d * cols, cols)
        lines[e : e + 1, pl.ds(at, cols)] = row[:, e * cols : (e + 1) * cols]
    for i in range(2):
        packed[pl.ds(2 * d + i, 1), :] = row[:, (2 + i) * cols : (3 + i) * cols]


def early_kernel(place, *refs):
    far, routers, refs = refs[:12], refs[12:14], refs[14:]
    (out, patched, lines, packed), refs = refs[:4], refs[4:]
    pieces, (sems, out_sems, router_sems) = refs[:12], refs[12:]
    arriving = fetch(far, pieces, sems)
    lines[...] = jnp.zeros_like(lines)
    copies = []
    cols = packed.shape[1]
    for n, blocks in enumerate(routers):
        for z in range(NZ):
            for x in range(NX):
                d = ((place[4] ^ x) * NZ + (place[5] ^ z)) * NC + (place[0] ^ n)
                at = pl.ds(pl.multiple_of(d * cols, cols), cols)
                copies.append(
                    pltpu.make_async_copy(
                        blocks.at[z * NX + x], patched.at[:, at], router_sems.at[len(copies)]
                    )
                )
                copies[-1].start()
    for n, piece in enumerate(pieces):
        arriving[n].wait()
        spot = (n // 2 % 2, n % 2, place[1 + n // 4], piece)
        copies += lay(place, [spot], out, out_sems.at[n])
    for n in range(2):
        core = place[0] ^ n
        extras = sum(to_float(p[p.shape[0] - EXTRA :, : p.shape[1] // NH]) for p in pieces[n::4])
        for r in range(NX * NZ):
            spread(core, extras[r : r + 1, :], r * NC + core, lines, packed)
    for copy in copies:
        copy.wait()


def early(place, pieces, routers):
    rows, wide = pieces[2].shape
    n_dp = NX * NZ * NC
    tall, cols = routers[0].shape[1:]
    call = kernel(
        early_kernel,
        [
            (FAR, (2, 2, NC, rows // 2, NY * wide), jnp.bfloat16),
            (FAR, (tall, n_dp * cols), jnp.bfloat16),
            (HELD, (8, n_dp * cols), jnp.float32),
            (HELD, (2 * n_dp, cols), jnp.float32),
        ],
        [SCALARS] + [FAR] * len(pieces) + [HELD] * 2,
        scratch=[pltpu.VMEM(p.shape, p.dtype) for p in pieces]
        + [
            pltpu.SemaphoreType.DMA((len(pieces),)),
            pltpu.SemaphoreType.DMA((len(pieces), 2)),
            pltpu.SemaphoreType.DMA((n_dp,)),
        ],
        name="early",
        cost=2**20,
    )
    return call(place, *pieces, *routers)


def relay_kernel(upper, lower, lines, out):
    out[: upper.shape[0], :] = upper[...]
    out[upper.shape[0] :, :] = lower[...]


def relay(upper, lower, lines):
    shape = (upper.shape[0] + lower.shape[0], upper.shape[1])
    call = kernel(
        relay_kernel, [(HELD, shape, jnp.bfloat16)], [LOCAL, LOCAL, HELD], name="relay"
    )
    return call(upper, lower, lines)[0]


def late_kernel(place, ids, whole, router, lines, packed, own, other, *refs):
    out, patched, small, lines_now, packed_now, block, sems, block_sems = refs
    split = 2 * out.shape[3] + EXTRA
    starts = [pl.multiple_of(lax.div(ids[n], 16) * 16, 16) for n in range(2)]
    blocks = [patched.at[pl.ds(at, 16), :] for at in starts]
    arriving = fetch(blocks, [block.at[0], block.at[1]], block_sems)
    pieces = []
    for n, piece in enumerate((own, other)):
        pieces.append((0, n, place[1], piece.at[: split - EXTRA, :]))
        pieces.append((1, n, place[1], piece.at[split:, :]))
    copies = lay(place, pieces, out, sems)
    lines_now[...] = lines[...]
    packed_now[...] = packed[...]
    for n, piece in enumerate((own, other)):
        core = place[0] ^ n
        extras = to_float(piece[split - EXTRA : split, : piece.shape[1] // NH])
        at = lax.broadcasted_iota(jnp.int32, extras.shape, 0)
        for zl in range(NZ):
            r = place[2] * NZ + zl
            row = jnp.sum(jnp.where(at == r, extras, 0.0), axis=0, keepdims=True)
            spread(core, row, r * NC + core, lines_now, packed_now)
    small[...] = to_low(packed_now[...])
    spot = lax.broadcasted_iota(jnp.int32, block.shape[1:], 0)
    for copy in arriving:
        copy.wait()
    for n, at in enumerate(starts):
        value = to_float(block[n])
        for e in range(2):
            value = jnp.where(spot + at == ids[e], lines_now[e : e + 1, :], value)
        block[n] = to_low(value)
    for n in range(2):
        move = pltpu.make_async_copy(block.at[n], blocks[n], block_sems.at[n])
        move.start()
        move.wait()
    for copy in copies:
        copy.wait()


def late(place, ids, whole, router, lines, packed, own, other):
    call = kernel(
        late_kernel,
        [
            (FAR, whole.shape, jnp.bfloat16),
            (FAR, router.shape, jnp.bfloat16),
            (LOCAL, packed.shape, jnp.bfloat16),
        ],
        [SCALARS] * 2 + [FAR] * 2 + [HELD] * 4,
        scratch=[
            pltpu.VMEM(lines.shape, jnp.float32),
            pltpu.VMEM(packed.shape, jnp.float32),
            pltpu.VMEM((2, 16, router.shape[1]), jnp.bfloat16),
            pltpu.SemaphoreType.DMA((8,)),
            pltpu.SemaphoreType.DMA((2,)),
        ],
        aliases={2: 0, 3: 1},
        name="late",
    )
    return call(place, ids, whole, router, lines, packed, own, other)


def body(
    hidden_act,
    out_grad,
    router_grads,
    small_grads,
    expert_ids,
    small_lengths,
    small_rate,
    expert_w,
    expert_m,
    expert_v,
    router_w,
    router_m,
    router_v,
    small_w,
    small_m,
    small_v,
):
    ix, iy, iz, ic = (lax.axis_index(name) for name in ("x", "y", "zl", "core"))
    dp_index = (ix * NZ + iz) * NC + ic
    shard_len = small_w.shape[0]

    opposite, above, below = ((ix + k) % NX for k in (2, 1, 3))
    far_own, far_send, own, send = product(
        numbers(ic, opposite, above, below, ix), hidden_act, out_grad
    )

    zero = jnp.zeros_like(router_w)
    router = adamw(after(router_w, far_send), router_m, router_v, zero, 1.0, decay_rate)[0]
    router = to_low(router)

    extras = pack_extras(after(router_grads[0], far_send), small_grads)
    extras = to_low(to_float(extras) + to_float(swap_core(extras)))
    up, down = pair_far(numbers(opposite), far_own, swap_core(far_send), extras)
    up, down = shift(up, "x", NX, 1), shift(down, "x", NX, 3)
    theirs = swap_core(send)
    hop = swap_with(router, "x", NX, 1)
    up, down, router = pair_near(
        numbers(above, below), own, theirs, extras, up, down, router, hop
    )
    hop = swap_with(router, "x", NX, 2)
    arrived = [shift(up, "x", NX, 1), shift(down, "x", NX, 3)]
    router_state = (router_w, router_m, router_v)
    small_state = [s.reshape(-1, 128) for s in (small_w, small_m, small_v)]
    parts = selected_parts(expert_ids, *router_state, *small_state)
    mine, *sends, router = total_up(
        numbers(ix, iz), own, theirs, extras, parts, arrived, router, hop
    )
    hop = swap_with(router, "zl", NZ, 1)
    arrived = [shift(send, "zl", NZ, j + 1) for j, send in enumerate(sends)]
    new_expert, expert_moment, expert_second, low, extras, more, router = expert_update(
        numbers(ix, iz, ic),
        small_lengths,
        small_rate,
        mine,
        arrived,
        expert_w,
        expert_m,
        expert_v,
        router,
        hop,
    )
    hop = swap_with(router, "zl", NZ, 2)
    others = others_update(
        numbers(iz * NC + ic, dp_index * shard_len),
        expert_ids,
        small_lengths,
        small_rate,
        more,
        router_state,
        small_state,
    )
    new_router, router_moment, router_second = others[:3]
    new_small, small_moment, small_second = (s.reshape(-1) for s in others[3:6])

    first, second = (lax.ppermute(low, AXES, to_owner_group(q)) for q in (0, 2))
    pieces = [first, swap_with(first, "zl", NZ, 1), second, swap_with(second, "zl", NZ, 1)]
    upper, lower, router = halve(numbers(iz), pieces, extras, others[6], router, hop)
    from_below = shift(upper, "x", NX, 1), shift(lower, "x", NX, 1)
    from_above = shift(upper, "x", NX, 3), shift(lower, "x", NX, 3)
    pieces = []
    for piece in (upper, lower) + from_below + from_above:
        pieces += [piece, swap_core(piece)]
    places = [(ix - iy - k) % NX for k in (0, 1, 3, 2)]
    whole, router, lines, packed = early(
        numbers(ic, *places[:3], ix, iz), pieces, [router, swap_core(router)]
    )
    last = relay(shift(from_below[0], "x", NX, 1), shift(from_above[1], "x", NX, 3), lines)
    whole, router_rollout, small_rollout = late(
        numbers(ic, places[3], opposite),
        expert_ids,
        whole,
        router,
        lines,
        packed,
        last,
        swap_core(last),
    )
    expert_rollout = whole.reshape(whole.shape[0], -1, whole.shape[-1])
    small_rollout = small_rollout.reshape(-1)
    return (
        new_expert,
        expert_moment,
        expert_second,
        new_router,
        router_moment,
        router_second,
        new_small,
        small_moment,
        small_second,
        expert_rollout,
        router_rollout,
        small_rollout,
    )


def solution(mesh):
    fine = Mesh(mesh.devices.reshape(SIZES), AXES)
    placed = (
        P(DP, None, None),
        P(DP, None, GROUP),
        P(DP, None, None),
        P(DP, None),
        P(),
        P(),
        P(),
        P(None, DP, GROUP),
        P(None, DP, GROUP),
        P(None, DP, GROUP),
        P(None, DP),
        P(None, DP),
        P(None, DP),
        P(DP),
        P(DP),
        P(DP),
    )
    return jax.shard_map(
        body,
        mesh=fine,
        in_specs=placed,
        out_specs=(
            P(None, DP, GROUP),
            P(None, DP, GROUP),
            P(None, DP, GROUP),
            P(None, DP),
            P(None, DP),
            P(None, DP),
            P(DP),
            P(DP),
            P(DP),
            P(None, GROUP, None),
            P(),
            P(),
        ),
        check_vma=False,
    )
```

time: 138 us -> 116 us (0.84)
  the two profiles are of different devices: /device:TPU:1 before, /device:TPU:79 now
where the time goes in v3:
time: 116 us
  starting transfers between devices  57.3 us (49%)
  waiting for transfers between devices  30.1 us (26%)
  Pallas kernels  22.7 us (20%)
  local copies, waits for them, and re-layouts  3.89 us (3%)
  between operations  1.18 us (1%)
    ppermute x6, starting transfers between devices, swap_with(): return lax.ppermute(value, axis, [(i, i ^ step) for i in range(size)])  23 us
    pallas_call x12, Pallas kernels, run(): return call(*placed)  22.7 us
    ppermute x6, waiting for transfers between devices, swap_with(): return lax.ppermute(value, axis, [(i, i ^ step) for i in range(size)])  14.2 us
    ppermute x11, starting transfers between devices, swap_core(): return lax.ppermute(value, 'core', [(0, 1), (1, 0)])  12.4 us
    ppermute x13, starting transfers between devices, shift(): lax.ppermute(value, axis, [(i, (i + step) % size) for i in range(size)])  12.2 us
    ppermute x13, waiting for transfers between devices, shift(): lax.ppermute(value, axis, [(i, (i + step) % size) for i in range(size)])  12.1 us
    ppermute x2, starting transfers between devices, body(): first, second = (lax.ppermute(low, AXES, to_owner_group(q)) for q in (0, 2))  9.68 us
    ppermute x11, waiting for transfers between devices, swap_core(): return lax.ppermute(value, 'core', [(0, 1), (1, 0)])  3.77 us
  transfers between devices with their start and end apart: 32, of which 11 were waited for; matrix products, arithmetic and copies ran while one was open for 0% of the time, Pallas kernels for 5%

profile of v3, /device:TPU:79, one launch (start us, length us, event | category | flops | bytes accessed | tf_op | source)
XLA Modules:
  0.0 115.6 jit_solution(4846467774433393536)
XLA Ops:
  0.8 1.6 %copy-done = bf16[1024,2,512]{2,1,0:T(2,128)(2,1)S(1)} copy-done((bf16[1024,2,512]{2,1,0:T(2,128)(2,1)S(1)}, bf16[1024,2,512]{2,1,0:T(2,128)(2,1)}, u32[]{:S(2)}) %copy-start) | copy-done | bytes 2097176
  2.4 7.3 %product.1 = (bf16[1,384,512]{2,1,0:T(8,128)(2,1)S(1)}, bf16[1,384,512]{2,1,0:T(8,128)(2,1)S(1)}, bf16[3,384,512]{2,1,0:T(8,128)(2,1)S(1)}, bf16[3,384,512]{2,1,0:T(8,128)(2,1)S(1)}) custom-call(s32[5]{0:T(128)S(1)} %stack.78.place, bf16[1024,2,1536]{2,1,0:T(2,128)(2,1)} %hidden.1, bf16[1024,2,512]{2,1,0:T(2,128)(2,1)S(1)} %copy-done), custom_call_target="tpu_custom_call" | custom-call | tf_op jit(solution)/shard_map/product/pallas_call | solution.py:111
  11.2 2.4 %collective-permute-done.1 = bf16[4,16,512]{2,1,0:T(8,128)(2,1)S(1)} collective-permute-done((bf16[4,16,512]{2,1,0:T(8,128)(2,1)S(1)}, bf16[4,16,512]{2,1,0:T(8,128)(2,1)S(1)}, u32[]{:S(2)}, u32[]{:S(2)}) %collective-permute-start.1) | collective-permute-done | bytes 65568 | tf_op jit(solution)/shard_map/ppermute | solution.py:48
  14.4 2.1 %collective-permute-start.3 = (bf16[208,512]{1,0:T(8,128)(2,1)S(1)}, bf16[208,512]{1,0:T(8,128)(2,1)S(1)}, u32[]{:S(2)}, u32[]{:S(2)}) collective-permute-start(bf16[208,512]{1,0:T(8,128)(2,1)S(1)} %get-tuple-element.57), channel_id=1, source_target_pairs={{0,64},{64,128},{128,192},{192,0},{1,65},{65,129},{129,193},{193,1... | collective-permute-start | bytes 638984 | tf_op jit(solution)/shard_map/ppermute | solution.py:40
  16.8 4.5 %collective-permute-done.5.hop = bf16[128,128]{1,0:T(8,128)(2,1)S(1)} collective-permute-done((bf16[128,128]{1,0:T(8,128)(2,1)S(1)}, bf16[128,128]{1,0:T(8,128)(2,1)S(1)}, u32[]{:S(2)}, u32[]{:S(2)}) %collective-permute-start.5) | collective-permute-done | bytes 32800 | tf_op jit(solution)/shard_map/ppermute | solution.py:44
  21.3 1.7 %pair_near.1 = (bf16[400,512]{1,0:T(8,128)(2,1)}, bf16[400,512]{1,0:T(8,128)(2,1)}, bf16[2,128,128]{2,1,0:T(8,128)(2,1)S(1)}) custom-call(s32[2]{0:T(128)S(1)} %pad_add_fusion.2.place, bf16[3,384,512]{2,1,0:T(8,128)(2,1)S(1)} %get-tuple-element.52.own, bf16[3,384,512]{2,1,0:T(8,128)(2,1)S(1)} %collective-permute-done.theirs, ...), custom_call_target="tpu_custom_call" | custom-call | tf_op jit(solution)/shard_map/pair_near/pallas_call | solution.py:111
  22.9 2.6 %collective-permute-start.6 = (bf16[400,512]{1,0:T(8,128)(2,1)}, bf16[400,512]{1,0:T(8,128)(2,1)S(1)}, u32[]{:S(2)}, u32[]{:S(2)}) collective-permute-start(bf16[400,512]{1,0:T(8,128)(2,1)} %get-tuple-element.60), channel_id=1, source_target_pairs={{0,64},{64,128},{128,192},{192,0},{1,65},{65,129},{129,193},{193,1... | collective-permute-start | bytes 1228808 | tf_op jit(solution)/shard_map/ppermute | solution.py:40
  26.2 1.3 %collective-permute-start.8 = (bf16[2,128,128]{2,1,0:T(8,128)(2,1)S(1)}, bf16[2,128,128]{2,1,0:T(8,128)(2,1)S(1)}, u32[]{:S(2)}, u32[]{:S(2)}) collective-permute-start(bf16[2,128,128]{2,1,0:T(8,128)(2,1)S(1)} %get-tuple-element.62.router), channel_id=1, source_target_pairs={{0,128},{64,192},{128,0},{192,64},{1,129},{65,193},{129,1},{193,65... | collective-permute-start | bytes 196616 | tf_op jit(solution)/shard_map/ppermute | solution.py:44
  27.6 8.5 %collective-permute-done.8.hop = bf16[2,128,128]{2,1,0:T(8,128)(2,1)S(1)} collective-permute-done((bf16[2,128,128]{2,1,0:T(8,128)(2,1)S(1)}, bf16[2,128,128]{2,1,0:T(8,128)(2,1)S(1)}, u32[]{:S(2)}, u32[]{:S(2)}) %collective-permute-start.8) | collective-permute-done | bytes 65568 | tf_op jit(solution)/shard_map/ppermute | solution.py:44
  38.3 1.6 %collective-permute-start.12 = (bf16[4,128,128]{2,1,0:T(8,128)(2,1)S(1)}, bf16[4,128,128]{2,1,0:T(8,128)(2,1)S(1)}, u32[]{:S(2)}, u32[]{:S(2)}) collective-permute-start(bf16[4,128,128]{2,1,0:T(8,128)(2,1)S(1)} %get-tuple-element.66.router), channel_id=1, source_target_pairs={{0,16},{16,0},{32,48},{48,32},{1,17},{17,1},{33,49},{49,33},{2,18}... | collective-permute-start | bytes 393224 | tf_op jit(solution)/shard_map/ppermute | solution.py:44
  40.0 1.7 %collective-permute-start.11 = (bf16[112,512]{1,0:T(8,128)(2,1)S(1)}, bf16[112,512]{1,0:T(8,128)(2,1)S(1)}, u32[]{:S(2)}, u32[]{:S(2)}) collective-permute-start(bf16[112,512]{1,0:T(8,128)(2,1)S(1)} %get-tuple-element.65), channel_id=1, source_target_pairs={{0,48},{16,0},{32,16},{48,32},{1,49},{17,1},{33,17},{49,33},{2,50}... | collective-permute-start | bytes 344072 | tf_op jit(solution)/shard_map/ppermute | solution.py:40
  41.7 3.2 %collective-permute-done.9.r1 = bf16[112,512]{1,0:T(8,128)(2,1)S(1)} collective-permute-done((bf16[112,512]{1,0:T(8,128)(2,1)S(1)}, bf16[112,512]{1,0:T(8,128)(2,1)S(1)}, u32[]{:S(2)}, u32[]{:S(2)}) %collective-permute-start.9) | collective-permute-done | bytes 114720 | tf_op jit(solution)/shard_map/ppermute | solution.py:40
  45.0 2.7 %collective-permute-done.11.r3 = bf16[112,512]{1,0:T(8,128)(2,1)S(1)} collective-permute-done((bf16[112,512]{1,0:T(8,128)(2,1)S(1)}, bf16[112,512]{1,0:T(8,128)(2,1)S(1)}, u32[]{:S(2)}, u32[]{:S(2)}) %collective-permute-start.11) | collective-permute-done | bytes 114720 | tf_op jit(solution)/shard_map/ppermute | solution.py:40
  47.7 2.8 %expert_update.1 = (f32[2,48,512]{2,1,0:T(8,128)}, f32[2,48,512]{2,1,0:T(8,128)}, f32[2,48,512]{2,1,0:T(8,128)}, bf16[2,48,512]{2,1,0:T(8,128)(2,1)S(1)}, bf16[1...) custom-call(s32[3]{0:T(128)S(1)} %pad_add_fusion.place, s32[16]{0:T(128)S(1)} %copy-done.13, ...), custom_call_target="tpu_custom_call" | custom-call | tf_op jit(solution)/shard_map/expert_update/pallas_call | solution.py:111
  50.5 1.8 %collective-permute-start.17 = (bf16[8,128,128]{2,1,0:T(8,128)(2,1)S(1)}, bf16[8,128,128]{2,1,0:T(8,128)(2,1)S(1)}, u32[]{:S(2)}, u32[]{:S(2)}) collective-permute-start(bf16[8,128,128]{2,1,0:T(8,128)(2,1)S(1)} %get-tuple-element.81.refs_6_), channel_id=1, source_target_pairs={{0,32},{16,48},{32,0},{48,16},{1,33},{17,49},{33,1},{49,17},{2,34}... | collective-permute-start | bytes 786440 | tf_op jit(solution)/shard_map/ppermute | solution.py:44
  52.4 7.8 %collective-permute-start.15 = (bf16[2,48,512]{2,1,0:T(8,128)(2,1)S(1)}, bf16[2,48,512]{2,1,0:T(8,128)(2,1)S(1)}, u32[]{:S(2)}, u32[]{:S(2)}) collective-permute-start(bf16[2,48,512]{2,1,0:T(8,128)(2,1)S(1)} %get-tuple-element.78), channel_id=1, source_target_pairs={{0,32},{1,0},{2,96},{3,64},{4,160},{5,128},{6,224},{7,192},{8,40},... | collective-permute-start | bytes 294920 | tf_op jit(solution)/shard_map/ppermute | solution.py:705
  60.1 1.9 %collective-permute-start.13 = (bf16[2,48,512]{2,1,0:T(8,128)(2,1)S(1)}, bf16[2,48,512]{2,1,0:T(8,128)(2,1)S(1)}, u32[]{:S(2)}, u32[]{:S(2)}) collective-permute-start(bf16[2,48,512]{2,1,0:T(8,128)(2,1)S(1)} %get-tuple-element.78), channel_id=1, source_target_pairs={{0,0},{1,32},{2,64},{3,96},{4,128},{5,160},{6,192},{7,224},{8,8},{... | collective-permute-start | bytes 294920 | tf_op jit(solution)/shard_map/ppermute | solution.py:705
  62.1 10.5 %collective-permute-start.16 = (bf16[2,48,512]{2,1,0:T(8,128)(2,1)S(1)}, bf16[2,48,512]{2,1,0:T(8,128)(2,1)S(1)}, u32[]{:S(2)}, u32[]{:S(2)}) collective-permute-start(bf16[2,48,512]{2,1,0:T(8,128)(2,1)S(1)} %collective-permute-done.15.refs_2_), channel_id=1, source_target_pairs={{0,16},{16,0},{32,48},{48,32},{1,17},{17,1},{33,49},{49,33},{2,18}... | collective-permute-start | bytes 294920 | tf_op jit(solution)/shard_map/ppermute | solution.py:44
  72.6 7.6 %collective-permute-start.14 = (bf16[2,48,512]{2,1,0:T(8,128)(2,1)S(1)}, bf16[2,48,512]{2,1,0:T(8,128)(2,1)S(1)}, u32[]{:S(2)}, u32[]{:S(2)}) collective-permute-start(bf16[2,48,512]{2,1,0:T(8,128)(2,1)S(1)} %collective-permute-done.13.refs_0_), channel_id=1, source_target_pairs={{0,16},{16,0},{32,48},{48,32},{1,17},{17,1},{33,49},{49,33},{2,18}... | collective-permute-start | bytes 294920 | tf_op jit(solution)/shard_map/ppermute | solution.py:44
  80.3 1.3 %others_update.1 = (f32[128,128]{1,0:T(8,128)}, f32[128,128]{1,0:T(8,128)}, f32[128,128]{1,0:T(8,128)}, f32[2,128]{1,0:T(2,128)}, f32[2,128]{1,0:T(2,128)}, /*index=5*/f32[2,128]{1,0:T(2,128)}, f32[8,128]{1,0:T(8,128)S(1)}) custom-call(s32[2]{0:T(128)S(1)} %pad_add_fusion.3.place, s32[2]{0:T(128)S(1)} %copy-done.9, s32[16]{0:T(128)S(1)} %copy-done.13, ...), custom_call_target="tpu_custom_call" | custom-call | bytes 4194304 | tf_op jit(solution)/shard_map/others_update/pallas_call | solution.py:111
  81.6 1.2 %collective-permute-done.14.refs_1_ = bf16[2,48,512]{2,1,0:T(8,128)(2,1)S(1)} collective-permute-done((bf16[2,48,512]{2,1,0:T(8,128)(2,1)S(1)}, bf16[2,48,512]{2,1,0:T(8,128)(2,1)S(1)}, u32[]{:S(2)}, u32[]{:S(2)}) %collective-permute-start.14) | collective-permute-done | bytes 98336 | tf_op jit(solution)/shard_map/ppermute | solution.py:44
  83.1 2.7 %collective-permute-start.22 = (bf16[96,1024]{1,0:T(8,128)(2,1)S(1)}, bf16[96,1024]{1,0:T(8,128)(2,1)S(1)}, u32[]{:S(2)}, u32[]{:S(2)}) collective-permute-start(bf16[96,1024]{1,0:T(8,128)(2,1)S(1)} %get-tuple-element.83.refs_2_), channel_id=1, source_target_pairs={{0,64},{64,128},{128,192},{192,0},{1,65},{65,129},{129,193},{193,1... | collective-permute-start | bytes 589832 | tf_op jit(solution)/shard_map/ppermute | solution.py:40
  85.8 1.7 %collective-permute-start.19 = (bf16[96,1024]{1,0:T(8,128)(2,1)S(1)}, bf16[96,1024]{1,0:T(8,128)(2,1)S(1)}, u32[]{:S(2)}, u32[]{:S(2)}) collective-permute-start(bf16[96,1024]{1,0:T(8,128)(2,1)S(1)} %get-tuple-element.83.refs_2_), channel_id=1, source_target_pairs={{0,8},{8,0},{1,9},{9,1},{2,10},{10,2},{3,11},{11,3},{4,12},{12,4},... | collective-permute-start | bytes 589832 | tf_op jit(solution)/shard_map/ppermute | solution.py:48
  87.5 2.2 %collective-permute-done.26.refs_10_ = bf16[96,1024]{1,0:T(8,128)(2,1)} collective-permute-done((bf16[96,1024]{1,0:T(8,128)(2,1)S(1)}, bf16[96,1024]{1,0:T(8,128)(2,1)}, u32[]{:S(2)}, u32[]{:S(2)}) %collective-permute-start.26) | collective-permute-done | bytes 196640 | tf_op jit(solution)/shard_map/ppermute | solution.py:40
  90.4 2.9 %collective-permute-start.18 = (bf16[112,1024]{1,0:T(8,128)(2,1)S(1)}, bf16[112,1024]{1,0:T(8,128)(2,1)S(1)}, u32[]{:S(2)}, u32[]{:S(2)}) collective-permute-start(bf16[112,1024]{1,0:T(8,128)(2,1)S(1)} %get-tuple-element.82.refs_0_), channel_id=1, source_target_pairs={{0,8},{8,0},{1,9},{9,1},{2,10},{10,2},{3,11},{11,3},{4,12},{12,4},... | collective-permute-start | bytes 688136 | tf_op jit(solution)/shard_map/ppermute | solution.py:48
  94.6 1.9 %collective-permute-start.23 = (bf16[96,1024]{1,0:T(8,128)(2,1)S(1)}, bf16[96,1024]{1,0:T(8,128)(2,1)S(1)}, u32[]{:S(2)}, u32[]{:S(2)}) collective-permute-start(bf16[96,1024]{1,0:T(8,128)(2,1)S(1)} %collective-permute-done.22.refs_6_), channel_id=1, source_target_pairs={{0,8},{8,0},{1,9},{9,1},{2,10},{10,2},{3,11},{11,3},{4,12},{12,4},... | collective-permute-start | bytes 589832 | tf_op jit(solution)/shard_map/ppermute | solution.py:48
  96.5 2.7 %collective-permute-start.25 = (bf16[112,1024]{1,0:T(8,128)(2,1)S(1)}, bf16[112,1024]{1,0:T(8,128)(2,1)S(1)}, u32[]{:S(2)}, u32[]{:S(2)}) collective-permute-start(bf16[112,1024]{1,0:T(8,128)(2,1)S(1)} %collective-permute-done.24.refs_8_), channel_id=1, source_target_pairs={{0,8},{8,0},{1,9},{9,1},{2,10},{10,2},{3,11},{11,3},{4,12},{12,4},... | collective-permute-start | bytes 688136 | tf_op jit(solution)/shard_map/ppermute | solution.py:48
  102.7 4.0 %early.1 = (bf16[2,2,2,48,4096]{4,3,2,1,0:T(8,128)(2,1)}, bf16[128,4096]{1,0:T(8,128)(2,1)}, f32[8,4096]{1,0:T(8,128)S(1)}, f32[64,128]{1,0:T(8,128)S(1)}) custom-call(s32[6]{0:T(128)S(1)} %stack.88.place, bf16[112,1024]{1,0:T(8,128)(2,1)} %copy-done.4, bf16[112,1024]{1,0:T(8,128)(2,1)} %copy-done.17, bf16[96,1024]{1,0:T(8,128)(2,1)} %copy-done.6, ...), custom_call_target="tpu_custom_call" | custom-call | bytes 1048576 | tf_op jit(solution)/shard_map/early/pallas_call | solution.py:111
  106.7 2.0 %collective-permute-done.30.lower = bf16[96,1024]{1,0:T(8,128)(2,1)S(1)} collective-permute-done((bf16[96,1024]{1,0:T(8,128)(2,1)}, bf16[96,1024]{1,0:T(8,128)(2,1)S(1)}, u32[]{:S(2)}, u32[]{:S(2)}) %collective-permute-start.30) | collective-permute-done | bytes 196640 | tf_op jit(solution)/shard_map/ppermute | solution.py:40
  108.8 1.4 %collective-permute-start.31 = (bf16[208,1024]{1,0:T(8,128)(2,1)S(1)}, bf16[208,1024]{1,0:T(8,128)(2,1)S(1)}, u32[]{:S(2)}, u32[]{:S(2)}) collective-permute-start(bf16[208,1024]{1,0:T(8,128)(2,1)S(1)} %relay.1.own), channel_id=1, source_target_pairs={{0,8},{8,0},{1,9},{9,1},{2,10},{10,2},{3,11},{11,3},{4,12},{12,4},... | collective-permute-start | bytes 1277960 | tf_op jit(solution)/shard_map/ppermute | solution.py:48
  110.2 1.3 %collective-permute-done.31.other = bf16[208,1024]{1,0:T(8,128)(2,1)S(1)} collective-permute-done((bf16[208,1024]{1,0:T(8,128)(2,1)S(1)}, bf16[208,1024]{1,0:T(8,128)(2,1)S(1)}, u32[]{:S(2)}, u32[]{:S(2)}) %collective-permute-start.31) | collective-permute-done | bytes 426016 | tf_op jit(solution)/shard_map/ppermute | solution.py:48
  111.6 3.9 %late.1 = (bf16[2,2,2,48,4096]{4,3,2,1,0:T(8,128)(2,1)}, bf16[128,4096]{1,0:T(8,128)(2,1)}, bf16[64,128]{1,0:T(8,128)(2,1)}) custom-call(s32[3]{0:T(128)S(1)} %pad_add_fusion.4.place, s32[2]{0:T(128)S(1)} %copy-done.9, bf16[2,2,2,48,4096]{4,3,2,1,0:T(8,128)(2,1)} %get-tuple-element.85.whole, ...), custom_call_target="tpu_custom_call", output_to_operand_aliasing={{0}: (2, {}), {1}: (3, {})} | custom-call | tf_op jit(solution)/shard_map/late/pallas_call | solution.py:111
  (101 shorter events, 11.3 us)
Async XLA Ops:
  9.7 11.5 %collective-permute-start = (bf16[3,384,512]{2,1,0:T(8,128)(2,1)S(1)}, bf16[3,384,512]{2,1,0:T(8,128)(2,1)S(1)}, u32[]{:S(2)}, u32[]{:S(2)}) collective-permute-start(bf16[3,384,512]{2,1,0:T(8,128)(2,1)S(1)} %get-tuple-element.53), channel_id=1, source_target_pairs={{0,8},{8,0},{1,9},{9,1},{2,10},{10,2},{3,11},{11,3},{4,12},{12,4},... | collective-permute-start | bytes 3538952 | tf_op jit(solution)/shard_map/ppermute | solution.py:48
  10.5 3.2 %collective-permute-start.2 = (bf16[1,384,512]{2,1,0:T(8,128)(2,1)S(1)}, bf16[1,384,512]{2,1,0:T(8,128)(2,1)S(1)}, u32[]{:S(2)}, u32[]{:S(2)}) collective-permute-start(bf16[1,384,512]{2,1,0:T(8,128)(2,1)S(1)} %get-tuple-element.54), channel_id=1, source_target_pairs={{0,8},{8,0},{1,9},{9,1},{2,10},{10,2},{3,11},{11,3},{4,12},{12,4},... | collective-permute-start | bytes 1179656 | tf_op jit(solution)/shard_map/ppermute | solution.py:48
  10.7 2.9 %collective-permute-start.1 = (bf16[4,16,512]{2,1,0:T(8,128)(2,1)S(1)}, bf16[4,16,512]{2,1,0:T(8,128)(2,1)S(1)}, u32[]{:S(2)}, u32[]{:S(2)}) collective-permute-start(bf16[4,16,512]{2,1,0:T(8,128)(2,1)S(1)} %extras.1), channel_id=1, source_target_pairs={{0,8},{8,0},{1,9},{9,1},{2,10},{10,2},{3,11},{11,3},{4,12},{12,4},... | collective-permute-start | bytes 196616 | tf_op jit(solution)/shard_map/ppermute | solution.py:48
  13.8 7.5 %collective-permute-start.4 = (bf16[192,512]{1,0:T(8,128)(2,1)S(1)}, bf16[192,512]{1,0:T(8,128)(2,1)S(1)}, u32[]{:S(2)}, u32[]{:S(2)}) collective-permute-start(bf16[192,512]{1,0:T(8,128)(2,1)S(1)} %get-tuple-element.58), channel_id=1, source_target_pairs={{0,192},{64,0},{128,64},{192,128},{1,193},{65,1},{129,65},{193,129... | collective-permute-start | bytes 589832 | tf_op jit(solution)/shard_map/ppermute | solution.py:40
  14.4 6.9 %collective-permute-start.3 = (bf16[208,512]{1,0:T(8,128)(2,1)S(1)}, bf16[208,512]{1,0:T(8,128)(2,1)S(1)}, u32[]{:S(2)}, u32[]{:S(2)}) collective-permute-start(bf16[208,512]{1,0:T(8,128)(2,1)S(1)} %get-tuple-element.57), channel_id=1, source_target_pairs={{0,64},{64,128},{128,192},{192,0},{1,65},{65,129},{129,193},{193,1... | collective-permute-start | bytes 638984 | tf_op jit(solution)/shard_map/ppermute | solution.py:40
  16.6 4.7 %collective-permute-start.5 = (bf16[128,128]{1,0:T(8,128)(2,1)S(1)}, bf16[128,128]{1,0:T(8,128)(2,1)S(1)}, u32[]{:S(2)}, u32[]{:S(2)}) collective-permute-start(bf16[128,128]{1,0:T(8,128)(2,1)S(1)} %subtract_convert_fusion.router), channel_id=1, source_target_pairs={{0,64},{64,0},{128,192},{192,128},{1,65},{65,1},{129,193},{193,129... | collective-permute-start | bytes 98312 | tf_op jit(solution)/shard_map/ppermute | solution.py:44
  22.9 13.2 %collective-permute-start.6 = (bf16[400,512]{1,0:T(8,128)(2,1)}, bf16[400,512]{1,0:T(8,128)(2,1)S(1)}, u32[]{:S(2)}, u32[]{:S(2)}) collective-permute-start(bf16[400,512]{1,0:T(8,128)(2,1)} %get-tuple-element.60), channel_id=1, source_target_pairs={{0,64},{64,128},{128,192},{192,0},{1,65},{65,129},{129,193},{193,1... | collective-permute-start | bytes 1228808 | tf_op jit(solution)/shard_map/ppermute | solution.py:40
  25.6 11.3 %collective-permute-start.7 = (bf16[400,512]{1,0:T(8,128)(2,1)}, bf16[400,512]{1,0:T(8,128)(2,1)S(1)}, u32[]{:S(2)}, u32[]{:S(2)}) collective-permute-start(bf16[400,512]{1,0:T(8,128)(2,1)} %get-tuple-element.61), channel_id=1, source_target_pairs={{0,192},{64,0},{128,64},{192,128},{1,193},{65,1},{129,65},{193,129... | collective-permute-start | bytes 1228808 | tf_op jit(solution)/shard_map/ppermute | solution.py:40
  26.2 9.9 %collective-permute-start.8 = (bf16[2,128,128]{2,1,0:T(8,128)(2,1)S(1)}, bf16[2,128,128]{2,1,0:T(8,128)(2,1)S(1)}, u32[]{:S(2)}, u32[]{:S(2)}) collective-permute-start(bf16[2,128,128]{2,1,0:T(8,128)(2,1)S(1)} %get-tuple-element.62.router), channel_id=1, source_target_pairs={{0,128},{64,192},{128,0},{192,64},{1,129},{65,193},{129,1},{193,65... | collective-permute-start | bytes 196616 | tf_op jit(solution)/shard_map/ppermute | solution.py:44
  38.3 9.4 %collective-permute-start.12 = (bf16[4,128,128]{2,1,0:T(8,128)(2,1)S(1)}, bf16[4,128,128]{2,1,0:T(8,128)(2,1)S(1)}, u32[]{:S(2)}, u32[]{:S(2)}) collective-permute-start(bf16[4,128,128]{2,1,0:T(8,128)(2,1)S(1)} %get-tuple-element.66.router), channel_id=1, source_target_pairs={{0,16},{16,0},{32,48},{48,32},{1,17},{17,1},{33,49},{49,33},{2,18}... | collective-permute-start | bytes 393224 | tf_op jit(solution)/shard_map/ppermute | solution.py:44
  39.9 5.1 %collective-permute-start.9 = (bf16[112,512]{1,0:T(8,128)(2,1)S(1)}, bf16[112,512]{1,0:T(8,128)(2,1)S(1)}, u32[]{:S(2)}, u32[]{:S(2)}) collective-permute-start(bf16[112,512]{1,0:T(8,128)(2,1)S(1)} %get-tuple-element.63), channel_id=1, source_target_pairs={{0,16},{16,32},{32,48},{48,0},{1,17},{17,33},{33,49},{49,1},{2,18}... | collective-permute-start | bytes 344072 | tf_op jit(solution)/shard_map/ppermute | solution.py:40
  40.0 5.0 %collective-permute-start.10 = (bf16[112,512]{1,0:T(8,128)(2,1)S(1)}, bf16[112,512]{1,0:T(8,128)(2,1)S(1)}, u32[]{:S(2)}, u32[]{:S(2)}) collective-permute-start(bf16[112,512]{1,0:T(8,128)(2,1)S(1)} %get-tuple-element.64), channel_id=1, source_target_pairs={{0,32},{16,48},{32,0},{48,16},{1,33},{17,49},{33,1},{49,17},{2,34}... | collective-permute-start | bytes 344072 | tf_op jit(solution)/shard_map/ppermute | solution.py:40
  40.0 7.8 %collective-permute-start.11 = (bf16[112,512]{1,0:T(8,128)(2,1)S(1)}, bf16[112,512]{1,0:T(8,128)(2,1)S(1)}, u32[]{:S(2)}, u32[]{:S(2)}) collective-permute-start(bf16[112,512]{1,0:T(8,128)(2,1)S(1)} %get-tuple-element.65), channel_id=1, source_target_pairs={{0,48},{16,0},{32,16},{48,32},{1,49},{17,1},{33,17},{49,33},{2,50}... | collective-permute-start | bytes 344072 | tf_op jit(solution)/shard_map/ppermute | solution.py:40
  50.5 32.3 %collective-permute-start.17 = (bf16[8,128,128]{2,1,0:T(8,128)(2,1)S(1)}, bf16[8,128,128]{2,1,0:T(8,128)(2,1)S(1)}, u32[]{:S(2)}, u32[]{:S(2)}) collective-permute-start(bf16[8,128,128]{2,1,0:T(8,128)(2,1)S(1)} %get-tuple-element.81.refs_6_), channel_id=1, source_target_pairs={{0,32},{16,48},{32,0},{48,16},{1,33},{17,49},{33,1},{49,17},{2,34}... | collective-permute-start | bytes 786440 | tf_op jit(solution)/shard_map/ppermute | solution.py:44
  52.4 9.7 %collective-permute-start.15 = (bf16[2,48,512]{2,1,0:T(8,128)(2,1)S(1)}, bf16[2,48,512]{2,1,0:T(8,128)(2,1)S(1)}, u32[]{:S(2)}, u32[]{:S(2)}) collective-permute-start(bf16[2,48,512]{2,1,0:T(8,128)(2,1)S(1)} %get-tuple-element.78), channel_id=1, source_target_pairs={{0,32},{1,0},{2,96},{3,64},{4,160},{5,128},{6,224},{7,192},{8,40},... | collective-permute-start | bytes 294920 | tf_op jit(solution)/shard_map/ppermute | solution.py:705
  60.1 12.4 %collective-permute-start.13 = (bf16[2,48,512]{2,1,0:T(8,128)(2,1)S(1)}, bf16[2,48,512]{2,1,0:T(8,128)(2,1)S(1)}, u32[]{:S(2)}, u32[]{:S(2)}) collective-permute-start(bf16[2,48,512]{2,1,0:T(8,128)(2,1)S(1)} %get-tuple-element.78), channel_id=1, source_target_pairs={{0,0},{1,32},{2,64},{3,96},{4,128},{5,160},{6,192},{7,224},{8,8},{... | collective-permute-start | bytes 294920 | tf_op jit(solution)/shard_map/ppermute | solution.py:705
  62.1 19.5 %collective-permute-start.16 = (bf16[2,48,512]{2,1,0:T(8,128)(2,1)S(1)}, bf16[2,48,512]{2,1,0:T(8,128)(2,1)S(1)}, u32[]{:S(2)}, u32[]{:S(2)}) collective-permute-start(bf16[2,48,512]{2,1,0:T(8,128)(2,1)S(1)} %collective-permute-done.15.refs_2_), channel_id=1, source_target_pairs={{0,16},{16,0},{32,48},{48,32},{1,17},{17,1},{33,49},{49,33},{2,18}... | collective-permute-start | bytes 294920 | tf_op jit(solution)/shard_map/ppermute | solution.py:44
  72.6 10.2 %collective-permute-start.14 = (bf16[2,48,512]{2,1,0:T(8,128)(2,1)S(1)}, bf16[2,48,512]{2,1,0:T(8,128)(2,1)S(1)}, u32[]{:S(2)}, u32[]{:S(2)}) collective-permute-start(bf16[2,48,512]{2,1,0:T(8,128)(2,1)S(1)} %collective-permute-done.13.refs_0_), channel_id=1, source_target_pairs={{0,16},{16,0},{32,48},{48,32},{1,17},{17,1},{33,49},{49,33},{2,18}... | collective-permute-start | bytes 294920 | tf_op jit(solution)/shard_map/ppermute | solution.py:44
  83.0 6.7 %collective-permute-start.26 = (bf16[96,1024]{1,0:T(8,128)(2,1)S(1)}, bf16[96,1024]{1,0:T(8,128)(2,1)}, u32[]{:S(2)}, u32[]{:S(2)}) collective-permute-start(bf16[96,1024]{1,0:T(8,128)(2,1)S(1)} %get-tuple-element.83.refs_2_), channel_id=1, source_target_pairs={{0,192},{64,0},{128,64},{192,128},{1,193},{65,1},{129,65},{193,129... | collective-permute-start | bytes 589832 | tf_op jit(solution)/shard_map/ppermute | solution.py:40
  83.1 7.3 %collective-permute-start.22 = (bf16[96,1024]{1,0:T(8,128)(2,1)S(1)}, bf16[96,1024]{1,0:T(8,128)(2,1)S(1)}, u32[]{:S(2)}, u32[]{:S(2)}) collective-permute-start(bf16[96,1024]{1,0:T(8,128)(2,1)S(1)} %get-tuple-element.83.refs_2_), channel_id=1, source_target_pairs={{0,64},{64,128},{128,192},{192,0},{1,65},{65,129},{129,193},{193,1... | collective-permute-start | bytes 589832 | tf_op jit(solution)/shard_map/ppermute | solution.py:40
  85.8 8.8 %collective-permute-start.24 = (bf16[112,1024]{1,0:T(8,128)(2,1)S(1)}, bf16[112,1024]{1,0:T(8,128)(2,1)S(1)}, u32[]{:S(2)}, u32[]{:S(2)}) collective-permute-start(bf16[112,1024]{1,0:T(8,128)(2,1)S(1)} %get-tuple-element.82.refs_0_), channel_id=1, source_target_pairs={{0,192},{64,0},{128,64},{192,128},{1,193},{65,1},{129,65},{193,129... | collective-permute-start | bytes 688136 | tf_op jit(solution)/shard_map/ppermute | solution.py:40
  85.8 7.6 %collective-permute-start.19 = (bf16[96,1024]{1,0:T(8,128)(2,1)S(1)}, bf16[96,1024]{1,0:T(8,128)(2,1)S(1)}, u32[]{:S(2)}, u32[]{:S(2)}) collective-permute-start(bf16[96,1024]{1,0:T(8,128)(2,1)S(1)} %get-tuple-element.83.refs_2_), channel_id=1, source_target_pairs={{0,8},{8,0},{1,9},{9,1},{2,10},{10,2},{3,11},{11,3},{4,12},{12,4},... | collective-permute-start | bytes 589832 | tf_op jit(solution)/shard_map/ppermute | solution.py:48
  87.5 14.5 %collective-permute-start.28 = (bf16[16,128,128]{2,1,0:T(8,128)(2,1)S(1)}, bf16[16,128,128]{2,1,0:T(8,128)(2,1)S(1)}, u32[]{:S(2)}, u32[]{:S(2)}) collective-permute-start(bf16[16,128,128]{2,1,0:T(8,128)(2,1)S(1)} %get-tuple-element.84.refs_12_), channel_id=1, source_target_pairs={{0,8},{8,0},{1,9},{9,1},{2,10},{10,2},{3,11},{11,3},{4,12},{12,4},... | collective-permute-start | bytes 1572872 | tf_op jit(solution)/shard_map/ppermute | solution.py:48
  89.7 6.9 %collective-permute-start.20 = (bf16[112,1024]{1,0:T(8,128)(2,1)S(1)}, bf16[112,1024]{1,0:T(8,128)(2,1)S(1)}, u32[]{:S(2)}, u32[]{:S(2)}) collective-permute-start(bf16[112,1024]{1,0:T(8,128)(2,1)S(1)} %get-tuple-element.82.refs_0_), channel_id=1, source_target_pairs={{0,64},{64,128},{128,192},{192,0},{1,65},{65,129},{129,193},{193,1... | collective-permute-start | bytes 688136 | tf_op jit(solution)/shard_map/ppermute | solution.py:40
  90.4 8.8 %collective-permute-start.18 = (bf16[112,1024]{1,0:T(8,128)(2,1)S(1)}, bf16[112,1024]{1,0:T(8,128)(2,1)S(1)}, u32[]{:S(2)}, u32[]{:S(2)}) collective-permute-start(bf16[112,1024]{1,0:T(8,128)(2,1)S(1)} %get-tuple-element.82.refs_0_), channel_id=1, source_target_pairs={{0,8},{8,0},{1,9},{9,1},{2,10},{10,2},{3,11},{11,3},{4,12},{12,4},... | collective-permute-start | bytes 688136 | tf_op jit(solution)/shard_map/ppermute | solution.py:48
  93.4 6.3 %collective-permute-start.27 = (bf16[96,1024]{1,0:T(8,128)(2,1)}, bf16[96,1024]{1,0:T(8,128)(2,1)S(1)}, u32[]{:S(2)}, u32[]{:S(2)}) collective-permute-start(bf16[96,1024]{1,0:T(8,128)(2,1)} %collective-permute-done.26.refs_10_), channel_id=1, source_target_pairs={{0,8},{8,0},{1,9},{9,1},{2,10},{10,2},{3,11},{11,3},{4,12},{12,4},... | collective-permute-start | bytes 589832 | tf_op jit(solution)/shard_map/ppermute | solution.py:48
  94.6 6.0 %collective-permute-start.23 = (bf16[96,1024]{1,0:T(8,128)(2,1)S(1)}, bf16[96,1024]{1,0:T(8,128)(2,1)S(1)}, u32[]{:S(2)}, u32[]{:S(2)}) collective-permute-start(bf16[96,1024]{1,0:T(8,128)(2,1)S(1)} %collective-permute-done.22.refs_6_), channel_id=1, source_target_pairs={{0,8},{8,0},{1,9},{9,1},{2,10},{10,2},{3,11},{11,3},{4,12},{12,4},... | collective-permute-start | bytes 589832 | tf_op jit(solution)/shard_map/ppermute | solution.py:48
  96.5 5.4 %collective-permute-start.25 = (bf16[112,1024]{1,0:T(8,128)(2,1)S(1)}, bf16[112,1024]{1,0:T(8,128)(2,1)S(1)}, u32[]{:S(2)}, u32[]{:S(2)}) collective-permute-start(bf16[112,1024]{1,0:T(8,128)(2,1)S(1)} %collective-permute-done.24.refs_8_), channel_id=1, source_target_pairs={{0,8},{8,0},{1,9},{9,1},{2,10},{10,2},{3,11},{11,3},{4,12},{12,4},... | collective-permute-start | bytes 688136 | tf_op jit(solution)/shard_map/ppermute | solution.py:48
  99.3 2.6 %collective-permute-start.21 = (bf16[112,1024]{1,0:T(8,128)(2,1)S(1)}, bf16[112,1024]{1,0:T(8,128)(2,1)S(1)}, u32[]{:S(2)}, u32[]{:S(2)}) collective-permute-start(bf16[112,1024]{1,0:T(8,128)(2,1)S(1)} %collective-permute-done.20.refs_4_), channel_id=1, source_target_pairs={{0,8},{8,0},{1,9},{9,1},{2,10},{10,2},{3,11},{11,3},{4,12},{12,4},... | collective-permute-start | bytes 688136 | tf_op jit(solution)/shard_map/ppermute | solution.py:48
  99.6 9.1 %collective-permute-start.29 = (bf16[112,1024]{1,0:T(8,128)(2,1)S(1)}, bf16[112,1024]{1,0:T(8,128)(2,1)S(1)}, u32[]{:S(2)}, u32[]{:S(2)}) collective-permute-start(bf16[112,1024]{1,0:T(8,128)(2,1)S(1)} %collective-permute-done.20.refs_4_), channel_id=1, source_target_pairs={{0,64},{64,128},{128,192},{192,0},{1,65},{65,129},{129,193},{193,1... | collective-permute-start | bytes 688136 | tf_op jit(solution)/shard_map/ppermute | solution.py:40
  101.3 7.4 %collective-permute-start.30 = (bf16[96,1024]{1,0:T(8,128)(2,1)}, bf16[96,1024]{1,0:T(8,128)(2,1)S(1)}, u32[]{:S(2)}, u32[]{:S(2)}) collective-permute-start(bf16[96,1024]{1,0:T(8,128)(2,1)} %collective-permute-done.26.refs_10_), channel_id=1, source_target_pairs={{0,192},{64,0},{128,64},{192,128},{1,193},{65,1},{129,65},{193,129... | collective-permute-start | bytes 589832 | tf_op jit(solution)/shard_map/ppermute | solution.py:40
  108.8 2.8 %collective-permute-start.31 = (bf16[208,1024]{1,0:T(8,128)(2,1)S(1)}, bf16[208,1024]{1,0:T(8,128)(2,1)S(1)}, u32[]{:S(2)}, u32[]{:S(2)}) collective-permute-start(bf16[208,1024]{1,0:T(8,128)(2,1)S(1)} %relay.1.own), channel_id=1, source_target_pairs={{0,8},{8,0},{1,9},{9,1},{2,10},{10,2},{3,11},{11,3},{4,12},{12,4},... | collective-permute-start | bytes 1277960 | tf_op jit(solution)/shard_map/ppermute | solution.py:48
  (24 other events, 244.7 us)

commit v4 on v3

v4 whole, which is shorter than its diff:
```python
import jax
import jax.numpy as jnp
from jax import lax
from jax.experimental import pallas as pl
from jax.experimental.pallas import tpu as pltpu
from jax.sharding import Mesh, PartitionSpec as P

beta_one = 0.9
beta_two = 0.95
learn_rate = 0.1
decay_rate = 0.1
eps = 1e-08
adam_step = 12

AXES = ("x", "zl", "core", "y", "zh")
SIZES = (4, 4, 2, 4, 2)
DP = AXES[:3]
GROUP = AXES[3:]
NX, NZ, NC, NY, NH = SIZES
EXTRA = 16

SCALARS = pl.BlockSpec(memory_space=pltpu.SMEM)
LOCAL = pl.BlockSpec(memory_space=pltpu.VMEM)
HELD = pl.BlockSpec(memory_space=pltpu.VMEM)
FAR = pl.BlockSpec(memory_space=pltpu.HBM)


def adamw(weight, moment, second, grad, factor, decay):
    moment_new = beta_one * moment + (1.0 - beta_one) * grad
    second_new = beta_two * second + (1.0 - beta_two) * grad * grad
    corrected = moment_new / (1.0 - beta_one**adam_step)
    scaled = second_new / (1.0 - beta_two**adam_step)
    weight_new = weight - learn_rate * factor * (
        corrected / (jnp.sqrt(scaled) + eps) + decay * weight
    )
    return (weight_new, moment_new, second_new)


def shift(value, axis, size, step):
    return lax.ppermute(value, axis, [(i, (i + step) % size) for i in range(size)])


def swap_with(value, axis, size, step):
    return lax.ppermute(value, axis, [(i, i ^ step) for i in range(size)])


def swap_core(value):
    return lax.ppermute(value, "core", [(0, 1), (1, 0)])


def flat(x, zl, core, y, zh):
    return (((x * NZ + zl) * NC + core) * NY + y) * NH + zh


def to_owner_group(step):
    pairs = []
    for x in range(NX):
        for zl in range(NZ):
            a, b = zl // 2, zl % 2
            for core in range(NC):
                for y in range(NY):
                    for zh in range(NH):
                        to = flat((x + y) % NX, (2 * zh + b) ^ step, core, x, a)
                        pairs.append((flat(x, zl, core, y, zh), to))
    return pairs


def after(value, *others):
    return lax.optimization_barrier((value,) + others)[0]


def to_float(value):
    return value.astype(jnp.float32)


def to_low(value):
    return value.astype(jnp.bfloat16)


def numbers(*values):
    return jnp.stack([jnp.asarray(v, jnp.int32) for v in values])


def kernel(body, outs, ins, scratch=(), aliases=None, name=None, cost=0, room=16):
    shapes = []
    for spec, shape, dtype in outs:
        if spec is HELD:
            shapes.append(pltpu.VMEM(shape, dtype))
        else:
            shapes.append(jax.ShapeDtypeStruct(shape, dtype))
    call = pl.pallas_call(
        body,
        out_shape=shapes,
        in_specs=ins,
        out_specs=[spec for spec, _, _ in outs],
        scratch_shapes=list(scratch),
        input_output_aliases=aliases or {},
        cost_estimate=pl.CostEstimate(flops=0, bytes_accessed=cost, transcendentals=0),
        compiler_params=pltpu.CompilerParams(vmem_limit_bytes=room * 2**20),
        name=name,
    )

    def run(*values):
        placed = []
        for spec, value in zip(ins, values):
            if spec is HELD:
                value = pltpu.with_memory_space_constraint(value, pltpu.VMEM)
            elif spec is FAR:
                value = pltpu.with_memory_space_constraint(value, pltpu.HBM)
            placed.append(value)
        return call(*placed)

    return run


def fetch(sources, targets, sems):
    copies = [
        pltpu.make_async_copy(a, b, sems.at[n]) for n, (a, b) in enumerate(zip(sources, targets))
    ]
    for copy in copies:
        copy.start()
    return copies


def product_kernel(place, hidden, grads_far, far_keep, far_send, keep, send, *scratch):
    raw, grads, left, right, sems = scratch
    tokens, experts, wide = hidden.shape
    wide = wide // NX
    rows = wide // (NZ * NC)
    blocks = sems.shape[0] - 1
    spans = [pl.ds(p * (tokens // blocks), tokens // blocks) for p in range(blocks)]
    copies = fetch(
        [grads_far] + [hidden.at[at] for at in spans], [grads] + [raw.at[at] for at in spans], sems
    )
    copies[0].wait()
    for at, copy in zip(spans, copies[1:]):
        right[:, at, :] = jnp.swapaxes(grads[at], 0, 1)
        copy.wait()
        left[:, at, :] = jnp.swapaxes(raw[at], 0, 1)
    for n in range(NX):
        at = pl.multiple_of(place[1 + n] * wide, 128)
        for e in range(experts):
            value = lax.dot_general(
                left[e, :, pl.ds(at, wide)],
                right[e],
                (((0,), (0,)), ((), ())),
                preferred_element_type=jnp.float32,
            )
            mine, other = (far_keep, far_send) if n == 0 else (keep, send)
            m = max(n - 1, 0)
            for zl in range(NZ):
                first = value[2 * zl * rows : (2 * zl + 1) * rows, :]
                second = value[(2 * zl + 1) * rows : (2 * zl + 2) * rows, :]
                to = (e * NZ + zl) * rows
                mine[m, to : to + rows, :] = to_low(jnp.where(place[0] == 0, first, second))
                other[m, to : to + rows, :] = to_low(jnp.where(place[0] == 0, second, first))


def product(place, hidden_act, out_grad):
    tokens, experts, hidden = hidden_act.shape
    feats = out_grad.shape[2]
    rows = experts * hidden // NX // NC
    one, rest = (1, rows, feats), (NX - 1, rows, feats)
    call = kernel(
        product_kernel,
        [(HELD, shape, jnp.bfloat16) for shape in (one, one, rest, rest)],
        [SCALARS, FAR, FAR],
        scratch=[
            pltpu.VMEM(hidden_act.shape, jnp.bfloat16),
            pltpu.VMEM(out_grad.shape, jnp.bfloat16),
            pltpu.VMEM((experts, tokens, hidden), jnp.bfloat16),
            pltpu.VMEM((experts, tokens, feats), jnp.bfloat16),
            pltpu.SemaphoreType.DMA((5,)),
        ],
        name="product",
        room=40,
    )
    return call(place, hidden_act, out_grad)


def parts_kernel(ids, w, m, v, sw, sm, sv, out, wide):
    tall, cols = w.shape
    wide[...] = jnp.zeros_like(wide)
    at = lax.broadcasted_iota(jnp.int32, (tall, cols), 0)
    for n, (router, small) in enumerate(((w, sw), (m, sm), (v, sv))):
        values = [
            jnp.sum(jnp.where(at == ids[e], router[...], 0.0), axis=0, keepdims=True)
            for e in range(2)
        ] + [small[i : i + 1, :] for i in range(2)]
        for part, value in enumerate(values):
            lanes = slice(part * cols, (part + 1) * cols)
            top = to_float(to_low(value))
            wide[8 + 2 * n : 9 + 2 * n, lanes] = top
            wide[9 + 2 * n : 10 + 2 * n, lanes] = value - top
    out[...] = to_low(wide[...])


def selected_parts(ids, *values):
    shape = (EXTRA, 512)
    call = kernel(
        parts_kernel,
        [(HELD, shape, jnp.bfloat16)],
        [SCALARS] + [LOCAL] * len(values),
        scratch=[pltpu.VMEM(shape, jnp.float32)],
        name="parts",
        cost=2 * 2**20,
    )
    return call(ids, *values)[0]


def extras_kernel(router, small, out, wide):
    cols, shard = 128, 256
    wide[...] = jnp.zeros_like(wide)
    for x in range(NX):
        for d in range(NZ * NC):
            at = x * NZ * NC + d
            for e in range(2):
                wide[x, d : d + 1, e * cols : (e + 1) * cols] = router[
                    e : e + 1, at * cols : (at + 1) * cols
                ]
            wide[x, d : d + 1, 2 * cols : 2 * cols + shard] = small[
                0:1, at * shard : (at + 1) * shard
            ]
    out[...] = to_low(wide[...])


def pack_extras(router_grads, small_grads):
    feats = 512
    call = kernel(
        extras_kernel,
        [(LOCAL, (NX, EXTRA, feats), jnp.bfloat16)],
        [LOCAL, LOCAL],
        scratch=[pltpu.VMEM((NX, EXTRA, feats), jnp.float32)],
        name="extras",
    )
    return call(router_grads, small_grads)[0]


def both_cores(own, theirs, start, rows):
    at = pl.ds(start, rows)
    return to_float(own[at, :]) + to_float(theirs[at, :])


def pair_kernel(place, own, theirs, extras, *refs):
    outs = refs[-own.shape[0] :]
    for n in range(min(own.shape[0], 2)):
        count = own.shape[1]
        outs[n][:count, :] = to_low(both_cores(own.at[n], theirs.at[n], 0, count))
        outs[n][count:, :] = extras[place[n]]
    if own.shape[0] > 1:
        router, hop = refs[:2]
        outs[2][0] = router[...]
        outs[2][1] = hop[...]


def pair(place, own, theirs, extras, *routers):
    chunks, rows, feats = own.shape
    out = (HELD, (rows + EXTRA, feats), jnp.bfloat16)
    joined = [(HELD, (2, *r.shape), jnp.bfloat16) for r in routers[:1]]
    call = kernel(
        pair_kernel,
        [out] * min(chunks, 2) + joined,
        [SCALARS] + [HELD] * (3 + len(routers)),
        name="pair",
    )
    return call(place, own, theirs, extras, *routers)


def total_kernel(
    place, own, theirs, extras, state, r1, r2, r3, router, hop, mine, s1, s2, s3, routers
):
    routers[:2] = router[...]
    routers[2:] = hop[...]
    _, count, feats = own.shape
    rows = count // (2 * NZ)
    more = to_float(extras[place[0]]) + to_float(state[...])
    for r in (r1, r2, r3):
        more = more + to_float(r[count:, :])
    for j, out in enumerate((mine, s1, s2, s3)):
        zl = lax.rem(place[1] + j, NZ)
        for e in range(2):
            at = pl.multiple_of((e * NZ + zl) * rows, 16)
            total = both_cores(own.at[2], theirs.at[2], at, rows)
            for r in (r1, r2, r3):
                total = total + to_float(r[pl.ds(at, rows), :])
            out[e * rows : (e + 1) * rows, :] = total.astype(out.dtype)
        out[2 * rows :, :] = more.astype(out.dtype)


def total_up(place, own, theirs, extras, state, arrived, router, hop):
    _, count, feats = own.shape
    rows = count // NZ + EXTRA
    call = kernel(
        total_kernel,
        [(HELD, (rows, feats), jnp.bfloat16)] * 4
        + [(HELD, (4, *router.shape[1:]), jnp.bfloat16)],
        [SCALARS] + [HELD] * 9,
        name="total",
    )
    return call(place, own, theirs, extras, state, *arrived, router, hop)


def rate_at(spot, lengths, rate):
    factor = jnp.zeros(spot.shape, jnp.float32)
    begin = jnp.int32(0)
    for k in range(lengths.shape[0]):
        end = begin + lengths[k]
        factor = jnp.where((spot >= begin) & (spot < end), rate[k], factor)
        begin = end
    return factor


def expert_kernel(
    place, lengths, rate, mine, r1, r2, r3, h0, h1, h2, h3, w_far, m_far, v_far, *refs
):
    low, extras, more, routers, w, m, v, sems = refs
    experts, rows, feats = w.shape
    copies = fetch((w_far, m_far, v_far), (w, m, v), sems)
    for k, hop in enumerate((h0, h1, h2, h3)):
        routers[NZ * k : NZ * (k + 1)] = hop[...]

    ix, iz, ic = place[0], place[1], place[2]
    blocks = [to_float(r[experts * rows :, :]) for r in (mine, r1, r2, r3)]
    sums = blocks[0] + blocks[1] + blocks[2] + blocks[3]
    more[...] = sums
    shape = blocks[0].shape
    row = lax.broadcasted_iota(jnp.int32, shape, 0)
    lane = lax.broadcasted_iota(jnp.int32, shape, 1)
    state = [jnp.zeros(shape, jnp.float32) for _ in range(4)]
    for j, block in enumerate(blocks):
        zl = lax.rem(iz - j + NZ, NZ)
        here = row == ix * NZ + zl
        for n in range(3):
            value = block[8 + 2 * n : 9 + 2 * n, :] + block[9 + 2 * n : 10 + 2 * n, :]
            state[n] = jnp.where(here, value, state[n])
        grad = jnp.sum(jnp.where(row == zl * NC + ic, sums, 0.0), axis=0, keepdims=True)
        state[3] = jnp.where(here, grad, state[3])
    half = feats // 2
    spot = (row * NC + ic) * half + lane - half
    factor = jnp.where(lane < half, 1.0, rate_at(spot, lengths, rate))
    decay = jnp.where(lane < half, decay_rate, 0.0)
    extras[...] = to_low(adamw(*state, factor, decay)[0])

    for copy in copies:
        copy.wait()
    for e in range(experts):
        at = slice(e * rows, (e + 1) * rows)
        grad = to_float(mine[at, :]) + to_float(r1[at, :]) + to_float(r2[at, :]) + to_float(r3[at, :])
        low[e] = to_low(adamw(w[e], m[e], v[e], grad, 1.0, decay_rate)[0])


def expert_update(place, lengths, rate, mine, arrived, w, m, v, routers):
    feats = w.shape[2]
    call = kernel(
        expert_kernel,
        [
            (HELD, w.shape, jnp.bfloat16),
            (HELD, (EXTRA, feats), jnp.bfloat16),
            (HELD, (EXTRA, feats), jnp.float32),
            (HELD, (NX * NZ, *routers[0].shape[1:]), jnp.bfloat16),
        ],
        [SCALARS] * 3 + [HELD] * 8 + [FAR] * 3,
        scratch=[pltpu.VMEM(w.shape, jnp.float32)] * 3 + [pltpu.SemaphoreType.DMA((3,))],
        name="expert_update",
    )
    return call(place, lengths, rate, mine, *arrived, *routers, w, m, v)


def others_kernel(place, ids, lengths, rate, more, r1, r2, r3, mine, *refs):
    (ew, em, ev, w, m, v, sw, sm, sv), refs = refs[:9], refs[9:]
    expert_outs, refs = refs[:3], refs[3:]
    new, moment, second, small_new, small_moment, small_second, token, held = refs
    experts, rows, feats = ew.shape
    for e in range(experts):
        at = slice(e * rows, (e + 1) * rows)
        grad = to_float(mine[at, :]) + to_float(r1[at, :]) + to_float(r2[at, :]) + to_float(r3[at, :])
        results = adamw(ew[e], em[e], ev[e], grad, 1.0, decay_rate)
        for out, value in zip(expert_outs, results):
            out[e] = value
    token[...] = jnp.zeros_like(token)
    tall, cols = w.shape
    shard_rows = sw.shape[0]
    rows = lax.broadcasted_iota(jnp.int32, more.shape, 0)
    grad_row = jnp.sum(jnp.where(rows == place[0], more[...], 0.0), axis=0, keepdims=True)
    at = lax.broadcasted_iota(jnp.int32, (tall, cols), 0)
    grad = jnp.zeros((tall, cols), jnp.float32)
    for e in range(ids.shape[0]):
        part = grad_row[:, e * cols : (e + 1) * cols]
        grad = grad + jnp.where(at == ids[e], part, 0.0)
    for i in range(shard_rows):
        part = (ids.shape[0] + i) * cols
        held[i : i + 1, :] = grad_row[:, part : part + cols]
    weight, first, squared = adamw(w[...], m[...], v[...], grad, 1.0, decay_rate)
    new[...] = weight
    moment[...] = first
    second[...] = squared
    spot = (
        place[1]
        + lax.broadcasted_iota(jnp.int32, (shard_rows, cols), 0) * cols
        + lax.broadcasted_iota(jnp.int32, (shard_rows, cols), 1)
    )
    factor = rate_at(spot, lengths, rate)
    weight, first, squared = adamw(
        sw[...], sm[...], sv[...], held[:shard_rows, :], factor, 0.0
    )
    small_new[...] = weight
    small_moment[...] = first
    small_second[...] = squared


def others_update(place, ids, lengths, rate, more, arrived, mine, expert, router, small):
    cols = router[0].shape[1]
    call = kernel(
        others_kernel,
        [(LOCAL, r.shape, jnp.float32) for r in (*expert, *router, *small)]
        + [(HELD, (8, cols), jnp.float32)],
        [SCALARS] * 4 + [HELD] * 4 + [LOCAL] * 10,
        scratch=[pltpu.VMEM((8, cols), jnp.float32)],
        name="others_update",
        cost=4 * 2**20,
    )
    return call(place, ids, lengths, rate, more, *arrived, mine, *expert, *router, *small)


def halve_kernel(place, *refs):
    pieces, (extras, token, out) = refs[:NZ], refs[NZ:]
    experts, rows, feats = pieces[0].shape
    for s in range(NZ):
        for q in range(NZ):

            @pl.when((place[0] ^ q) == s)
            def _():
                for e in range(experts):
                    to = (2 * e + s % 2) * rows
                    lanes = slice((s // 2) * feats, (s // 2 + 1) * feats)
                    out[to : to + rows, lanes] = pieces[q][e]

    out[2 * experts * rows :, :feats] = extras[...]
    out[2 * experts * rows :, feats:] = jnp.zeros((EXTRA, feats), jnp.bfloat16)


def halve(place, pieces, extras, token):
    experts, rows, feats = pieces[0].shape
    call = kernel(
        halve_kernel,
        [
            (HELD, (2 * experts * rows + EXTRA, NH * feats), jnp.bfloat16),
        ],
        [SCALARS] + [HELD] * (NZ + 2),
        name="halve",
    )
    return call(place, *pieces, extras, token)[0]


def lay(place, n, x, piece, out, sems):
    rows, wide = out.shape[3], piece.shape[1]
    at = pl.multiple_of(x * wide, wide)
    copies = []
    for e in range(2):
        for b in range(2):
            part = (2 * e + b) * rows
            copies.append(
                pltpu.make_async_copy(
                    piece.at[part : part + rows, :],
                    out.at[e, b, place[0] ^ n, :, pl.ds(at, wide)],
                    sems.at[len(copies)],
                )
            )
            copies[-1].start()
    return copies


def spread(core, row, d, lines, packed):
    cols = packed.shape[1]
    for e in range(2):
        at = pl.multiple_of(d * cols, cols)
        lines[e : e + 1, pl.ds(at, cols)] = row[:, e * cols : (e + 1) * cols]
    for i in range(2):
        packed[pl.ds(2 * d + i, 1), :] = row[:, (2 + i) * cols : (3 + i) * cols]


def finish_kernel(place, ids, *refs):
    count = 2 * NX
    pieces, routers, refs = refs[:count], refs[count : count + 2], refs[count + 2 :]
    out, patched_far, small, patched, lines, packed, out_sems, sem = refs
    cols = packed.shape[1]
    copies = []
    for n, piece in enumerate(pieces):
        copies += lay(place, n % 2, place[1 + n // 2], piece, out, out_sems.at[n])
    for n, blocks in enumerate(routers):
        for x in range(NX):
            for z in range(NZ):
                d = ((place[5] ^ x) * NZ + (place[6] ^ z)) * NC + (place[0] ^ n)
                at = pl.ds(pl.multiple_of(d * cols, cols), cols)
                patched[:, at] = blocks[x * NZ + z]
    for n in range(2):
        core = place[0] ^ n
        extras = sum(to_float(p[p.shape[0] - EXTRA :, : p.shape[1] // NH]) for p in pieces[n::2])
        for r in range(NX * NZ):
            spread(core, extras[r : r + 1, :], r * NC + core, lines, packed)
    spot = lax.broadcasted_iota(jnp.int32, (16, patched.shape[1]), 0)
    for n in range(2):
        at = pl.multiple_of(lax.div(ids[n], 16) * 16, 16)
        value = to_float(patched[pl.ds(at, 16), :])
        value = jnp.where(spot + at == ids[n], lines[n : n + 1, :], value)
        patched[pl.ds(at, 16), :] = to_low(value)
    move = pltpu.make_async_copy(patched, patched_far, sem)
    move.start()
    small[...] = to_low(packed[...])
    for copy in copies:
        copy.wait()
    move.wait()


def finish(place, ids, pieces, routers):
    rows, wide = pieces[0].shape
    n_dp = NX * NZ * NC
    tall, cols = routers[0].shape[1:]
    call = kernel(
        finish_kernel,
        [
            (FAR, (2, 2, NC, (rows - EXTRA) // 4, NY * wide), jnp.bfloat16),
            (FAR, (tall, n_dp * cols), jnp.bfloat16),
            (LOCAL, (2 * n_dp, cols), jnp.bfloat16),
        ],
        [SCALARS] * 2 + [HELD] * (len(pieces) + len(routers)),
        scratch=[
            pltpu.VMEM((tall, n_dp * cols), jnp.bfloat16),
            pltpu.VMEM((2, n_dp * cols), jnp.float32),
            pltpu.VMEM((2 * n_dp, cols), jnp.float32),
            pltpu.SemaphoreType.DMA((len(pieces), 4)),
            pltpu.SemaphoreType.DMA,
        ],
        name="finish",
    )
    return call(place, ids, *pieces, *routers)


def body(
    hidden_act,
    out_grad,
    router_grads,
    small_grads,
    expert_ids,
    small_lengths,
    small_rate,
    expert_w,
    expert_m,
    expert_v,
    router_w,
    router_m,
    router_v,
    small_w,
    small_m,
    small_v,
):
    ix, iy, iz, ic = (lax.axis_index(name) for name in ("x", "y", "zl", "core"))
    dp_index = (ix * NZ + iz) * NC + ic
    shard_len = small_w.shape[0]

    opposite, above, below = ((ix + k) % NX for k in (2, 1, 3))
    far_own, far_send, own, send = product(
        numbers(ic, opposite, above, below, ix), hidden_act, out_grad
    )

    zero = jnp.zeros_like(router_w)
    router = adamw(after(router_w, far_send), router_m, router_v, zero, 1.0, decay_rate)[0]
    router = to_low(router)

    extras = pack_extras(after(router_grads[0], far_send), small_grads)
    extras = to_low(to_float(extras) + to_float(swap_core(extras)))
    sent = list(pair(numbers(opposite), far_own, swap_core(far_send), extras))
    theirs = swap_core(send)
    hop = swap_with(router, "zl", NZ, 1)
    *near, router = pair(numbers(above, below), own, theirs, extras, router, hop)
    sent += near
    arrived = [shift(value, "x", NX, k) for k, value in zip((2, 1, 3), sent)]
    router_state = (router_w, router_m, router_v)
    small_state = [s.reshape(-1, 128) for s in (small_w, small_m, small_v)]
    parts = selected_parts(expert_ids, *router_state, *small_state)
    hop = swap_with(router, "zl", NZ, 2)
    mine, *sends, router = total_up(
        numbers(ix, iz), own, theirs, extras, parts, arrived, router, hop
    )
    routers = [router] + [swap_with(router, "x", NX, k) for k in (1, 2, 3)]
    arrived = [shift(send, "zl", NZ, j + 1) for j, send in enumerate(sends)]
    expert_state = (expert_w, expert_m, expert_v)
    low, extras, more, router = expert_update(
        numbers(ix, iz, ic), small_lengths, small_rate, mine, arrived, *expert_state, routers
    )
    others = others_update(
        numbers(iz * NC + ic, dp_index * shard_len),
        expert_ids,
        small_lengths,
        small_rate,
        more,
        arrived,
        mine,
        expert_state,
        router_state,
        small_state,
    )
    new_expert, expert_moment, expert_second = others[:3]
    new_router, router_moment, router_second = others[3:6]
    new_small, small_moment, small_second = (s.reshape(-1) for s in others[6:9])

    first, second = (lax.ppermute(low, AXES, to_owner_group(q)) for q in (0, 2))
    pieces = [first, swap_with(first, "zl", NZ, 1), second, swap_with(second, "zl", NZ, 1)]
    half = halve(numbers(iz), pieces, extras, others[9])
    pieces = []
    for k in (0, 1, 3, 2):
        piece = shift(half, "x", NX, k) if k else half
        pieces += [piece, swap_core(piece)]
    places = [(ix - iy - k) % NX for k in (0, 1, 3, 2)]
    whole, router_rollout, small_rollout = finish(
        numbers(ic, *places, ix, iz), expert_ids, pieces, [router, swap_core(router)]
    )
    expert_rollout = whole.reshape(whole.shape[0], -1, whole.shape[-1])
    small_rollout = small_rollout.reshape(-1)
    return (
        new_expert,
        expert_moment,
        expert_second,
        new_router,
        router_moment,
        router_second,
        new_small,
        small_moment,
        small_second,
        expert_rollout,
        router_rollout,
        small_rollout,
    )


def solution(mesh):
    fine = Mesh(mesh.devices.reshape(SIZES), AXES)
    placed = (
        P(DP, None, None),
        P(DP, None, GROUP),
        P(DP, None, None),
        P(DP, None),
        P(),
        P(),
        P(),
        P(None, DP, GROUP),
        P(None, DP, GROUP),
        P(None, DP, GROUP),
        P(None, DP),
        P(None, DP),
        P(None, DP),
        P(DP),
        P(DP),
        P(DP),
    )
    return jax.shard_map(
        body,
        mesh=fine,
        in_specs=placed,
        out_specs=(
            P(None, DP, GROUP),
            P(None, DP, GROUP),
            P(None, DP, GROUP),
            P(None, DP),
            P(None, DP),
            P(None, DP),
            P(DP),
            P(DP),
            P(DP),
            P(None, GROUP, None),
            P(),
            P(),
        ),
        check_vma=False,
    )
```

time: 116 us -> 106 us (0.914)
  the two profiles are of different devices: /device:TPU:79 before, /device:TPU:67 now
where the time goes in v4:
time: 106 us
  starting transfers between devices  49.4 us (47%)
  waiting for transfers between devices  34.5 us (33%)
  Pallas kernels  20.4 us (19%)
    ppermute x9, waiting for transfers between devices, shift(): lax.ppermute(value, axis, [(i, (i + step) % size) for i in range(size)])  25.9 us
    pallas_call x10, Pallas kernels, run(): return call(*placed)  20.4 us
    ppermute x8, starting transfers between devices, swap_core(): return lax.ppermute(value, 'core', [(0, 1), (1, 0)])  17.1 us
    ppermute x9, starting transfers between devices, shift(): lax.ppermute(value, axis, [(i, (i + step) % size) for i in range(size)])  13.7 us
    ppermute x7, starting transfers between devices, swap_with(): return lax.ppermute(value, axis, [(i, i ^ step) for i in range(size)])  10 us
    ppermute x2, starting transfers between devices, body(): first, second = (lax.ppermute(low, AXES, to_owner_group(q)) for q in (0, 2))  8.62 us
    ppermute x2, waiting for transfers between devices, body(): first, second = (lax.ppermute(low, AXES, to_owner_group(q)) for q in (0, 2))  6.02 us
    ppermute x8, waiting for transfers between devices, swap_core(): return lax.ppermute(value, 'core', [(0, 1), (1, 0)])  2.26 us
  transfers between devices with their start and end apart: 26, of which 11 were waited for; matrix products, arithmetic and copies ran while one was open for 0% of the time, Pallas kernels for 4%

profile of v4, /device:TPU:67, one launch (start us, length us, event | category | flops | bytes accessed | tf_op | source)
XLA Modules:
  0.0 105.9 jit_solution(1753548098503629364)
XLA Ops:
  0.8 8.0 %product.1 = (bf16[1,384,512]{2,1,0:T(8,128)(2,1)S(1)}, bf16[1,384,512]{2,1,0:T(8,128)(2,1)S(1)}, bf16[3,384,512]{2,1,0:T(8,128)(2,1)S(1)}, bf16[3,384,512]{2,1,0:T(8,128)(2,1)S(1)}) custom-call(s32[5]{0:T(128)S(1)} %stack.76.place, bf16[1024,2,1536]{2,1,0:T(2,128)(2,1)} %hidden.1, bf16[1024,2,512]{2,1,0:T(2,128)(2,1)} %grads_far.1), custom_call_target="tpu_custom_call" | custom-call | tf_op jit(solution)/shard_map/product/pallas_call | solution.py:111
  9.8 1.7 %collective-permute-start.4 = (bf16[128,128]{1,0:T(8,128)(2,1)S(1)}, bf16[128,128]{1,0:T(8,128)(2,1)S(1)}, u32[]{:S(2)}, u32[]{:S(2)}) collective-permute-start(bf16[128,128]{1,0:T(8,128)(2,1)S(1)} %subtract_convert_fusion.refs_0_), channel_id=1, source_target_pairs={{0,16},{16,0},{32,48},{48,32},{1,17},{17,1},{33,49},{49,33},{2,18}... | collective-permute-start | bytes 98312 | tf_op jit(solution)/shard_map/ppermute | solution.py:44
  12.4 0.8 collective-permute-done.1
  13.3 0.8 pair.2
  14.1 1.8 %collective-permute-start.3 = (bf16[400,512]{1,0:T(8,128)(2,1)}, bf16[400,512]{1,0:T(8,128)(2,1)}, u32[]{:S(2)}, u32[]{:S(2)}) collective-permute-start(bf16[400,512]{1,0:T(8,128)(2,1)} %pair.2), channel_id=1, source_target_pairs={{0,128},{64,192},{128,0},{192,64},{1,129},{65,193},{129,1},{193,65... | collective-permute-start | bytes 1228808 | tf_op jit(solution)/shard_map/ppermute | solution.py:40
  16.0 1.6 %pair.3 = (bf16[400,512]{1,0:T(8,128)(2,1)}, bf16[400,512]{1,0:T(8,128)(2,1)}, bf16[2,128,128]{2,1,0:T(8,128)(2,1)S(1)}) custom-call(s32[2]{0:T(128)S(1)} %pad_add_fusion.3.place, bf16[3,384,512]{2,1,0:T(8,128)(2,1)S(1)} %get-tuple-element.43.own, bf16[3,384,512]{2,1,0:T(8,128)(2,1)S(1)} %collective-permute-done.theirs, ...), custom_call_target="tpu_custom_call" | custom-call | tf_op jit(solution)/shard_map/pair/pallas_call | solution.py:111
  17.5 1.5 %collective-permute-start.6 = (bf16[400,512]{1,0:T(8,128)(2,1)}, bf16[400,512]{1,0:T(8,128)(2,1)}, u32[]{:S(2)}, u32[]{:S(2)}) collective-permute-start(bf16[400,512]{1,0:T(8,128)(2,1)} %get-tuple-element.50), channel_id=1, source_target_pairs={{0,192},{64,0},{128,64},{192,128},{1,193},{65,1},{129,65},{193,129... | collective-permute-start | bytes 1228808 | tf_op jit(solution)/shard_map/ppermute | solution.py:40
  19.8 6.9 %collective-permute-done.3.r1 = bf16[400,512]{1,0:T(8,128)(2,1)} collective-permute-done((bf16[400,512]{1,0:T(8,128)(2,1)}, bf16[400,512]{1,0:T(8,128)(2,1)}, u32[]{:S(2)}, u32[]{:S(2)}) %collective-permute-start.3) | collective-permute-done | bytes 409632 | tf_op jit(solution)/shard_map/ppermute | solution.py:40
  26.7 8.8 %collective-permute-done.5.r2 = bf16[400,512]{1,0:T(8,128)(2,1)} collective-permute-done((bf16[400,512]{1,0:T(8,128)(2,1)}, bf16[400,512]{1,0:T(8,128)(2,1)}, u32[]{:S(2)}, u32[]{:S(2)}) %collective-permute-start.5) | collective-permute-done | bytes 409632 | tf_op jit(solution)/shard_map/ppermute | solution.py:40
  36.1 1.5 %total.1 = (bf16[112,512]{1,0:T(8,128)(2,1)S(1)}, bf16[112,512]{1,0:T(8,128)(2,1)S(1)}, bf16[112,512]{1,0:T(8,128)(2,1)S(1)}, bf16[112,512]{1,0:T(8,128)(2,1)S(1)}, bf16[4,128,128]{2,1,0:T(8,128)(2,1)S(1)}) custom-call(s32[2]{0:T(128)S(1)} %pad_add_fusion.2.place, bf16[3,384,512]{2,1,0:T(8,128)(2,1)S(1)} %get-tuple-element.43.own, ...), custom_call_target="tpu_custom_call" | custom-call | tf_op jit(solution)/shard_map/total/pallas_call | solution.py:111
  37.6 1.2 %collective-permute-start.8 = (bf16[112,512]{1,0:T(8,128)(2,1)S(1)}, bf16[112,512]{1,0:T(8,128)(2,1)S(1)}, u32[]{:S(2)}, u32[]{:S(2)}) collective-permute-start(bf16[112,512]{1,0:T(8,128)(2,1)S(1)} %get-tuple-element.53), channel_id=1, source_target_pairs={{0,16},{16,32},{32,48},{48,0},{1,17},{17,33},{33,49},{49,1},{2,18}... | collective-permute-start | bytes 344072 | tf_op jit(solution)/shard_map/ppermute | solution.py:40
  38.8 1.2 %collective-permute-start.13 = (bf16[4,128,128]{2,1,0:T(8,128)(2,1)S(1)}, bf16[4,128,128]{2,1,0:T(8,128)(2,1)S(1)}, u32[]{:S(2)}, u32[]{:S(2)}) collective-permute-start(bf16[4,128,128]{2,1,0:T(8,128)(2,1)S(1)} %get-tuple-element.56.h0), channel_id=1, source_target_pairs={{0,192},{64,128},{128,64},{192,0},{1,193},{65,129},{129,65},{193,1... | collective-permute-start | bytes 393224 | tf_op jit(solution)/shard_map/ppermute | solution.py:44
  40.8 1.2 %collective-permute-start.11 = (bf16[4,128,128]{2,1,0:T(8,128)(2,1)S(1)}, bf16[4,128,128]{2,1,0:T(8,128)(2,1)S(1)}, u32[]{:S(2)}, u32[]{:S(2)}) collective-permute-start(bf16[4,128,128]{2,1,0:T(8,128)(2,1)S(1)} %get-tuple-element.56.h0), channel_id=1, source_target_pairs={{0,64},{64,0},{128,192},{192,128},{1,65},{65,1},{129,193},{193,129... | collective-permute-start | bytes 393224 | tf_op jit(solution)/shard_map/ppermute | solution.py:44
  42.1 1.5 %collective-permute-start.10 = (bf16[112,512]{1,0:T(8,128)(2,1)S(1)}, bf16[112,512]{1,0:T(8,128)(2,1)S(1)}, u32[]{:S(2)}, u32[]{:S(2)}) collective-permute-start(bf16[112,512]{1,0:T(8,128)(2,1)S(1)} %get-tuple-element.55), channel_id=1, source_target_pairs={{0,48},{16,0},{32,16},{48,32},{1,49},{17,1},{33,17},{49,33},{2,50}... | collective-permute-start | bytes 344072 | tf_op jit(solution)/shard_map/ppermute | solution.py:40
  43.6 3.3 %collective-permute-done.9.r2 = bf16[112,512]{1,0:T(8,128)(2,1)S(1)} collective-permute-done((bf16[112,512]{1,0:T(8,128)(2,1)S(1)}, bf16[112,512]{1,0:T(8,128)(2,1)S(1)}, u32[]{:S(2)}, u32[]{:S(2)}) %collective-permute-start.9) | collective-permute-done | bytes 114720 | tf_op jit(solution)/shard_map/ppermute | solution.py:40
  46.9 1.8 %collective-permute-done.10.r3 = bf16[112,512]{1,0:T(8,128)(2,1)S(1)} collective-permute-done((bf16[112,512]{1,0:T(8,128)(2,1)S(1)}, bf16[112,512]{1,0:T(8,128)(2,1)S(1)}, u32[]{:S(2)}, u32[]{:S(2)}) %collective-permute-start.10) | collective-permute-done | bytes 114720 | tf_op jit(solution)/shard_map/ppermute | solution.py:40
  48.7 1.9 %expert_update.1 = (bf16[2,48,512]{2,1,0:T(8,128)(2,1)S(1)}, bf16[16,512]{1,0:T(8,128)(2,1)S(1)}, f32[16,512]{1,0:T(8,128)S(1)}, bf16[16,128,128]{2,1,0:T(8,128)(2,1)S(1)}) custom-call(s32[3]{0:T(128)S(1)} %pad_add_fusion.1.place, s32[16]{0:T(128)S(1)} %copy-done.12, f32[16]{0:T(128)S(1)} %copy-done.13, bf16[112,512]{1,0:T(8,128)(2,1)S(1)} %get-tuple-element.52.mine, ...), custom_call_target="tpu_custom_call" | custom-call | tf_op jit(solution)/shard_map/expert_update/pallas_call | solution.py:111
  50.7 6.7 %collective-permute-start.16 = (bf16[2,48,512]{2,1,0:T(8,128)(2,1)S(1)}, bf16[2,48,512]{2,1,0:T(8,128)(2,1)S(1)}, u32[]{:S(2)}, u32[]{:S(2)}) collective-permute-start(bf16[2,48,512]{2,1,0:T(8,128)(2,1)S(1)} %get-tuple-element.67), channel_id=1, source_target_pairs={{0,32},{1,0},{2,96},{3,64},{4,160},{5,128},{6,224},{7,192},{8,40},... | collective-permute-start | bytes 294920 | tf_op jit(solution)/shard_map/ppermute | solution.py:607
  57.4 1.9 %collective-permute-start.14 = (bf16[2,48,512]{2,1,0:T(8,128)(2,1)S(1)}, bf16[2,48,512]{2,1,0:T(8,128)(2,1)S(1)}, u32[]{:S(2)}, u32[]{:S(2)}) collective-permute-start(bf16[2,48,512]{2,1,0:T(8,128)(2,1)S(1)} %get-tuple-element.67), channel_id=1, source_target_pairs={{0,0},{1,32},{2,64},{3,96},{4,128},{5,160},{6,192},{7,224},{8,8},{... | collective-permute-start | bytes 294920 | tf_op jit(solution)/shard_map/ppermute | solution.py:607
  59.3 2.3 %collective-permute-done.16.refs_2_ = bf16[2,48,512]{2,1,0:T(8,128)(2,1)S(1)} collective-permute-done((bf16[2,48,512]{2,1,0:T(8,128)(2,1)S(1)}, bf16[2,48,512]{2,1,0:T(8,128)(2,1)S(1)}, u32[]{:S(2)}, u32[]{:S(2)}) %collective-permute-start.16) | collective-permute-done | bytes 98336 | tf_op jit(solution)/shard_map/ppermute | solution.py:607
  61.6 1.4 %collective-permute-start.17 = (bf16[2,48,512]{2,1,0:T(8,128)(2,1)S(1)}, bf16[2,48,512]{2,1,0:T(8,128)(2,1)S(1)}, u32[]{:S(2)}, u32[]{:S(2)}) collective-permute-start(bf16[2,48,512]{2,1,0:T(8,128)(2,1)S(1)} %collective-permute-done.16.refs_2_), channel_id=1, source_target_pairs={{0,16},{16,0},{32,48},{48,32},{1,17},{17,1},{33,49},{49,33},{2,18}... | collective-permute-start | bytes 294920 | tf_op jit(solution)/shard_map/ppermute | solution.py:44
  63.0 3.7 %collective-permute-done.14.refs_0_ = bf16[2,48,512]{2,1,0:T(8,128)(2,1)S(1)} collective-permute-done((bf16[2,48,512]{2,1,0:T(8,128)(2,1)S(1)}, bf16[2,48,512]{2,1,0:T(8,128)(2,1)S(1)}, u32[]{:S(2)}, u32[]{:S(2)}) %collective-permute-start.14) | collective-permute-done | bytes 98336 | tf_op jit(solution)/shard_map/ppermute | solution.py:607
  66.7 3.5 %collective-permute-start.15 = (bf16[2,48,512]{2,1,0:T(8,128)(2,1)S(1)}, bf16[2,48,512]{2,1,0:T(8,128)(2,1)S(1)}, u32[]{:S(2)}, u32[]{:S(2)}) collective-permute-start(bf16[2,48,512]{2,1,0:T(8,128)(2,1)S(1)} %collective-permute-done.14.refs_0_), channel_id=1, source_target_pairs={{0,16},{16,0},{32,48},{48,32},{1,17},{17,1},{33,49},{49,33},{2,18}... | collective-permute-start | bytes 294920 | tf_op jit(solution)/shard_map/ppermute | solution.py:44
  70.3 1.6 %others_update.1 = (f32[2,48,512]{2,1,0:T(8,128)}, f32[2,48,512]{2,1,0:T(8,128)}, f32[2,48,512]{2,1,0:T(8,128)}, f32[128,128]{1,0:T(8,128)}, f32[128,128]{1,0:T(...) custom-call(s32[2]{0:T(128)S(1)} %pad_add_fusion.place, ...), custom_call_target="tpu_custom_call" | custom-call | bytes 4194304 | tf_op jit(solution)/shard_map/others_update/pallas_call | solution.py:111
  72.4 5.8 %collective-permute-start.23 = (bf16[208,1024]{1,0:T(8,128)(2,1)S(1)}, bf16[208,1024]{1,0:T(8,128)(2,1)S(1)}, u32[]{:S(2)}, u32[]{:S(2)}) collective-permute-start(bf16[208,1024]{1,0:T(8,128)(2,1)S(1)} %halve.1.refs_0_), channel_id=1, source_target_pairs={{0,128},{64,192},{128,0},{192,64},{1,129},{65,193},{129,1},{193,65... | collective-permute-start | bytes 1277960 | tf_op jit(solution)/shard_map/ppermute | solution.py:40
  78.1 2.0 %collective-permute-start.21 = (bf16[208,1024]{1,0:T(8,128)(2,1)S(1)}, bf16[208,1024]{1,0:T(8,128)(2,1)S(1)}, u32[]{:S(2)}, u32[]{:S(2)}) collective-permute-start(bf16[208,1024]{1,0:T(8,128)(2,1)S(1)} %halve.1.refs_0_), channel_id=1, source_target_pairs={{0,192},{64,0},{128,64},{192,128},{1,193},{65,1},{129,65},{193,129... | collective-permute-start | bytes 1277960 | tf_op jit(solution)/shard_map/ppermute | solution.py:40
  80.1 4.8 %collective-permute-start.25 = (bf16[16,128,128]{2,1,0:T(8,128)(2,1)S(1)}, bf16[16,128,128]{2,1,0:T(8,128)(2,1)S(1)}, u32[]{:S(2)}, u32[]{:S(2)}) collective-permute-start(bf16[16,128,128]{2,1,0:T(8,128)(2,1)S(1)} %get-tuple-element.70.refs_8_), channel_id=1, source_target_pairs={{0,8},{8,0},{1,9},{9,1},{2,10},{10,2},{3,11},{11,3},{4,12},{12,4},... | collective-permute-start | bytes 1572872 | tf_op jit(solution)/shard_map/ppermute | solution.py:48
  84.9 7.9 %collective-permute-start.24 = (bf16[208,1024]{1,0:T(8,128)(2,1)S(1)}, bf16[208,1024]{1,0:T(8,128)(2,1)}, u32[]{:S(2)}, u32[]{:S(2)}) collective-permute-start(bf16[208,1024]{1,0:T(8,128)(2,1)S(1)} %collective-permute-done.23.refs_6_), channel_id=1, source_target_pairs={{0,8},{8,0},{1,9},{9,1},{2,10},{10,2},{3,11},{11,3},{4,12},{12,4},... | collective-permute-start | bytes 1277960 | tf_op jit(solution)/shard_map/ppermute | solution.py:48
  92.8 4.5 %collective-permute-done.21.refs_4_ = bf16[208,1024]{1,0:T(8,128)(2,1)S(1)} collective-permute-done((bf16[208,1024]{1,0:T(8,128)(2,1)S(1)}, bf16[208,1024]{1,0:T(8,128)(2,1)S(1)}, u32[]{:S(2)}, u32[]{:S(2)}) %collective-permute-start.21) | collective-permute-done | bytes 426016 | tf_op jit(solution)/shard_map/ppermute | solution.py:40
  98.0 2.0 %collective-permute-start.20 = (bf16[208,1024]{1,0:T(8,128)(2,1)S(1)}, bf16[208,1024]{1,0:T(8,128)(2,1)}, u32[]{:S(2)}, u32[]{:S(2)}) collective-permute-start(bf16[208,1024]{1,0:T(8,128)(2,1)S(1)} %collective-permute-done.19.refs_2_), channel_id=1, source_target_pairs={{0,8},{8,0},{1,9},{9,1},{2,10},{10,2},{3,11},{11,3},{4,12},{12,4},... | collective-permute-start | bytes 1277960 | tf_op jit(solution)/shard_map/ppermute | solution.py:48
  100.1 1.4 %collective-permute-done.20.refs_3_ = bf16[208,1024]{1,0:T(8,128)(2,1)} collective-permute-done((bf16[208,1024]{1,0:T(8,128)(2,1)S(1)}, bf16[208,1024]{1,0:T(8,128)(2,1)}, u32[]{:S(2)}, u32[]{:S(2)}) %collective-permute-start.20) | collective-permute-done | bytes 426016 | tf_op jit(solution)/shard_map/ppermute | solution.py:48
  101.6 4.2 %finish.1 = (bf16[2,2,2,48,4096]{4,3,2,1,0:T(8,128)(2,1)}, bf16[128,4096]{1,0:T(8,128)(2,1)}, bf16[64,128]{1,0:T(8,128)(2,1)}) custom-call(s32[7]{0:T(128)S(1)} %stack.82.place, s32[2]{0:T(128)S(1)} %copy-done.8, bf16[208,1024]{1,0:T(8,128)(2,1)S(1)} %halve.1.refs_0_, bf16[208,1024]{1,0:T(8,128)(2,1)S(1)} %collective-permute-done.18.refs_1_, ...), custom_call_target="tpu_custom_call" | custom-call | tf_op jit(solution)/shard_map/finish/pallas_call | solution.py:111
  (66 shorter events, 5.6 us)
Async XLA Ops:
  0.8 10.7 %copy-start.6 = (f32[1,2,4096]{2,1,0:T(2,128)S(1)}, f32[1,2,4096]{2,1,0:T(2,128)}, u32[]{:S(2)}) copy-start(f32[1,2,4096]{2,1,0:T(2,128)} %param.18) | copy-start | bytes 98308
  8.8 7.2 %collective-permute-start = (bf16[3,384,512]{2,1,0:T(8,128)(2,1)S(1)}, bf16[3,384,512]{2,1,0:T(8,128)(2,1)S(1)}, u32[]{:S(2)}, u32[]{:S(2)}) collective-permute-start(bf16[3,384,512]{2,1,0:T(8,128)(2,1)S(1)} %get-tuple-element.44), channel_id=1, source_target_pairs={{0,8},{8,0},{1,9},{9,1},{2,10},{10,2},{3,11},{11,3},{4,12},{12,4},... | collective-permute-start | bytes 3538952 | tf_op jit(solution)/shard_map/ppermute | solution.py:48
  9.6 3.7 %collective-permute-start.2 = (bf16[1,384,512]{2,1,0:T(8,128)(2,1)S(1)}, bf16[1,384,512]{2,1,0:T(8,128)(2,1)S(1)}, u32[]{:S(2)}, u32[]{:S(2)}) collective-permute-start(bf16[1,384,512]{2,1,0:T(8,128)(2,1)S(1)} %get-tuple-element.45), channel_id=1, source_target_pairs={{0,8},{8,0},{1,9},{9,1},{2,10},{10,2},{3,11},{11,3},{4,12},{12,4},... | collective-permute-start | bytes 1179656 | tf_op jit(solution)/shard_map/ppermute | solution.py:48
  9.8 6.2 %collective-permute-start.4 = (bf16[128,128]{1,0:T(8,128)(2,1)S(1)}, bf16[128,128]{1,0:T(8,128)(2,1)S(1)}, u32[]{:S(2)}, u32[]{:S(2)}) collective-permute-start(bf16[128,128]{1,0:T(8,128)(2,1)S(1)} %subtract_convert_fusion.refs_0_), channel_id=1, source_target_pairs={{0,16},{16,0},{32,48},{48,32},{1,17},{17,1},{33,49},{49,33},{2,18}... | collective-permute-start | bytes 98312 | tf_op jit(solution)/shard_map/ppermute | solution.py:44
  11.5 1.7 %collective-permute-start.1 = (bf16[4,16,512]{2,1,0:T(8,128)(2,1)S(1)}, bf16[4,16,512]{2,1,0:T(8,128)(2,1)S(1)}, u32[]{:S(2)}, u32[]{:S(2)}) collective-permute-start(bf16[4,16,512]{2,1,0:T(8,128)(2,1)S(1)} %extras.1), channel_id=1, source_target_pairs={{0,8},{8,0},{1,9},{9,1},{2,10},{10,2},{3,11},{11,3},{4,12},{12,4},... | collective-permute-start | bytes 196616 | tf_op jit(solution)/shard_map/ppermute | solution.py:48
  14.1 12.6 %collective-permute-start.3 = (bf16[400,512]{1,0:T(8,128)(2,1)}, bf16[400,512]{1,0:T(8,128)(2,1)}, u32[]{:S(2)}, u32[]{:S(2)}) collective-permute-start(bf16[400,512]{1,0:T(8,128)(2,1)} %pair.2), channel_id=1, source_target_pairs={{0,128},{64,192},{128,0},{192,64},{1,129},{65,193},{129,1},{193,65... | collective-permute-start | bytes 1228808 | tf_op jit(solution)/shard_map/ppermute | solution.py:40
  17.5 31.2 %copy-start.12 = (s32[16]{0:T(128)S(1)}, s32[16]{0:T(128)}, u32[]{:S(2)}) copy-start(s32[16]{0:T(128)} %lengths.3) | copy-start | bytes 196
  17.5 31.2 %copy-start.13 = (f32[16]{0:T(128)S(1)}, f32[16]{0:T(128)}, u32[]{:S(2)}) copy-start(f32[16]{0:T(128)} %rate.3) | copy-start | bytes 196
  17.5 17.9 %collective-permute-start.5 = (bf16[400,512]{1,0:T(8,128)(2,1)}, bf16[400,512]{1,0:T(8,128)(2,1)}, u32[]{:S(2)}, u32[]{:S(2)}) collective-permute-start(bf16[400,512]{1,0:T(8,128)(2,1)} %get-tuple-element.49), channel_id=1, source_target_pairs={{0,64},{64,128},{128,192},{192,0},{1,65},{65,129},{129,193},{193,1... | collective-permute-start | bytes 1228808 | tf_op jit(solution)/shard_map/ppermute | solution.py:40
  17.5 18.5 %collective-permute-start.6 = (bf16[400,512]{1,0:T(8,128)(2,1)}, bf16[400,512]{1,0:T(8,128)(2,1)}, u32[]{:S(2)}, u32[]{:S(2)}) collective-permute-start(bf16[400,512]{1,0:T(8,128)(2,1)} %get-tuple-element.50), channel_id=1, source_target_pairs={{0,192},{64,0},{128,64},{192,128},{1,193},{65,1},{129,65},{193,129... | collective-permute-start | bytes 1228808 | tf_op jit(solution)/shard_map/ppermute | solution.py:40
  19.6 7.0 %collective-permute-start.7 = (bf16[2,128,128]{2,1,0:T(8,128)(2,1)S(1)}, bf16[2,128,128]{2,1,0:T(8,128)(2,1)S(1)}, u32[]{:S(2)}, u32[]{:S(2)}) collective-permute-start(bf16[2,128,128]{2,1,0:T(8,128)(2,1)S(1)} %get-tuple-element.51.router), channel_id=1, source_target_pairs={{0,32},{16,48},{32,0},{48,16},{1,33},{17,49},{33,1},{49,17},{2,34}... | collective-permute-start | bytes 196616 | tf_op jit(solution)/shard_map/ppermute | solution.py:44
  19.8 50.5 %copy-start = (f32[2,48,512]{2,1,0:T(8,128)S(1)}, f32[2,48,512]{2,1,0:T(8,128)}, u32[]{:S(2)}) copy-start(f32[2,48,512]{2,1,0:T(8,128)} %refs_0_.1) | copy-start | bytes 589828
  19.8 50.5 %copy-start.1 = (f32[2,48,512]{2,1,0:T(8,128)S(1)}, f32[2,48,512]{2,1,0:T(8,128)}, u32[]{:S(2)}) copy-start(f32[2,48,512]{2,1,0:T(8,128)} %refs_1_.1) | copy-start | bytes 589828
  19.8 50.5 %copy-start.2 = (f32[2,48,512]{2,1,0:T(8,128)S(1)}, f32[2,48,512]{2,1,0:T(8,128)}, u32[]{:S(2)}) copy-start(f32[2,48,512]{2,1,0:T(8,128)} %refs_2_.1) | copy-start | bytes 589828
  37.6 4.4 %collective-permute-start.8 = (bf16[112,512]{1,0:T(8,128)(2,1)S(1)}, bf16[112,512]{1,0:T(8,128)(2,1)S(1)}, u32[]{:S(2)}, u32[]{:S(2)}) collective-permute-start(bf16[112,512]{1,0:T(8,128)(2,1)S(1)} %get-tuple-element.53), channel_id=1, source_target_pairs={{0,16},{16,32},{32,48},{48,0},{1,17},{17,33},{33,49},{49,1},{2,18}... | collective-permute-start | bytes 344072 | tf_op jit(solution)/shard_map/ppermute | solution.py:40
  38.8 9.9 %collective-permute-start.13 = (bf16[4,128,128]{2,1,0:T(8,128)(2,1)S(1)}, bf16[4,128,128]{2,1,0:T(8,128)(2,1)S(1)}, u32[]{:S(2)}, u32[]{:S(2)}) collective-permute-start(bf16[4,128,128]{2,1,0:T(8,128)(2,1)S(1)} %get-tuple-element.56.h0), channel_id=1, source_target_pairs={{0,192},{64,128},{128,64},{192,0},{1,193},{65,129},{129,65},{193,1... | collective-permute-start | bytes 393224 | tf_op jit(solution)/shard_map/ppermute | solution.py:44
  40.0 8.7 %collective-permute-start.12 = (bf16[4,128,128]{2,1,0:T(8,128)(2,1)S(1)}, bf16[4,128,128]{2,1,0:T(8,128)(2,1)S(1)}, u32[]{:S(2)}, u32[]{:S(2)}) collective-permute-start(bf16[4,128,128]{2,1,0:T(8,128)(2,1)S(1)} %get-tuple-element.56.h0), channel_id=1, source_target_pairs={{0,128},{64,192},{128,0},{192,64},{1,129},{65,193},{129,1},{193,65... | collective-permute-start | bytes 393224 | tf_op jit(solution)/shard_map/ppermute | solution.py:44
  40.8 7.9 %collective-permute-start.11 = (bf16[4,128,128]{2,1,0:T(8,128)(2,1)S(1)}, bf16[4,128,128]{2,1,0:T(8,128)(2,1)S(1)}, u32[]{:S(2)}, u32[]{:S(2)}) collective-permute-start(bf16[4,128,128]{2,1,0:T(8,128)(2,1)S(1)} %get-tuple-element.56.h0), channel_id=1, source_target_pairs={{0,64},{64,0},{128,192},{192,128},{1,65},{65,1},{129,193},{193,129... | collective-permute-start | bytes 393224 | tf_op jit(solution)/shard_map/ppermute | solution.py:44
  42.0 4.9 %collective-permute-start.9 = (bf16[112,512]{1,0:T(8,128)(2,1)S(1)}, bf16[112,512]{1,0:T(8,128)(2,1)S(1)}, u32[]{:S(2)}, u32[]{:S(2)}) collective-permute-start(bf16[112,512]{1,0:T(8,128)(2,1)S(1)} %get-tuple-element.54), channel_id=1, source_target_pairs={{0,32},{16,48},{32,0},{48,16},{1,33},{17,49},{33,1},{49,17},{2,34}... | collective-permute-start | bytes 344072 | tf_op jit(solution)/shard_map/ppermute | solution.py:40
  42.1 6.7 %collective-permute-start.10 = (bf16[112,512]{1,0:T(8,128)(2,1)S(1)}, bf16[112,512]{1,0:T(8,128)(2,1)S(1)}, u32[]{:S(2)}, u32[]{:S(2)}) collective-permute-start(bf16[112,512]{1,0:T(8,128)(2,1)S(1)} %get-tuple-element.55), channel_id=1, source_target_pairs={{0,48},{16,0},{32,16},{48,32},{1,49},{17,1},{33,17},{49,33},{2,50}... | collective-permute-start | bytes 344072 | tf_op jit(solution)/shard_map/ppermute | solution.py:40
  50.7 11.0 %collective-permute-start.16 = (bf16[2,48,512]{2,1,0:T(8,128)(2,1)S(1)}, bf16[2,48,512]{2,1,0:T(8,128)(2,1)S(1)}, u32[]{:S(2)}, u32[]{:S(2)}) collective-permute-start(bf16[2,48,512]{2,1,0:T(8,128)(2,1)S(1)} %get-tuple-element.67), channel_id=1, source_target_pairs={{0,32},{1,0},{2,96},{3,64},{4,160},{5,128},{6,224},{7,192},{8,40},... | collective-permute-start | bytes 294920 | tf_op jit(solution)/shard_map/ppermute | solution.py:607
  57.4 9.4 %collective-permute-start.14 = (bf16[2,48,512]{2,1,0:T(8,128)(2,1)S(1)}, bf16[2,48,512]{2,1,0:T(8,128)(2,1)S(1)}, u32[]{:S(2)}, u32[]{:S(2)}) collective-permute-start(bf16[2,48,512]{2,1,0:T(8,128)(2,1)S(1)} %get-tuple-element.67), channel_id=1, source_target_pairs={{0,0},{1,32},{2,64},{3,96},{4,128},{5,160},{6,192},{7,224},{8,8},{... | collective-permute-start | bytes 294920 | tf_op jit(solution)/shard_map/ppermute | solution.py:607
  61.6 10.3 %collective-permute-start.17 = (bf16[2,48,512]{2,1,0:T(8,128)(2,1)S(1)}, bf16[2,48,512]{2,1,0:T(8,128)(2,1)S(1)}, u32[]{:S(2)}, u32[]{:S(2)}) collective-permute-start(bf16[2,48,512]{2,1,0:T(8,128)(2,1)S(1)} %collective-permute-done.16.refs_2_), channel_id=1, source_target_pairs={{0,16},{16,0},{32,48},{48,32},{1,17},{17,1},{33,49},{49,33},{2,18}... | collective-permute-start | bytes 294920 | tf_op jit(solution)/shard_map/ppermute | solution.py:44
  66.7 5.5 %collective-permute-start.15 = (bf16[2,48,512]{2,1,0:T(8,128)(2,1)S(1)}, bf16[2,48,512]{2,1,0:T(8,128)(2,1)S(1)}, u32[]{:S(2)}, u32[]{:S(2)}) collective-permute-start(bf16[2,48,512]{2,1,0:T(8,128)(2,1)S(1)} %collective-permute-done.14.refs_0_), channel_id=1, source_target_pairs={{0,16},{16,0},{32,48},{48,32},{1,17},{17,1},{33,49},{49,33},{2,18}... | collective-permute-start | bytes 294920 | tf_op jit(solution)/shard_map/ppermute | solution.py:44
  72.4 12.6 %collective-permute-start.23 = (bf16[208,1024]{1,0:T(8,128)(2,1)S(1)}, bf16[208,1024]{1,0:T(8,128)(2,1)S(1)}, u32[]{:S(2)}, u32[]{:S(2)}) collective-permute-start(bf16[208,1024]{1,0:T(8,128)(2,1)S(1)} %halve.1.refs_0_), channel_id=1, source_target_pairs={{0,128},{64,192},{128,0},{192,64},{1,129},{65,193},{129,1},{193,65... | collective-permute-start | bytes 1277960 | tf_op jit(solution)/shard_map/ppermute | solution.py:40
  78.1 19.2 %collective-permute-start.21 = (bf16[208,1024]{1,0:T(8,128)(2,1)S(1)}, bf16[208,1024]{1,0:T(8,128)(2,1)S(1)}, u32[]{:S(2)}, u32[]{:S(2)}) collective-permute-start(bf16[208,1024]{1,0:T(8,128)(2,1)S(1)} %halve.1.refs_0_), channel_id=1, source_target_pairs={{0,192},{64,0},{128,64},{192,128},{1,193},{65,1},{129,65},{193,129... | collective-permute-start | bytes 1277960 | tf_op jit(solution)/shard_map/ppermute | solution.py:40
  80.1 17.9 %collective-permute-start.19 = (bf16[208,1024]{1,0:T(8,128)(2,1)S(1)}, bf16[208,1024]{1,0:T(8,128)(2,1)S(1)}, u32[]{:S(2)}, u32[]{:S(2)}) collective-permute-start(bf16[208,1024]{1,0:T(8,128)(2,1)S(1)} %halve.1.refs_0_), channel_id=1, source_target_pairs={{0,64},{64,128},{128,192},{192,0},{1,65},{65,129},{129,193},{193,1... | collective-permute-start | bytes 1277960 | tf_op jit(solution)/shard_map/ppermute | solution.py:40
  80.1 20.0 %collective-permute-start.25 = (bf16[16,128,128]{2,1,0:T(8,128)(2,1)S(1)}, bf16[16,128,128]{2,1,0:T(8,128)(2,1)S(1)}, u32[]{:S(2)}, u32[]{:S(2)}) collective-permute-start(bf16[16,128,128]{2,1,0:T(8,128)(2,1)S(1)} %get-tuple-element.70.refs_8_), channel_id=1, source_target_pairs={{0,8},{8,0},{1,9},{9,1},{2,10},{10,2},{3,11},{11,3},{4,12},{12,4},... | collective-permute-start | bytes 1572872 | tf_op jit(solution)/shard_map/ppermute | solution.py:48
  84.9 15.2 %collective-permute-start.18 = (bf16[208,1024]{1,0:T(8,128)(2,1)S(1)}, bf16[208,1024]{1,0:T(8,128)(2,1)S(1)}, u32[]{:S(2)}, u32[]{:S(2)}) collective-permute-start(bf16[208,1024]{1,0:T(8,128)(2,1)S(1)} %halve.1.refs_0_), channel_id=1, source_target_pairs={{0,8},{8,0},{1,9},{9,1},{2,10},{10,2},{3,11},{11,3},{4,12},{12,4},... | collective-permute-start | bytes 1277960 | tf_op jit(solution)/shard_map/ppermute | solution.py:48
  84.9 15.2 %collective-permute-start.24 = (bf16[208,1024]{1,0:T(8,128)(2,1)S(1)}, bf16[208,1024]{1,0:T(8,128)(2,1)}, u32[]{:S(2)}, u32[]{:S(2)}) collective-permute-start(bf16[208,1024]{1,0:T(8,128)(2,1)S(1)} %collective-permute-done.23.refs_6_), channel_id=1, source_target_pairs={{0,8},{8,0},{1,9},{9,1},{2,10},{10,2},{3,11},{11,3},{4,12},{12,4},... | collective-permute-start | bytes 1277960 | tf_op jit(solution)/shard_map/ppermute | solution.py:48
  97.3 2.8 %collective-permute-start.22 = (bf16[208,1024]{1,0:T(8,128)(2,1)S(1)}, bf16[208,1024]{1,0:T(8,128)(2,1)}, u32[]{:S(2)}, u32[]{:S(2)}) collective-permute-start(bf16[208,1024]{1,0:T(8,128)(2,1)S(1)} %collective-permute-done.21.refs_4_), channel_id=1, source_target_pairs={{0,8},{8,0},{1,9},{9,1},{2,10},{10,2},{3,11},{11,3},{4,12},{12,4},... | collective-permute-start | bytes 1277960 | tf_op jit(solution)/shard_map/ppermute | solution.py:48
  98.0 3.5 %collective-permute-start.20 = (bf16[208,1024]{1,0:T(8,128)(2,1)S(1)}, bf16[208,1024]{1,0:T(8,128)(2,1)}, u32[]{:S(2)}, u32[]{:S(2)}) collective-permute-start(bf16[208,1024]{1,0:T(8,128)(2,1)S(1)} %collective-permute-done.19.refs_2_), channel_id=1, source_target_pairs={{0,8},{8,0},{1,9},{9,1},{2,10},{10,2},{3,11},{11,3},{4,12},{12,4},... | collective-permute-start | bytes 1277960 | tf_op jit(solution)/shard_map/ppermute | solution.py:48
  (8 other events, 74.5 us)

commit v5 on v4

--- a/solution.py
+++ b/solution.py
@@ -558,7 +558,7 @@
     dp_index = (ix * NZ + iz) * NC + ic
     shard_len = small_w.shape[0]
 
-    opposite, above, below = ((ix + k) % NX for k in (2, 1, 3))
+    opposite, above, below = (ix ^ k for k in (2, 1, 3))
     far_own, far_send, own, send = product(
         numbers(ic, opposite, above, below, ix), hidden_act, out_grad
     )
@@ -574,7 +574,7 @@
     hop = swap_with(router, "zl", NZ, 1)
     *near, router = pair(numbers(above, below), own, theirs, extras, router, hop)
     sent += near
-    arrived = [shift(value, "x", NX, k) for k, value in zip((2, 1, 3), sent)]
+    arrived = [swap_with(value, "x", NX, k) for k, value in zip((2, 1, 3), sent)]
     router_state = (router_w, router_m, router_v)
     small_state = [s.reshape(-1, 128) for s in (small_w, small_m, small_v)]
     parts = selected_parts(expert_ids, *router_state, *small_state)

time: 106 us -> 106 us (level)
    ppermute x7 -> x10, waiting for transfers between devices: 0.32 us -> 16.6 us  [swap_with(): return lax.ppermute(value, axis, [(i, i ^ step) for i in range(size)])]
    ppermute x9 -> x6, waiting for transfers between devices: 25.9 us -> 9.75 us  [shift(): lax.ppermute(value, axis, [(i, (i + step) % size) for i in range(size)])]
    ppermute x9 -> x6, starting transfers between devices: 13.7 us -> 10.2 us  [shift(): lax.ppermute(value, axis, [(i, (i + step) % size) for i in range(size)])]
    ppermute x7 -> x10, starting transfers between devices: 10 us -> 13.4 us  [swap_with(): return lax.ppermute(value, axis, [(i, i ^ step) for i in range(size)])]
where the time goes in v5:
time: 106 us
  starting transfers between devices  49.3 us (47%)
  waiting for transfers between devices  34.5 us (33%)
  Pallas kernels  20.4 us (19%)
    pallas_call x10, Pallas kernels, run(): return call(*placed)  20.4 us
    ppermute x8, starting transfers between devices, swap_core(): return lax.ppermute(value, 'core', [(0, 1), (1, 0)])  17.1 us
    ppermute x10, waiting for transfers between devices, swap_with(): return lax.ppermute(value, axis, [(i, i ^ step) for i in range(size)])  16.6 us
    ppermute x10, starting transfers between devices, swap_with(): return lax.ppermute(value, axis, [(i, i ^ step) for i in range(size)])  13.4 us
    ppermute x6, starting transfers between devices, shift(): lax.ppermute(value, axis, [(i, (i + step) % size) for i in range(size)])  10.2 us
    ppermute x6, waiting for transfers between devices, shift(): lax.ppermute(value, axis, [(i, (i + step) % size) for i in range(size)])  9.75 us
    ppermute x2, starting transfers between devices, body(): first, second = (lax.ppermute(low, AXES, to_owner_group(q)) for q in (0, 2))  8.63 us
    ppermute x2, waiting for transfers between devices, body(): first, second = (lax.ppermute(low, AXES, to_owner_group(q)) for q in (0, 2))  5.9 us
  transfers between devices with their start and end apart: 26, of which 11 were waited for; matrix products, arithmetic and copies ran while one was open for 0% of the time, Pallas kernels for 4%

profile of v5, /device:TPU:67, one launch (start us, length us, event | category | flops | bytes accessed | tf_op | source)
XLA Modules:
  0.0 105.8 jit_solution(1821769440246654653)
XLA Ops:
  0.8 8.0 %product.1 = (bf16[1,384,512]{2,1,0:T(8,128)(2,1)S(1)}, bf16[1,384,512]{2,1,0:T(8,128)(2,1)S(1)}, bf16[3,384,512]{2,1,0:T(8,128)(2,1)S(1)}, bf16[3,384,512]{2,1,0:T(8,128)(2,1)S(1)}) custom-call(s32[5]{0:T(128)S(1)} %stack.76.place, bf16[1024,2,1536]{2,1,0:T(2,128)(2,1)} %hidden.1, bf16[1024,2,512]{2,1,0:T(2,128)(2,1)} %grads_far.1), custom_call_target="tpu_custom_call" | custom-call | tf_op jit(solution)/shard_map/product/pallas_call | solution.py:111
  9.7 1.7 %collective-permute-start.4 = (bf16[128,128]{1,0:T(8,128)(2,1)S(1)}, bf16[128,128]{1,0:T(8,128)(2,1)S(1)}, u32[]{:S(2)}, u32[]{:S(2)}) collective-permute-start(bf16[128,128]{1,0:T(8,128)(2,1)S(1)} %subtract_convert_fusion.refs_0_), channel_id=1, source_target_pairs={{0,16},{16,0},{32,48},{48,32},{1,17},{17,1},{33,49},{49,33},{2,18}... | collective-permute-start | bytes 98312 | tf_op jit(solution)/shard_map/ppermute | solution.py:44
  12.4 0.8 collective-permute-done.1
  13.2 0.8 pair.2
  14.1 1.8 %collective-permute-start.3 = (bf16[400,512]{1,0:T(8,128)(2,1)}, bf16[400,512]{1,0:T(8,128)(2,1)}, u32[]{:S(2)}, u32[]{:S(2)}) collective-permute-start(bf16[400,512]{1,0:T(8,128)(2,1)} %pair.2), channel_id=1, source_target_pairs={{0,128},{64,192},{128,0},{192,64},{1,129},{65,193},{129,1},{193,65... | collective-permute-start | bytes 1228808 | tf_op jit(solution)/shard_map/ppermute | solution.py:44
  15.9 1.6 %pair.3 = (bf16[400,512]{1,0:T(8,128)(2,1)}, bf16[400,512]{1,0:T(8,128)(2,1)}, bf16[2,128,128]{2,1,0:T(8,128)(2,1)S(1)}) custom-call(s32[2]{0:T(128)S(1)} %pad_add_fusion.3.place, bf16[3,384,512]{2,1,0:T(8,128)(2,1)S(1)} %get-tuple-element.43.own, bf16[3,384,512]{2,1,0:T(8,128)(2,1)S(1)} %collective-permute-done.theirs, ...), custom_call_target="tpu_custom_call" | custom-call | tf_op jit(solution)/shard_map/pair/pallas_call | solution.py:111
  17.5 1.2 %collective-permute-start.5 = (bf16[400,512]{1,0:T(8,128)(2,1)}, bf16[400,512]{1,0:T(8,128)(2,1)}, u32[]{:S(2)}, u32[]{:S(2)}) collective-permute-start(bf16[400,512]{1,0:T(8,128)(2,1)} %get-tuple-element.49), channel_id=1, source_target_pairs={{0,64},{64,0},{128,192},{192,128},{1,65},{65,1},{129,193},{193,129... | collective-permute-start | bytes 1228808 | tf_op jit(solution)/shard_map/ppermute | solution.py:44
  19.7 6.9 %collective-permute-done.3.r1 = bf16[400,512]{1,0:T(8,128)(2,1)} collective-permute-done((bf16[400,512]{1,0:T(8,128)(2,1)}, bf16[400,512]{1,0:T(8,128)(2,1)}, u32[]{:S(2)}, u32[]{:S(2)}) %collective-permute-start.3) | collective-permute-done | bytes 409632 | tf_op jit(solution)/shard_map/ppermute | solution.py:44
  26.6 8.8 %collective-permute-done.5.r2 = bf16[400,512]{1,0:T(8,128)(2,1)} collective-permute-done((bf16[400,512]{1,0:T(8,128)(2,1)}, bf16[400,512]{1,0:T(8,128)(2,1)}, u32[]{:S(2)}, u32[]{:S(2)}) %collective-permute-start.5) | collective-permute-done | bytes 409632 | tf_op jit(solution)/shard_map/ppermute | solution.py:44
  36.1 1.5 %total.1 = (bf16[112,512]{1,0:T(8,128)(2,1)S(1)}, bf16[112,512]{1,0:T(8,128)(2,1)S(1)}, bf16[112,512]{1,0:T(8,128)(2,1)S(1)}, bf16[112,512]{1,0:T(8,128)(2,1)S(1)}, bf16[4,128,128]{2,1,0:T(8,128)(2,1)S(1)}) custom-call(s32[2]{0:T(128)S(1)} %pad_add_fusion.2.place, bf16[3,384,512]{2,1,0:T(8,128)(2,1)S(1)} %get-tuple-element.43.own, ...), custom_call_target="tpu_custom_call" | custom-call | tf_op jit(solution)/shard_map/total/pallas_call | solution.py:111
  37.6 1.2 %collective-permute-start.8 = (bf16[112,512]{1,0:T(8,128)(2,1)S(1)}, bf16[112,512]{1,0:T(8,128)(2,1)S(1)}, u32[]{:S(2)}, u32[]{:S(2)}) collective-permute-start(bf16[112,512]{1,0:T(8,128)(2,1)S(1)} %get-tuple-element.53), channel_id=1, source_target_pairs={{0,16},{16,32},{32,48},{48,0},{1,17},{17,33},{33,49},{49,1},{2,18}... | collective-permute-start | bytes 344072 | tf_op jit(solution)/shard_map/ppermute | solution.py:40
  38.8 1.2 %collective-permute-start.13 = (bf16[4,128,128]{2,1,0:T(8,128)(2,1)S(1)}, bf16[4,128,128]{2,1,0:T(8,128)(2,1)S(1)}, u32[]{:S(2)}, u32[]{:S(2)}) collective-permute-start(bf16[4,128,128]{2,1,0:T(8,128)(2,1)S(1)} %get-tuple-element.56.h0), channel_id=1, source_target_pairs={{0,192},{64,128},{128,64},{192,0},{1,193},{65,129},{129,65},{193,1... | collective-permute-start | bytes 393224 | tf_op jit(solution)/shard_map/ppermute | solution.py:44
  40.8 1.2 %collective-permute-start.11 = (bf16[4,128,128]{2,1,0:T(8,128)(2,1)S(1)}, bf16[4,128,128]{2,1,0:T(8,128)(2,1)S(1)}, u32[]{:S(2)}, u32[]{:S(2)}) collective-permute-start(bf16[4,128,128]{2,1,0:T(8,128)(2,1)S(1)} %get-tuple-element.56.h0), channel_id=1, source_target_pairs={{0,64},{64,0},{128,192},{192,128},{1,65},{65,1},{129,193},{193,129... | collective-permute-start | bytes 393224 | tf_op jit(solution)/shard_map/ppermute | solution.py:44
  42.0 1.3 %collective-permute-start.10 = (bf16[112,512]{1,0:T(8,128)(2,1)S(1)}, bf16[112,512]{1,0:T(8,128)(2,1)S(1)}, u32[]{:S(2)}, u32[]{:S(2)}) collective-permute-start(bf16[112,512]{1,0:T(8,128)(2,1)S(1)} %get-tuple-element.55), channel_id=1, source_target_pairs={{0,48},{16,0},{32,16},{48,32},{1,49},{17,1},{33,17},{49,33},{2,50}... | collective-permute-start | bytes 344072 | tf_op jit(solution)/shard_map/ppermute | solution.py:40
  43.4 3.5 %collective-permute-done.9.r2 = bf16[112,512]{1,0:T(8,128)(2,1)S(1)} collective-permute-done((bf16[112,512]{1,0:T(8,128)(2,1)S(1)}, bf16[112,512]{1,0:T(8,128)(2,1)S(1)}, u32[]{:S(2)}, u32[]{:S(2)}) %collective-permute-start.9) | collective-permute-done | bytes 114720 | tf_op jit(solution)/shard_map/ppermute | solution.py:40
  46.9 1.8 %collective-permute-done.10.r3 = bf16[112,512]{1,0:T(8,128)(2,1)S(1)} collective-permute-done((bf16[112,512]{1,0:T(8,128)(2,1)S(1)}, bf16[112,512]{1,0:T(8,128)(2,1)S(1)}, u32[]{:S(2)}, u32[]{:S(2)}) %collective-permute-start.10) | collective-permute-done | bytes 114720 | tf_op jit(solution)/shard_map/ppermute | solution.py:40
  48.7 1.9 %expert_update.1 = (bf16[2,48,512]{2,1,0:T(8,128)(2,1)S(1)}, bf16[16,512]{1,0:T(8,128)(2,1)S(1)}, f32[16,512]{1,0:T(8,128)S(1)}, bf16[16,128,128]{2,1,0:T(8,128)(2,1)S(1)}) custom-call(s32[3]{0:T(128)S(1)} %pad_add_fusion.1.place, s32[16]{0:T(128)S(1)} %copy-done.12, f32[16]{0:T(128)S(1)} %copy-done.13, bf16[112,512]{1,0:T(8,128)(2,1)S(1)} %get-tuple-element.52.mine, ...), custom_call_target="tpu_custom_call" | custom-call | tf_op jit(solution)/shard_map/expert_update/pallas_call | solution.py:111
  50.6 6.7 %collective-permute-start.16 = (bf16[2,48,512]{2,1,0:T(8,128)(2,1)S(1)}, bf16[2,48,512]{2,1,0:T(8,128)(2,1)S(1)}, u32[]{:S(2)}, u32[]{:S(2)}) collective-permute-start(bf16[2,48,512]{2,1,0:T(8,128)(2,1)S(1)} %get-tuple-element.67), channel_id=1, source_target_pairs={{0,32},{1,0},{2,96},{3,64},{4,160},{5,128},{6,224},{7,192},{8,40},... | collective-permute-start | bytes 294920 | tf_op jit(solution)/shard_map/ppermute | solution.py:607
  57.3 1.9 %collective-permute-start.14 = (bf16[2,48,512]{2,1,0:T(8,128)(2,1)S(1)}, bf16[2,48,512]{2,1,0:T(8,128)(2,1)S(1)}, u32[]{:S(2)}, u32[]{:S(2)}) collective-permute-start(bf16[2,48,512]{2,1,0:T(8,128)(2,1)S(1)} %get-tuple-element.67), channel_id=1, source_target_pairs={{0,0},{1,32},{2,64},{3,96},{4,128},{5,160},{6,192},{7,224},{8,8},{... | collective-permute-start | bytes 294920 | tf_op jit(solution)/shard_map/ppermute | solution.py:607
  59.3 2.2 %collective-permute-done.16.refs_2_ = bf16[2,48,512]{2,1,0:T(8,128)(2,1)S(1)} collective-permute-done((bf16[2,48,512]{2,1,0:T(8,128)(2,1)S(1)}, bf16[2,48,512]{2,1,0:T(8,128)(2,1)S(1)}, u32[]{:S(2)}, u32[]{:S(2)}) %collective-permute-start.16) | collective-permute-done | bytes 98336 | tf_op jit(solution)/shard_map/ppermute | solution.py:607
  61.5 1.5 %collective-permute-start.17 = (bf16[2,48,512]{2,1,0:T(8,128)(2,1)S(1)}, bf16[2,48,512]{2,1,0:T(8,128)(2,1)S(1)}, u32[]{:S(2)}, u32[]{:S(2)}) collective-permute-start(bf16[2,48,512]{2,1,0:T(8,128)(2,1)S(1)} %collective-permute-done.16.refs_2_), channel_id=1, source_target_pairs={{0,16},{16,0},{32,48},{48,32},{1,17},{17,1},{33,49},{49,33},{2,18}... | collective-permute-start | bytes 294920 | tf_op jit(solution)/shard_map/ppermute | solution.py:44
  63.0 3.7 %collective-permute-done.14.refs_0_ = bf16[2,48,512]{2,1,0:T(8,128)(2,1)S(1)} collective-permute-done((bf16[2,48,512]{2,1,0:T(8,128)(2,1)S(1)}, bf16[2,48,512]{2,1,0:T(8,128)(2,1)S(1)}, u32[]{:S(2)}, u32[]{:S(2)}) %collective-permute-start.14) | collective-permute-done | bytes 98336 | tf_op jit(solution)/shard_map/ppermute | solution.py:607
  66.7 3.5 %collective-permute-start.15 = (bf16[2,48,512]{2,1,0:T(8,128)(2,1)S(1)}, bf16[2,48,512]{2,1,0:T(8,128)(2,1)S(1)}, u32[]{:S(2)}, u32[]{:S(2)}) collective-permute-start(bf16[2,48,512]{2,1,0:T(8,128)(2,1)S(1)} %collective-permute-done.14.refs_0_), channel_id=1, source_target_pairs={{0,16},{16,0},{32,48},{48,32},{1,17},{17,1},{33,49},{49,33},{2,18}... | collective-permute-start | bytes 294920 | tf_op jit(solution)/shard_map/ppermute | solution.py:44
  70.3 1.6 %others_update.1 = (f32[2,48,512]{2,1,0:T(8,128)}, f32[2,48,512]{2,1,0:T(8,128)}, f32[2,48,512]{2,1,0:T(8,128)}, f32[128,128]{1,0:T(8,128)}, f32[128,128]{1,0:T(...) custom-call(s32[2]{0:T(128)S(1)} %pad_add_fusion.place, ...), custom_call_target="tpu_custom_call" | custom-call | bytes 4194304 | tf_op jit(solution)/shard_map/others_update/pallas_call | solution.py:111
  72.3 5.8 %collective-permute-start.23 = (bf16[208,1024]{1,0:T(8,128)(2,1)S(1)}, bf16[208,1024]{1,0:T(8,128)(2,1)S(1)}, u32[]{:S(2)}, u32[]{:S(2)}) collective-permute-start(bf16[208,1024]{1,0:T(8,128)(2,1)S(1)} %halve.1.refs_0_), channel_id=1, source_target_pairs={{0,128},{64,192},{128,0},{192,64},{1,129},{65,193},{129,1},{193,65... | collective-permute-start | bytes 1277960 | tf_op jit(solution)/shard_map/ppermute | solution.py:40
  78.1 1.9 %collective-permute-start.21 = (bf16[208,1024]{1,0:T(8,128)(2,1)S(1)}, bf16[208,1024]{1,0:T(8,128)(2,1)S(1)}, u32[]{:S(2)}, u32[]{:S(2)}) collective-permute-start(bf16[208,1024]{1,0:T(8,128)(2,1)S(1)} %halve.1.refs_0_), channel_id=1, source_target_pairs={{0,192},{64,0},{128,64},{192,128},{1,193},{65,1},{129,65},{193,129... | collective-permute-start | bytes 1277960 | tf_op jit(solution)/shard_map/ppermute | solution.py:40
  80.0 4.8 %collective-permute-start.25 = (bf16[16,128,128]{2,1,0:T(8,128)(2,1)S(1)}, bf16[16,128,128]{2,1,0:T(8,128)(2,1)S(1)}, u32[]{:S(2)}, u32[]{:S(2)}) collective-permute-start(bf16[16,128,128]{2,1,0:T(8,128)(2,1)S(1)} %get-tuple-element.70.refs_8_), channel_id=1, source_target_pairs={{0,8},{8,0},{1,9},{9,1},{2,10},{10,2},{3,11},{11,3},{4,12},{12,4},... | collective-permute-start | bytes 1572872 | tf_op jit(solution)/shard_map/ppermute | solution.py:48
  84.9 7.9 %collective-permute-start.24 = (bf16[208,1024]{1,0:T(8,128)(2,1)S(1)}, bf16[208,1024]{1,0:T(8,128)(2,1)}, u32[]{:S(2)}, u32[]{:S(2)}) collective-permute-start(bf16[208,1024]{1,0:T(8,128)(2,1)S(1)} %collective-permute-done.23.refs_6_), channel_id=1, source_target_pairs={{0,8},{8,0},{1,9},{9,1},{2,10},{10,2},{3,11},{11,3},{4,12},{12,4},... | collective-permute-start | bytes 1277960 | tf_op jit(solution)/shard_map/ppermute | solution.py:48
  92.8 4.5 %collective-permute-done.21.refs_4_ = bf16[208,1024]{1,0:T(8,128)(2,1)S(1)} collective-permute-done((bf16[208,1024]{1,0:T(8,128)(2,1)S(1)}, bf16[208,1024]{1,0:T(8,128)(2,1)S(1)}, u32[]{:S(2)}, u32[]{:S(2)}) %collective-permute-start.21) | collective-permute-done | bytes 426016 | tf_op jit(solution)/shard_map/ppermute | solution.py:40
  98.0 2.0 %collective-permute-start.20 = (bf16[208,1024]{1,0:T(8,128)(2,1)S(1)}, bf16[208,1024]{1,0:T(8,128)(2,1)}, u32[]{:S(2)}, u32[]{:S(2)}) collective-permute-start(bf16[208,1024]{1,0:T(8,128)(2,1)S(1)} %collective-permute-done.19.refs_2_), channel_id=1, source_target_pairs={{0,8},{8,0},{1,9},{9,1},{2,10},{10,2},{3,11},{11,3},{4,12},{12,4},... | collective-permute-start | bytes 1277960 | tf_op jit(solution)/shard_map/ppermute | solution.py:48
  100.1 1.4 %collective-permute-done.20.refs_3_ = bf16[208,1024]{1,0:T(8,128)(2,1)} collective-permute-done((bf16[208,1024]{1,0:T(8,128)(2,1)S(1)}, bf16[208,1024]{1,0:T(8,128)(2,1)}, u32[]{:S(2)}, u32[]{:S(2)}) %collective-permute-start.20) | collective-permute-done | bytes 426016 | tf_op jit(solution)/shard_map/ppermute | solution.py:48
  101.5 4.2 %finish.1 = (bf16[2,2,2,48,4096]{4,3,2,1,0:T(8,128)(2,1)}, bf16[128,4096]{1,0:T(8,128)(2,1)}, bf16[64,128]{1,0:T(8,128)(2,1)}) custom-call(s32[7]{0:T(128)S(1)} %stack.82.place, s32[2]{0:T(128)S(1)} %copy-done.8, bf16[208,1024]{1,0:T(8,128)(2,1)S(1)} %halve.1.refs_0_, bf16[208,1024]{1,0:T(8,128)(2,1)S(1)} %collective-permute-done.18.refs_1_, ...), custom_call_target="tpu_custom_call" | custom-call | tf_op jit(solution)/shard_map/finish/pallas_call | solution.py:111
  (66 shorter events, 5.9 us)
Async XLA Ops:
  0.7 10.7 %copy-start.6 = (f32[1,2,4096]{2,1,0:T(2,128)S(1)}, f32[1,2,4096]{2,1,0:T(2,128)}, u32[]{:S(2)}) copy-start(f32[1,2,4096]{2,1,0:T(2,128)} %param.18) | copy-start | bytes 98308
  8.8 7.2 %collective-permute-start = (bf16[3,384,512]{2,1,0:T(8,128)(2,1)S(1)}, bf16[3,384,512]{2,1,0:T(8,128)(2,1)S(1)}, u32[]{:S(2)}, u32[]{:S(2)}) collective-permute-start(bf16[3,384,512]{2,1,0:T(8,128)(2,1)S(1)} %get-tuple-element.44), channel_id=1, source_target_pairs={{0,8},{8,0},{1,9},{9,1},{2,10},{10,2},{3,11},{11,3},{4,12},{12,4},... | collective-permute-start | bytes 3538952 | tf_op jit(solution)/shard_map/ppermute | solution.py:48
  9.5 3.7 %collective-permute-start.2 = (bf16[1,384,512]{2,1,0:T(8,128)(2,1)S(1)}, bf16[1,384,512]{2,1,0:T(8,128)(2,1)S(1)}, u32[]{:S(2)}, u32[]{:S(2)}) collective-permute-start(bf16[1,384,512]{2,1,0:T(8,128)(2,1)S(1)} %get-tuple-element.45), channel_id=1, source_target_pairs={{0,8},{8,0},{1,9},{9,1},{2,10},{10,2},{3,11},{11,3},{4,12},{12,4},... | collective-permute-start | bytes 1179656 | tf_op jit(solution)/shard_map/ppermute | solution.py:48
  9.7 6.2 %collective-permute-start.4 = (bf16[128,128]{1,0:T(8,128)(2,1)S(1)}, bf16[128,128]{1,0:T(8,128)(2,1)S(1)}, u32[]{:S(2)}, u32[]{:S(2)}) collective-permute-start(bf16[128,128]{1,0:T(8,128)(2,1)S(1)} %subtract_convert_fusion.refs_0_), channel_id=1, source_target_pairs={{0,16},{16,0},{32,48},{48,32},{1,17},{17,1},{33,49},{49,33},{2,18}... | collective-permute-start | bytes 98312 | tf_op jit(solution)/shard_map/ppermute | solution.py:44
  11.5 1.7 %collective-permute-start.1 = (bf16[4,16,512]{2,1,0:T(8,128)(2,1)S(1)}, bf16[4,16,512]{2,1,0:T(8,128)(2,1)S(1)}, u32[]{:S(2)}, u32[]{:S(2)}) collective-permute-start(bf16[4,16,512]{2,1,0:T(8,128)(2,1)S(1)} %extras.1), channel_id=1, source_target_pairs={{0,8},{8,0},{1,9},{9,1},{2,10},{10,2},{3,11},{11,3},{4,12},{12,4},... | collective-permute-start | bytes 196616 | tf_op jit(solution)/shard_map/ppermute | solution.py:48
  14.1 12.6 %collective-permute-start.3 = (bf16[400,512]{1,0:T(8,128)(2,1)}, bf16[400,512]{1,0:T(8,128)(2,1)}, u32[]{:S(2)}, u32[]{:S(2)}) collective-permute-start(bf16[400,512]{1,0:T(8,128)(2,1)} %pair.2), channel_id=1, source_target_pairs={{0,128},{64,192},{128,0},{192,64},{1,129},{65,193},{129,1},{193,65... | collective-permute-start | bytes 1228808 | tf_op jit(solution)/shard_map/ppermute | solution.py:44
  17.5 31.2 %copy-start.12 = (s32[16]{0:T(128)S(1)}, s32[16]{0:T(128)}, u32[]{:S(2)}) copy-start(s32[16]{0:T(128)} %lengths.3) | copy-start | bytes 196
  17.5 31.2 %copy-start.13 = (f32[16]{0:T(128)S(1)}, f32[16]{0:T(128)}, u32[]{:S(2)}) copy-start(f32[16]{0:T(128)} %rate.3) | copy-start | bytes 196
  17.5 17.9 %collective-permute-start.5 = (bf16[400,512]{1,0:T(8,128)(2,1)}, bf16[400,512]{1,0:T(8,128)(2,1)}, u32[]{:S(2)}, u32[]{:S(2)}) collective-permute-start(bf16[400,512]{1,0:T(8,128)(2,1)} %get-tuple-element.49), channel_id=1, source_target_pairs={{0,64},{64,0},{128,192},{192,128},{1,65},{65,1},{129,193},{193,129... | collective-permute-start | bytes 1228808 | tf_op jit(solution)/shard_map/ppermute | solution.py:44
  18.7 17.4 %collective-permute-start.6 = (bf16[400,512]{1,0:T(8,128)(2,1)}, bf16[400,512]{1,0:T(8,128)(2,1)}, u32[]{:S(2)}, u32[]{:S(2)}) collective-permute-start(bf16[400,512]{1,0:T(8,128)(2,1)} %get-tuple-element.50), channel_id=1, source_target_pairs={{0,192},{64,128},{128,64},{192,0},{1,193},{65,129},{129,65},{193,1... | collective-permute-start | bytes 1228808 | tf_op jit(solution)/shard_map/ppermute | solution.py:44
  19.6 7.1 %collective-permute-start.7 = (bf16[2,128,128]{2,1,0:T(8,128)(2,1)S(1)}, bf16[2,128,128]{2,1,0:T(8,128)(2,1)S(1)}, u32[]{:S(2)}, u32[]{:S(2)}) collective-permute-start(bf16[2,128,128]{2,1,0:T(8,128)(2,1)S(1)} %get-tuple-element.51.router), channel_id=1, source_target_pairs={{0,32},{16,48},{32,0},{48,16},{1,33},{17,49},{33,1},{49,17},{2,34}... | collective-permute-start | bytes 196616 | tf_op jit(solution)/shard_map/ppermute | solution.py:44
  19.7 50.6 %copy-start = (f32[2,48,512]{2,1,0:T(8,128)S(1)}, f32[2,48,512]{2,1,0:T(8,128)}, u32[]{:S(2)}) copy-start(f32[2,48,512]{2,1,0:T(8,128)} %refs_0_.1) | copy-start | bytes 589828
  19.7 50.6 %copy-start.1 = (f32[2,48,512]{2,1,0:T(8,128)S(1)}, f32[2,48,512]{2,1,0:T(8,128)}, u32[]{:S(2)}) copy-start(f32[2,48,512]{2,1,0:T(8,128)} %refs_1_.1) | copy-start | bytes 589828
  19.7 50.6 %copy-start.2 = (f32[2,48,512]{2,1,0:T(8,128)S(1)}, f32[2,48,512]{2,1,0:T(8,128)}, u32[]{:S(2)}) copy-start(f32[2,48,512]{2,1,0:T(8,128)} %refs_2_.1) | copy-start | bytes 589828
  37.6 4.4 %collective-permute-start.8 = (bf16[112,512]{1,0:T(8,128)(2,1)S(1)}, bf16[112,512]{1,0:T(8,128)(2,1)S(1)}, u32[]{:S(2)}, u32[]{:S(2)}) collective-permute-start(bf16[112,512]{1,0:T(8,128)(2,1)S(1)} %get-tuple-element.53), channel_id=1, source_target_pairs={{0,16},{16,32},{32,48},{48,0},{1,17},{17,33},{33,49},{49,1},{2,18}... | collective-permute-start | bytes 344072 | tf_op jit(solution)/shard_map/ppermute | solution.py:40
  38.8 9.9 %collective-permute-start.13 = (bf16[4,128,128]{2,1,0:T(8,128)(2,1)S(1)}, bf16[4,128,128]{2,1,0:T(8,128)(2,1)S(1)}, u32[]{:S(2)}, u32[]{:S(2)}) collective-permute-start(bf16[4,128,128]{2,1,0:T(8,128)(2,1)S(1)} %get-tuple-element.56.h0), channel_id=1, source_target_pairs={{0,192},{64,128},{128,64},{192,0},{1,193},{65,129},{129,65},{193,1... | collective-permute-start | bytes 393224 | tf_op jit(solution)/shard_map/ppermute | solution.py:44
  40.0 8.7 %collective-permute-start.12 = (bf16[4,128,128]{2,1,0:T(8,128)(2,1)S(1)}, bf16[4,128,128]{2,1,0:T(8,128)(2,1)S(1)}, u32[]{:S(2)}, u32[]{:S(2)}) collective-permute-start(bf16[4,128,128]{2,1,0:T(8,128)(2,1)S(1)} %get-tuple-element.56.h0), channel_id=1, source_target_pairs={{0,128},{64,192},{128,0},{192,64},{1,129},{65,193},{129,1},{193,65... | collective-permute-start | bytes 393224 | tf_op jit(solution)/shard_map/ppermute | solution.py:44
  40.8 7.9 %collective-permute-start.11 = (bf16[4,128,128]{2,1,0:T(8,128)(2,1)S(1)}, bf16[4,128,128]{2,1,0:T(8,128)(2,1)S(1)}, u32[]{:S(2)}, u32[]{:S(2)}) collective-permute-start(bf16[4,128,128]{2,1,0:T(8,128)(2,1)S(1)} %get-tuple-element.56.h0), channel_id=1, source_target_pairs={{0,64},{64,0},{128,192},{192,128},{1,65},{65,1},{129,193},{193,129... | collective-permute-start | bytes 393224 | tf_op jit(solution)/shard_map/ppermute | solution.py:44
  42.0 4.9 %collective-permute-start.9 = (bf16[112,512]{1,0:T(8,128)(2,1)S(1)}, bf16[112,512]{1,0:T(8,128)(2,1)S(1)}, u32[]{:S(2)}, u32[]{:S(2)}) collective-permute-start(bf16[112,512]{1,0:T(8,128)(2,1)S(1)} %get-tuple-element.54), channel_id=1, source_target_pairs={{0,32},{16,48},{32,0},{48,16},{1,33},{17,49},{33,1},{49,17},{2,34}... | collective-permute-start | bytes 344072 | tf_op jit(solution)/shard_map/ppermute | solution.py:40
  42.0 6.6 %collective-permute-start.10 = (bf16[112,512]{1,0:T(8,128)(2,1)S(1)}, bf16[112,512]{1,0:T(8,128)(2,1)S(1)}, u32[]{:S(2)}, u32[]{:S(2)}) collective-permute-start(bf16[112,512]{1,0:T(8,128)(2,1)S(1)} %get-tuple-element.55), channel_id=1, source_target_pairs={{0,48},{16,0},{32,16},{48,32},{1,49},{17,1},{33,17},{49,33},{2,50}... | collective-permute-start | bytes 344072 | tf_op jit(solution)/shard_map/ppermute | solution.py:40
  50.6 10.9 %collective-permute-start.16 = (bf16[2,48,512]{2,1,0:T(8,128)(2,1)S(1)}, bf16[2,48,512]{2,1,0:T(8,128)(2,1)S(1)}, u32[]{:S(2)}, u32[]{:S(2)}) collective-permute-start(bf16[2,48,512]{2,1,0:T(8,128)(2,1)S(1)} %get-tuple-element.67), channel_id=1, source_target_pairs={{0,32},{1,0},{2,96},{3,64},{4,160},{5,128},{6,224},{7,192},{8,40},... | collective-permute-start | bytes 294920 | tf_op jit(solution)/shard_map/ppermute | solution.py:607
  57.3 9.4 %collective-permute-start.14 = (bf16[2,48,512]{2,1,0:T(8,128)(2,1)S(1)}, bf16[2,48,512]{2,1,0:T(8,128)(2,1)S(1)}, u32[]{:S(2)}, u32[]{:S(2)}) collective-permute-start(bf16[2,48,512]{2,1,0:T(8,128)(2,1)S(1)} %get-tuple-element.67), channel_id=1, source_target_pairs={{0,0},{1,32},{2,64},{3,96},{4,128},{5,160},{6,192},{7,224},{8,8},{... | collective-permute-start | bytes 294920 | tf_op jit(solution)/shard_map/ppermute | solution.py:607
  61.5 10.5 %collective-permute-start.17 = (bf16[2,48,512]{2,1,0:T(8,128)(2,1)S(1)}, bf16[2,48,512]{2,1,0:T(8,128)(2,1)S(1)}, u32[]{:S(2)}, u32[]{:S(2)}) collective-permute-start(bf16[2,48,512]{2,1,0:T(8,128)(2,1)S(1)} %collective-permute-done.16.refs_2_), channel_id=1, source_target_pairs={{0,16},{16,0},{32,48},{48,32},{1,17},{17,1},{33,49},{49,33},{2,18}... | collective-permute-start | bytes 294920 | tf_op jit(solution)/shard_map/ppermute | solution.py:44
  66.7 5.5 %collective-permute-start.15 = (bf16[2,48,512]{2,1,0:T(8,128)(2,1)S(1)}, bf16[2,48,512]{2,1,0:T(8,128)(2,1)S(1)}, u32[]{:S(2)}, u32[]{:S(2)}) collective-permute-start(bf16[2,48,512]{2,1,0:T(8,128)(2,1)S(1)} %collective-permute-done.14.refs_0_), channel_id=1, source_target_pairs={{0,16},{16,0},{32,48},{48,32},{1,17},{17,1},{33,49},{49,33},{2,18}... | collective-permute-start | bytes 294920 | tf_op jit(solution)/shard_map/ppermute | solution.py:44
  72.3 12.6 %collective-permute-start.23 = (bf16[208,1024]{1,0:T(8,128)(2,1)S(1)}, bf16[208,1024]{1,0:T(8,128)(2,1)S(1)}, u32[]{:S(2)}, u32[]{:S(2)}) collective-permute-start(bf16[208,1024]{1,0:T(8,128)(2,1)S(1)} %halve.1.refs_0_), channel_id=1, source_target_pairs={{0,128},{64,192},{128,0},{192,64},{1,129},{65,193},{129,1},{193,65... | collective-permute-start | bytes 1277960 | tf_op jit(solution)/shard_map/ppermute | solution.py:40
  78.1 19.2 %collective-permute-start.21 = (bf16[208,1024]{1,0:T(8,128)(2,1)S(1)}, bf16[208,1024]{1,0:T(8,128)(2,1)S(1)}, u32[]{:S(2)}, u32[]{:S(2)}) collective-permute-start(bf16[208,1024]{1,0:T(8,128)(2,1)S(1)} %halve.1.refs_0_), channel_id=1, source_target_pairs={{0,192},{64,0},{128,64},{192,128},{1,193},{65,1},{129,65},{193,129... | collective-permute-start | bytes 1277960 | tf_op jit(solution)/shard_map/ppermute | solution.py:40
  80.0 18.0 %collective-permute-start.19 = (bf16[208,1024]{1,0:T(8,128)(2,1)S(1)}, bf16[208,1024]{1,0:T(8,128)(2,1)S(1)}, u32[]{:S(2)}, u32[]{:S(2)}) collective-permute-start(bf16[208,1024]{1,0:T(8,128)(2,1)S(1)} %halve.1.refs_0_), channel_id=1, source_target_pairs={{0,64},{64,128},{128,192},{192,0},{1,65},{65,129},{129,193},{193,1... | collective-permute-start | bytes 1277960 | tf_op jit(solution)/shard_map/ppermute | solution.py:40
  80.0 20.0 %collective-permute-start.25 = (bf16[16,128,128]{2,1,0:T(8,128)(2,1)S(1)}, bf16[16,128,128]{2,1,0:T(8,128)(2,1)S(1)}, u32[]{:S(2)}, u32[]{:S(2)}) collective-permute-start(bf16[16,128,128]{2,1,0:T(8,128)(2,1)S(1)} %get-tuple-element.70.refs_8_), channel_id=1, source_target_pairs={{0,8},{8,0},{1,9},{9,1},{2,10},{10,2},{3,11},{11,3},{4,12},{12,4},... | collective-permute-start | bytes 1572872 | tf_op jit(solution)/shard_map/ppermute | solution.py:48
  84.9 15.2 %collective-permute-start.18 = (bf16[208,1024]{1,0:T(8,128)(2,1)S(1)}, bf16[208,1024]{1,0:T(8,128)(2,1)S(1)}, u32[]{:S(2)}, u32[]{:S(2)}) collective-permute-start(bf16[208,1024]{1,0:T(8,128)(2,1)S(1)} %halve.1.refs_0_), channel_id=1, source_target_pairs={{0,8},{8,0},{1,9},{9,1},{2,10},{10,2},{3,11},{11,3},{4,12},{12,4},... | collective-permute-start | bytes 1277960 | tf_op jit(solution)/shard_map/ppermute | solution.py:48
  84.9 15.2 %collective-permute-start.24 = (bf16[208,1024]{1,0:T(8,128)(2,1)S(1)}, bf16[208,1024]{1,0:T(8,128)(2,1)}, u32[]{:S(2)}, u32[]{:S(2)}) collective-permute-start(bf16[208,1024]{1,0:T(8,128)(2,1)S(1)} %collective-permute-done.23.refs_6_), channel_id=1, source_target_pairs={{0,8},{8,0},{1,9},{9,1},{2,10},{10,2},{3,11},{11,3},{4,12},{12,4},... | collective-permute-start | bytes 1277960 | tf_op jit(solution)/shard_map/ppermute | solution.py:48
  97.3 2.8 %collective-permute-start.22 = (bf16[208,1024]{1,0:T(8,128)(2,1)S(1)}, bf16[208,1024]{1,0:T(8,128)(2,1)}, u32[]{:S(2)}, u32[]{:S(2)}) collective-permute-start(bf16[208,1024]{1,0:T(8,128)(2,1)S(1)} %collective-permute-done.21.refs_4_), channel_id=1, source_target_pairs={{0,8},{8,0},{1,9},{9,1},{2,10},{10,2},{3,11},{11,3},{4,12},{12,4},... | collective-permute-start | bytes 1277960 | tf_op jit(solution)/shard_map/ppermute | solution.py:48
  98.0 3.5 %collective-permute-start.20 = (bf16[208,1024]{1,0:T(8,128)(2,1)S(1)}, bf16[208,1024]{1,0:T(8,128)(2,1)}, u32[]{:S(2)}, u32[]{:S(2)}) collective-permute-start(bf16[208,1024]{1,0:T(8,128)(2,1)S(1)} %collective-permute-done.19.refs_2_), channel_id=1, source_target_pairs={{0,8},{8,0},{1,9},{9,1},{2,10},{10,2},{3,11},{11,3},{4,12},{12,4},... | collective-permute-start | bytes 1277960 | tf_op jit(solution)/shard_map/ppermute | solution.py:48
  (8 other events, 74.3 us)
